TPU v7x, 256 devices: a whole 4x4x8 slice. The times are simulated.
256 devices in a mesh: slab: 32 (over y, x, core), led: 8 (over z).
Axes of the slice: x: 4, y: 4, z: 8, core: 2. Of those that a mesh axis runs over, the one named last changes fastest.
Arguments:
- spectrum: float32 [2, 4096, 3072], P(None, 'slab'), may hold values from -6 to 6
- pupil: float32 [2, 2048, 2048], P(None, 'slab'), may hold values from -6 to 6
- intensity: float32 [8, 2048, 2048], P('led', 'slab'), may hold values from 0.1 to 4
- row_offsets: int32 [8], replicated, may hold values from 0 to 2048, as said below
- col_offsets: int32 [8], replicated, may hold values from 0 to 1024, as said below
Outputs:
- new_spectrum: float32 [2, 4096, 3072], P(None, 'slab')
- pupil_grad: float32 [2, 2048, 2048], P(None, 'slab')
Inputs may be any that keep to these rules, and one draw needn't show every extreme that they name: `row_offsets`: every LED's subaperture lies inside the spectrum; some LED starts at row 0 and some at row 2048. `col_offsets`: every LED's subaperture lies inside the spectrum; some LED starts at column 0 and some at column 1024.
All inputs are finite; a program needn't handle non-finite values.
Results may differ from a plain program's by a relative error of at most 0.012.
The roundings to bfloat16 on the way count: a program that leaves them out, or rounds other values in their place, can miss the bound.
Values may be sent and summed in bfloat16 or wider, within the bound.
No kernel may reach another device: no remote copies, remote signals or barrier semaphores. Data moves between devices by JAX's collectives and lax.ppermute only.
A program may use at most 64 MiB of HBM per device.

v0:
```python
import math

import jax
import jax.numpy as jnp
from jax import lax
from jax.sharding import PartitionSpec as P

AMPLITUDE_FLOOR = 0.5
PUPIL_DAMPING = 0.5


def tables(length):
    counter = jnp.arange(length, dtype=jnp.int32)
    products = counter[:, None] * counter[None, :] % length
    phases = products.astype(jnp.float32) * (2.0 * math.pi / length)
    factor = 1.0 / math.sqrt(length)
    return (
        (jnp.cos(phases) * factor).astype(jnp.bfloat16),
        (jnp.sin(phases) * factor).astype(jnp.bfloat16),
    )


def transform(values, cosine_table, sine_table, direction):
    height = values.shape[1]
    flattened = values.reshape(2 * height, values.shape[2])
    with_cos = jnp.dot(flattened, cosine_table, preferred_element_type=jnp.float32).reshape(
        2, height, -1
    )
    with_sin = jnp.dot(flattened, sine_table, preferred_element_type=jnp.float32).reshape(
        2, height, -1
    )
    real_part = with_cos[0] - direction * with_sin[1]
    imag_part = with_cos[1] + direction * with_sin[0]
    return jnp.stack([real_part, imag_part])


def transform_across(values, cosine_table, sine_table, direction):
    with_cos = jnp.einsum("kqm,qn->kmn", values, cosine_table, preferred_element_type=jnp.float32)
    with_sin = jnp.einsum("kqm,qn->kmn", values, sine_table, preferred_element_type=jnp.float32)
    real_part = with_cos[0] - direction * with_sin[1]
    imag_part = with_cos[1] + direction * with_sin[0]
    return jnp.stack([real_part, imag_part])


def turn_bands(values):
    return lax.all_to_all(values, "slab", split_axis=2, concat_axis=1, tiled=True)


def per_device(spectrum, pupil, intensity, row_offsets, col_offsets):
    slab_count = lax.axis_size("slab")
    slab_index = lax.axis_index("slab")
    led_index = lax.axis_index("led")
    local_rows = spectrum.shape[1]
    band_size = pupil.shape[1]
    window_size = pupil.shape[2]
    leds_here = intensity.shape[0]
    cosine_table, sine_table = tables(window_size)
    row_ids = slab_index * local_rows + jnp.arange(local_rows, dtype=jnp.int32)
    pupil_weight = pupil[0] * pupil[0] + pupil[1] * pupil[1] + PUPIL_DAMPING
    update = jnp.zeros(spectrum.shape, jnp.float32)
    led_number = led_index * leds_here + 0
    row_start = row_offsets[led_number]
    col_start = col_offsets[led_number]
    columns = lax.dynamic_slice_in_dim(spectrum, col_start, window_size, 2)
    inside = (row_ids >= row_start) & (row_ids < row_start + window_size)
    columns = jnp.where(inside[None, :, None], columns, 0.0).astype(jnp.bfloat16)
    outgoing = jnp.swapaxes(columns, 1, 2)
    arrived = lax.all_to_all(outgoing, "slab", split_axis=1, concat_axis=2, tiled=True)
    window = lax.dynamic_slice_in_dim(arrived, row_start, window_size, 2).astype(jnp.float32)
    prod_real = window[0] * pupil[0] - window[1] * pupil[1]
    prod_imag = window[0] * pupil[1] + window[1] * pupil[0]
    product = jnp.stack([prod_real, prod_imag])
    first_pass = transform(product.astype(jnp.bfloat16), cosine_table, sine_table, 1.0).astype(
        jnp.bfloat16
    )
    turned = turn_bands(first_pass)
    image_field = transform_across(turned, cosine_table, sine_table, 1.0)
    magnitude = jnp.sqrt(image_field[0] * image_field[0] + image_field[1] * image_field[1])
    scaling = jnp.sqrt(intensity[0]) / jnp.maximum(magnitude, AMPLITUDE_FLOOR)
    replaced = (image_field * scaling).astype(jnp.bfloat16)
    second_pass = transform(replaced, cosine_table, sine_table, -1.0).astype(jnp.bfloat16)
    returned = turn_bands(second_pass)
    estimate = transform_across(returned, cosine_table, sine_table, -1.0)
    change = estimate - product
    grad_real = window[0] * change[0] + window[1] * change[1]
    grad_imag = window[0] * change[1] - window[1] * change[0]
    gradient = jnp.stack([grad_real, grad_imag])
    corr_real = (pupil[0] * change[0] + pupil[1] * change[1]) / pupil_weight
    corr_imag = (pupil[0] * change[1] - pupil[1] * change[0]) / pupil_weight
    correction = jnp.stack([corr_real, corr_imag])
    placed = lax.dynamic_update_slice_in_dim(
        jnp.zeros((2, band_size, slab_count * local_rows), jnp.float32), correction, row_start, 2
    )
    landed = lax.all_to_all(placed, "slab", split_axis=2, concat_axis=1, tiled=True)
    landed = jnp.swapaxes(landed, 1, 2)
    update = lax.dynamic_update_slice_in_dim(update, landed, col_start, 2)
    grad_total, update_total = lax.psum((gradient, update), "led")
    new_spectrum = spectrum + update_total
    return (new_spectrum, grad_total)


def solution(mesh):
    in_specs = (P(None, "slab", None), P(None, "slab", None), P("led", "slab", None), P(), P())
    out_specs = (P(None, "slab", None), P(None, "slab", None))
    return jax.shard_map(
        per_device, mesh=mesh, in_specs=in_specs, out_specs=out_specs, check_vma=False
    )
```

profile of v0, /device:TPU:2, one launch (start us, length us, event | category | flops | bytes accessed | tf_op | source)
XLA Modules:
  0.0 788.0 jit_solution(1831103482243353476)
XLA Ops:
  10.4 2.0 constant_dynamic-slice_fusion
  15.1 1.8 fusion.18
  16.9 7.8 all-to-all-start
  26.6 14.1 %all-to-all-done = bf16[2,2048,128]{2,0,1:T(2,128)(2,1)S(1)} async-done(((bf16[2,2048,128]{2,0,1:T(2,128)(2,1)}), bf16[2,2048,128]{2,0,1:T(2,128)(2,1)S(1)}, u32[]{:S(2)}, u32[]{:S(2)}) %all-to-all-start) | async-done | bytes 1048608 | tf_op jit(solution)/shard_map/all_to_all | solution.py:68
  41.6 62.8 %fusion.15 = f32[128,2048]{1,0:T(8,128)S(1)} fusion(bf16[128,2048]{1,0:T(8,128)(2,1)S(1)} %bitcast.88), kind=kOutput, calls=%fused_computation.20 | convolution fusion | flops 1140850688 | bytes 1572864 | tf_op jit(solution)/shard_map/dot_general | solution.py:26
  104.4 63.5 %fusion.17 = f32[128,2048]{1,0:T(8,128)S(1)} fusion(bf16[128,2048]{1,0:T(8,128)(2,1)S(1)} %bitcast.89), kind=kOutput, calls=%fused_computation.22 | convolution fusion | flops 1140850688 | bytes 1572864 | tf_op jit(solution)/shard_map/dot_general | solution.py:29
  169.7 15.5 %all_to_all.72 = bf16[32,2,4096]{2,1,0:T(2,128)(2,1)S(1)} all-to-all(bf16[32,2,4096]{2,1,0:T(2,128)(2,1)S(1)} %reshape.59), channel_id=1, replica_groups=mesh['slab'=32,'led'=8] {'slab'}, dimensions={0} | all-to-all | bytes 1048576 | tf_op jit(solution)/shard_map/all_to_all | solution.py:46
  187.3 62.8 %fusion.12 = f32[2,64,2048]{2,1,0:T(8,128)S(1)} fusion(bf16[2,2048,64]{1,2,0:T(8,128)(2,1)S(1)} %all_to_all.59), kind=kOutput, calls=%fused_computation.17 | convolution fusion | flops 1140850688 | bytes 1572864 | tf_op jit(solution)/shard_map/kqm,qn->kmn/dot_general | solution.py:38
  250.1 63.5 %fusion.8 = f32[2,64,2048]{2,1,0:T(8,128)S(1)} fusion(bf16[2,2048,64]{1,2,0:T(8,128)(2,1)S(1)} %all_to_all.59), kind=kOutput, calls=%fused_computation.13 | convolution fusion | flops 1140850688 | bytes 1572864 | tf_op jit(solution)/shard_map/kqm,qn->kmn/dot_general | solution.py:39
  314.1 63.0 %fusion.14 = f32[128,2048]{1,0:T(8,128)S(1)} fusion(bf16[128,2048]{1,0:T(8,128)(2,1)S(1)} %bitcast.90), kind=kOutput, calls=%fused_computation.19 | convolution fusion | flops 1140850688 | bytes 1572864 | tf_op jit(solution)/shard_map/dot_general | solution.py:26
  377.1 63.7 %fusion.16 = f32[128,2048]{1,0:T(8,128)S(1)} fusion(bf16[128,2048]{1,0:T(8,128)(2,1)S(1)} %bitcast.91), kind=kOutput, calls=%fused_computation.21 | convolution fusion | flops 1140850688 | bytes 1572864 | tf_op jit(solution)/shard_map/dot_general | solution.py:29
  442.6 15.4 %all_to_all.73 = bf16[32,2,4096]{2,1,0:T(2,128)(2,1)S(1)} all-to-all(bf16[32,2,4096]{2,1,0:T(2,128)(2,1)S(1)} %reshape.61), channel_id=1, replica_groups=mesh['slab'=32,'led'=8] {'slab'}, dimensions={0} | all-to-all | bytes 1048576 | tf_op jit(solution)/shard_map/all_to_all | solution.py:46
  460.1 62.8 %fusion.10 = f32[2,64,2048]{2,1,0:T(8,128)S(1)} fusion(bf16[2,2048,64]{1,2,0:T(8,128)(2,1)S(1)} %all_to_all.63), kind=kOutput, calls=%fused_computation.15 | convolution fusion | flops 1140850688 | bytes 1572864 | tf_op jit(solution)/shard_map/kqm,qn->kmn/dot_general | solution.py:38
  522.9 63.5 %fusion.6 = f32[2,64,2048]{2,1,0:T(8,128)S(1)} fusion(bf16[2,2048,64]{1,2,0:T(8,128)(2,1)S(1)} %all_to_all.63), kind=kOutput, calls=%fused_computation.11 | convolution fusion | flops 1140850688 | bytes 1572864 | tf_op jit(solution)/shard_map/kqm,qn->kmn/dot_general | solution.py:39
  590.6 2.9 broadcast_in_dim.23
  594.9 5.6 reshape.63
  600.5 32.6 %all_to_all.74 = f32[32,1,16384]{2,1,0:T(1,128)} all-to-all(f32[32,1,16384]{2,1,0:T(1,128)S(1)} %reshape.63), channel_id=1, replica_groups=mesh['slab'=32,'led'=8] {'slab'}, dimensions={0} | all-to-all | bytes 4194304 | tf_op jit(solution)/shard_map/all_to_all | solution.py:94
  633.6 7.4 reduce
  641.0 4.4 reshape.64
  645.4 5.4 copy.28
  650.8 1.8 copy.26
  653.0 10.3 %dynamic_update_slice.7 = f32[2,128,3072]{2,1,0:T(8,128)S(1)} dynamic-update-slice(f32[2,128,3072]{2,1,0:T(8,128)S(1)} %broadcast_in_dim.22, f32[2,128,2048]{2,1,0:T(8,128)} %copy.26, s32[]{:T(128)} %constant.12.clone.1, s32[]{:T(128)} %constant.12.clone.1, s32[]{:T(128)S(6)} %select_n.38) | dynamic-update-slice | bytes 4194308 | tf_op jit(solution)/shard_map/dynamic_update_slice | solution.py:96
  665.0 109.6 %all-reduce.3.cloned.1.call-done = (f32[2,128,3072]{2,1,0:T(8,128)}, f32[2,64,2048]{2,1,0:T(8,128)}) async-done(((f32[2,128,3072]{2,1,0:T(8,128)}, f32[2,64,2048]{2,1,0:T(8,128)}), (f32[2,128,3072]{2,1,0:T(8,128)}, f32[2,64,2048]{2,1,0:T(8,128)})) %all-reduce.3.cloned.1.call-update) | async-done | bytes 4194320 | tf_op jit(solution)/shard_map/psum | solution.py:97
  774.6 5.1 add.119
  (60 shorter events, 21.2 us)
Async XLA Ops:
  7.2 6.0 copy-start.11
  16.9 24.5 %copy-start.7 = (f32[2,64,2048]{2,1,0:T(8,128)S(1)}, f32[2,64,2048]{2,1,0:T(8,128)}, u32[]{:S(2)}) copy-start(f32[2,64,2048]{2,1,0:T(8,128)} %param.6) | copy-start | bytes 3145732
  16.9 23.9 %all-to-all-start = ((bf16[2,2048,128]{2,0,1:T(2,128)(2,1)}), bf16[2,2048,128]{2,0,1:T(2,128)(2,1)S(1)}, u32[]{:S(2)}, u32[]{:S(2)}) async-start(bf16[2,2048,128]{2,0,1:T(2,128)(2,1)} %fusion.18), calls=%async_computation | async-start | bytes 2097152 | tf_op jit(solution)/shard_map/all_to_all | solution.py:68
  24.6 750.0 %all-reduce.3.cloned.1.call-start = ((), (), s32[]{:S(2)}) async-start(), calls=%async_computation.4 | async-start | bytes 8388608 | tf_op jit(solution)/shard_map/psum | solution.py:97
  41.4 63.1 %copy-start.1 = (f32[2,64,2048]{2,1,0:T(8,128)}, f32[2,64,2048]{2,1,0:T(8,128)S(1)}, u32[]{:S(2)}) copy-start(f32[2,64,2048]{2,1,0:T(8,128)S(1)} %dynamic-slice_convert_fusion) | copy-start | bytes 3145732
  41.5 62.9 %copy-start.3 = (f32[1,64,2048]{2,1,0:T(8,128)}, f32[1,64,2048]{2,1,0:T(8,128)S(1)}, u32[]{:S(2)}) copy-start(f32[1,64,2048]{2,1,0:T(8,128)S(1)} %get-tuple-element.17) | copy-start | bytes 1572868
  41.5 62.9 %copy-start.5 = (f32[1,64,2048]{2,1,0:T(8,128)}, f32[1,64,2048]{2,1,0:T(8,128)S(1)}, u32[]{:S(2)}) copy-start(f32[1,64,2048]{2,1,0:T(8,128)S(1)} %get-tuple-element.18) | copy-start | bytes 1572868
  250.1 63.5 %copy-start.10 = (f32[1,64,2048]{2,1,0:T(8,128)S(1)}, f32[1,64,2048]{2,1,0:T(8,128)}, u32[]{:S(2)}) copy-start(f32[1,64,2048]{2,1,0:T(8,128)} %param.7) | copy-start | bytes 1572868
  522.9 63.7 %copy-start.4 = (f32[1,64,2048]{2,1,0:T(8,128)S(1)}, f32[1,64,2048]{2,1,0:T(8,128)}, u32[]{:S(2)}) copy-start(f32[1,64,2048]{2,1,0:T(8,128)} %copy-done.3) | copy-start | bytes 1572868
  522.9 63.7 %copy-start.6 = (f32[1,64,2048]{2,1,0:T(8,128)S(1)}, f32[1,64,2048]{2,1,0:T(8,128)}, u32[]{:S(2)}) copy-start(f32[1,64,2048]{2,1,0:T(8,128)} %copy-done.5) | copy-start | bytes 1572868
  586.5 1.2 copy-start.2
  586.5 1.5 copy-start.8
  663.3 1.7 copy-start
  774.6 5.1 copy-start.9
Sparse Core Ops, SparseCore 0:
  665.2 109.4 all-reduce.2
where the time goes:
time: 797 us; the launch traced here: 788 us
  matrix products  506 us (63%)
  waiting for transfers between devices  124 us (16%)
  blocking collectives  63.4 us (8%)
  local copies, waits for them, and re-layouts  50 us (6%)
  between operations  19.5 us (2%)
  other arithmetic  17.9 us (2%)
    dot_general x2, matrix products, transform(): jnp.dot(flattened, sine_table, preferred_element_type=jnp.float32)  127 us
    dot_general x2, matrix products, transform_across(): jnp.einsum('kqm,qn->kmn', values, sine_table, preferred_element_type=jnp....  127 us
    dot_general x2, matrix products, transform(): jnp.dot(flattened, cosine_table, preferred_element_type=jnp.float32)  126 us
    dot_general x2, matrix products, transform_across(): jnp.einsum('kqm,qn->kmn', values, cosine_table, preferred_element_type=jn...  126 us
    psum x1, waiting for transfers between devices, per_device(): grad_total, update_total = lax.psum((gradient, update), 'led')  110 us
    all_to_all x1, blocking collectives, per_device(): lax.all_to_all(placed, 'slab', split_axis=2, concat_axis=1, tiled=True)  32.6 us
    all_to_all x2, blocking collectives, turn_bands(): lax.all_to_all(values, 'slab', split_axis=2, concat_axis=1, tiled=True)  30.8 us
    unnamed x32, local copies, waits for them, and re-layouts  17.5 us
  transfers between devices with their start and end apart: 2, of which 2 were waited for; matrix products, arithmetic and copies ran while one was open for 0% of the time, Pallas kernels for 0%

commit v1 on v0

v1 whole, which is shorter than its diff:
```python
import functools
import math

import jax
import jax.numpy as jnp
import numpy as np
from jax import lax
from jax.experimental import pallas as pl
from jax.experimental.pallas import tpu as pltpu
from jax.sharding import PartitionSpec as P

W = 2048
QUARTER = W // 4
BAND = 64
NC = 3072
AMPLITUDE_FLOOR = 0.5
PUPIL_DAMPING = 0.5
MIB = 1024 * 1024

VMEM = pltpu.VMEM
F32 = jnp.float32
BF16 = jnp.bfloat16


def table():
    rows = np.arange(QUARTER, dtype=np.int64)[:, None]
    cols = np.arange(W, dtype=np.int64)[None, :]
    phases = ((rows * cols) % W).astype(np.float32) * np.float32(2.0 * math.pi / W)
    factor = np.float32(1.0 / math.sqrt(W))
    parts = []
    for res in range(4):
        part = phases[:, res::4]
        parts.append(np.concatenate([np.cos(part) * factor, np.sin(part) * factor], 1))
    return np.stack(parts).astype(jnp.bfloat16)


def low_half(shape):
    return lax.broadcasted_iota(jnp.int32, shape, 1) < BAND


def swap(x):
    return pltpu.roll(x, BAND, 1)


def times_i(x):
    s = swap(x)
    return jnp.where(low_half(x.shape), -s, s)


def dft(x_ref, t_ref, g_ref, sign, emit):
    for res in range(4):
        x = x_ref[pl.ds(res, QUARTER, stride=4), :]
        ix = times_i(x)
        if sign < 0:
            ix = -ix
        operand = jnp.concatenate([x.astype(BF16), ix.astype(BF16)], 0)
        g_ref[res] = jnp.dot(t_ref[res], operand, preferred_element_type=F32)

    def combine(step, carry):
        rows = pl.ds(pl.multiple_of(step * 128, 128), 128)
        g0, g1, g2, g3 = g_ref[0, rows, :], g_ref[1, rows, :], g_ref[2, rows, :], g_ref[3, rows, :]
        h0, h1, h2 = g0 + g2, g0 - g2, g1 + g3
        h3 = times_i(g1 - g3)
        if sign < 0:
            h3 = -h3
        emit(0, step, h0 + h2)
        emit(1, step, h1 + h3)
        emit(2, step, h0 - h2)
        emit(3, step, h1 - h3)
        return carry

    lax.fori_loop(0, QUARTER // 128, combine, 0)


def emit_turned(out_ref):
    def emit(r, step, value):
        turned = value.T
        a, b = turned[:BAND], turned[BAND:]
        low = low_half(a.shape)
        first = jnp.where(low, a, swap(b)).astype(BF16)
        second = jnp.where(low, swap(a), b).astype(BF16)
        base = pl.multiple_of(r * QUARTER + step * 128, 128)
        out_ref[pl.ds(base, BAND), :] = first
        out_ref[pl.ds(pl.multiple_of(base + BAND, BAND), BAND), :] = second

    return emit


def gather_kernel(off_ref, spec_ref, out_ref):
    col = off_ref[1]
    tile = col // 128
    lo = col - tile * 128
    shift = lax.rem(128 - lo, 128)
    lanes = lax.broadcasted_iota(jnp.int32, (128, 128), 1)
    keep = lanes < 128 - lo
    low = lanes < BAND

    def load(k, t):
        t = jnp.minimum(tile + t, NC // 128 - 1)
        x = spec_ref[k, :, pl.ds(pl.multiple_of(t * 128, 128), 128)]
        return pltpu.roll(x, shift, 1)

    def step(t, carry):
        nxt = (load(0, t + 1), load(1, t + 1))
        a = jnp.where(keep, carry[0], nxt[0])
        b = jnp.where(keep, carry[1], nxt[1])
        base = pl.multiple_of(t * 256, 256)
        out_ref[pl.ds(base, 128), :] = jnp.where(low, a, swap(b)).astype(BF16)
        out_ref[pl.ds(pl.multiple_of(base + 128, 128), 128), :] = jnp.where(low, swap(a), b).astype(BF16)
        return nxt

    lax.fori_loop(0, W // 128, step, (load(0, 0), load(1, 0)))


def prepare_kernel(pupil_ref, intensity_ref, pr_ref, pi_ref, root_ref):
    def step(t, carry):
        rows = pl.ds(pl.multiple_of(t * 128, 128), 128)
        x = jnp.concatenate([pupil_ref[0, :, rows], pupil_ref[1, :, rows]], 0).T
        s = swap(x)
        low = low_half(x.shape)
        pr_ref[rows, :] = jnp.where(low, x, s)
        pi_ref[rows, :] = jnp.where(low, -s, x)
        v = jnp.sqrt(intensity_ref[0, :, rows])
        root_ref[rows, :] = jnp.concatenate([v, v], 0).T
        return carry

    lax.fori_loop(0, W // 128, step, 0)


def first_kernel(off_ref, recv_ref, pr_ref, pi_ref, t_ref, out_ref, win_ref, wide_ref, x_ref, g_ref):
    row = off_ref[0]
    base = jnp.minimum(row // 16 * 16, 2 * W - (W + 16))
    off = row - base

    def widen(step, carry):
        src = pl.ds(pl.multiple_of(base + step * 48, 16), 48)
        wide_ref[pl.ds(pl.multiple_of(step * 48, 16), 48), :] = recv_ref[src, :].astype(F32)
        return carry

    lax.fori_loop(0, (W + 16) // 48, widen, 0)

    def multiply(step, carry):
        rows = pl.ds(pl.multiple_of(step * 128, 128), 128)
        w = wide_ref[pl.ds(off + step * 128, 128), :]
        product = w * pr_ref[rows, :] + swap(w) * pi_ref[rows, :]
        win_ref[rows, :] = w.astype(BF16)
        x_ref[rows, :] = product.astype(BF16).astype(F32)
        return carry

    lax.fori_loop(0, W // 128, multiply, 0)
    dft(x_ref, t_ref, g_ref, 1, emit_turned(out_ref))


def widen_rows(recv_ref, x_ref):
    def widen(step, carry):
        rows = pl.ds(pl.multiple_of(step * 128, 128), 128)
        x_ref[rows, :] = recv_ref[rows, :].astype(F32)
        return carry

    lax.fori_loop(0, W // 128, widen, 0)


def middle_kernel(recv_ref, root_ref, t_ref, out_ref, x_ref, y_ref, g_ref):
    widen_rows(recv_ref, x_ref)

    def replace(r, step, value):
        squared = value * value
        magnitude = jnp.sqrt(squared + swap(squared))
        rows = pl.ds(pl.multiple_of(r * QUARTER + step * 128, 128), 128)
        scaling = root_ref[rows, :] / jnp.maximum(magnitude, AMPLITUDE_FLOOR)
        y_ref[rows, :] = (value * scaling).astype(BF16).astype(F32)

    dft(x_ref, t_ref, g_ref, 1, replace)
    dft(y_ref, t_ref, g_ref, -1, emit_turned(out_ref))


def last_kernel(off_ref, recv_ref, win_ref, pr_ref, pi_ref, t_ref, grad_ref, corr_ref, x_ref, c_ref, g_ref):
    row = off_ref[0]
    widen_rows(recv_ref, x_ref)

    def update(r, step, estimate):
        start = r * QUARTER + step * 128
        rows = pl.ds(pl.multiple_of(start, 128), 128)
        w = win_ref[rows, :].astype(F32)
        pr, pi = pr_ref[rows, :], pi_ref[rows, :]
        ws = swap(w)
        low = low_half(w.shape)
        change = estimate - (w * pr + ws * pi)
        cs = swap(change)
        wr = jnp.where(low, w, ws)
        wi = jnp.where(low, ws, -w)
        grad_ref[rows, :] = (change * wr + cs * wi).astype(BF16)
        c_ref[pl.ds(row + start, 128), :] = (change * pr - cs * pi) / (pr * pr + pi * pi + PUPIL_DAMPING)

    c_ref[...] = jnp.zeros_like(c_ref)
    dft(x_ref, t_ref, g_ref, -1, update)

    def store(step, carry):
        rows = pl.ds(pl.multiple_of(step * 128, 128), 128)
        corr_ref[rows, :] = c_ref[rows, :].astype(BF16)
        return carry

    lax.fori_loop(0, 2 * W // 128, store, 0)


def place_kernel(off_ref, recv_ref, out_ref):
    col = off_ref[1]
    tile = col // 128
    lo = col - tile * 128
    lanes = lax.broadcasted_iota(jnp.int32, (128, 128), 1)
    low = lanes < BAND
    take = lanes >= lo
    out_ref[...] = jnp.zeros_like(out_ref)

    def put(k, t, value):
        t = jnp.minimum(tile + t, NC // 128 - 1)
        out_ref[k, :, pl.ds(pl.multiple_of(t * 128, 128), 128)] = value.astype(BF16)

    def step(t, carry):
        base = pl.multiple_of(t * 256, 256)
        x = recv_ref[pl.ds(base, 128), :].astype(F32)
        y = recv_ref[pl.ds(pl.multiple_of(base + 128, 128), 128), :].astype(F32)
        a = pltpu.roll(jnp.where(low, x, swap(y)), lo, 1)
        b = pltpu.roll(jnp.where(low, swap(x), y), lo, 1)
        put(0, t, jnp.where(take, a, carry[0]))
        put(1, t, jnp.where(take, b, carry[1]))
        return a, b

    zero = jnp.zeros((128, 128), F32)
    a, b = lax.fori_loop(0, W // 128, step, (zero, zero))

    @pl.when(lo > 0)
    def _():
        put(0, W // 128, jnp.where(take, 0.0, a))
        put(1, W // 128, jnp.where(take, 0.0, b))


def finish_kernel(spec_ref, update_ref, grad_ref, new_ref, out_ref):
    for k in range(2):
        def add(step, carry):
            rows = pl.ds(pl.multiple_of(step * 16, 16), 16)
            new_ref[k, rows, :] = spec_ref[k, rows, :] + update_ref[k, rows, :].astype(F32)
            return carry

        lax.fori_loop(0, 8, add, 0)

    def turn(t, carry):
        rows = pl.ds(pl.multiple_of(t * 128, 128), 128)
        x = grad_ref[rows, :].astype(F32).T
        out_ref[0, :, rows] = x[:BAND]
        out_ref[1, :, rows] = x[BAND:]
        return carry

    lax.fori_loop(0, W // 128, turn, 0)


def call(kernel, outs, scalars, arrays, scratch=(), flops=0):
    shapes = [jax.ShapeDtypeStruct(s, d) for s, d in outs]
    moved = sum(math.prod(s) * jnp.dtype(d).itemsize for s, d in outs)
    moved += sum(a.size * a.dtype.itemsize for a in arrays)
    return pl.pallas_call(
        kernel,
        out_shape=shapes,
        in_specs=[pl.BlockSpec(memory_space=pltpu.SMEM)] * len(scalars)
        + [pl.BlockSpec(memory_space=VMEM)] * len(arrays),
        out_specs=[pl.BlockSpec(memory_space=VMEM)] * len(outs),
        scratch_shapes=list(scratch),
        compiler_params=pltpu.CompilerParams(vmem_limit_bytes=40 * MIB),
        cost_estimate=pl.CostEstimate(flops=flops, bytes_accessed=moved, transcendentals=0),
    )(*scalars, *arrays)


def turn_bands(values):
    blocks = values.reshape(32, -1, 128)
    return lax.all_to_all(blocks, "slab", 0, 0).reshape(-1, 128)


def ring_gather(piece):
    forward = backward = piece
    found = [(0, piece)]
    for hop in range(1, 5):
        forward = lax.ppermute(forward, "led", [(i, (i + 1) % 8) for i in range(8)])
        found.append((hop, forward))
        if hop < 4:
            backward = lax.ppermute(backward, "led", [(i, (i - 1) % 8) for i in range(8)])
            found.append((-hop, backward))
    me = lax.axis_index("led")
    out = jnp.zeros((8,) + piece.shape, piece.dtype)
    for hop, value in found:
        out = lax.dynamic_update_index_in_dim(out, value, (me - hop) % 8, 0)
    return out


def per_device(spectrum, pupil, intensity, row_offsets, col_offsets):
    led = lax.axis_index("led")
    offsets = jnp.stack([row_offsets[led], col_offsets[led]])
    tab = jnp.asarray(table())
    rows128 = (W, 128)
    flops = 8 * QUARTER * 1024 * 128

    (outgoing,) = call(gather_kernel, [((2 * W, 128), BF16)], [offsets], [spectrum])
    arrived = turn_bands(outgoing)
    pr, pi, root = call(prepare_kernel, [(rows128, F32)] * 3, [], [pupil, intensity])
    scratch = [VMEM(rows128, F32), VMEM((4, QUARTER, 128), F32)]
    first, window = call(
        first_kernel,
        [(rows128, BF16), (rows128, BF16)],
        [offsets],
        [arrived, pr, pi, tab],
        [VMEM((W + 16, 128), F32)] + scratch,
        flops,
    )
    turned = turn_bands(first)
    (second,) = call(
        middle_kernel, [(rows128, BF16)], [], [turned, root, tab], [VMEM(rows128, F32)] + scratch, 2 * flops
    )
    returned = turn_bands(second)
    gradient, correction = call(
        last_kernel,
        [(rows128, BF16), ((2 * W, 128), BF16)],
        [offsets],
        [returned, window, pr, pi, tab],
        [VMEM(rows128, F32), VMEM((2 * W, 128), F32), VMEM((4, QUARTER, 128), F32)],
        flops,
    )
    grad_part = lax.psum_scatter(gradient.reshape(8, W // 8, 128), "led", scatter_dimension=0)
    landed = turn_bands(correction)
    (placed,) = call(place_kernel, [((2, 128, NC), BF16)], [offsets], [landed])
    update_part = lax.psum_scatter(placed.reshape(2, 8, 16, NC), "led", scatter_dimension=1)
    grad_total = ring_gather(grad_part).reshape(rows128)
    update_total = jnp.swapaxes(ring_gather(update_part), 0, 1).reshape(2, 128, NC)
    new_spectrum, grad = call(
        finish_kernel,
        [((2, 128, NC), F32), ((2, BAND, W), F32)],
        [],
        [spectrum, update_total, grad_total],
    )
    return new_spectrum, grad


def solution(mesh):
    in_specs = (P(None, "slab", None), P(None, "slab", None), P("led", "slab", None), P(), P())
    out_specs = (P(None, "slab", None), P(None, "slab", None))
    return jax.shard_map(per_device, mesh=mesh, in_specs=in_specs, out_specs=out_specs, check_vma=False)
```

time: 797 us -> 211 us (0.26); the launches traced: 788 us -> 211 us
  matrix products: 506 us -> 0 us
  waiting for transfers between devices: 124 us -> 75.2 us
  local copies, waits for them, and re-layouts: 50 us -> 13.2 us
  Pallas kernels: 0 us -> 27.9 us
  starting transfers between devices: 7.79 us -> 27.4 us
  other arithmetic: 17.9 us -> 1.37 us
  blocking collectives: 63.4 us -> 51.3 us
    dot_general x8 -> x0, matrix products: 506 us -> none  [the longest x2 127 us: transform(): jnp.dot(flattened, sine_table, preferred_element_type=jnp.float32)]
    psum x1 -> x0, waiting for transfers between devices: 110 us -> none  [per_device(): grad_total, update_total = lax.psum((gradient, update), 'led')]
    ppermute x0 -> x14, waiting for transfers between devices: none -> 33.7 us  [the longest x8 33.7 us: ring_gather(): forward = lax.ppermute(forward, 'led', [(i, (i + 1) % 8) for i in range(8)])]
    reduce_scatter x0 -> x2, waiting for transfers between devices: none -> 31.3 us  [the longest x1 19.3 us: per_device(): lax.psum_scatter(placed.reshape(2, 8, 16, NC), 'led', scatter_dimension=1)]
    pallas_call x0 -> x7, Pallas kernels: none -> 27.9 us  [call(): pl.pallas_call(kernel, out_shape=shapes, in_specs=[pl.BlockSpec(memory_sp...]
    ppermute x0 -> x14, starting transfers between devices: none -> 19.7 us  [the longest x6 16.8 us: ring_gather(): lax.ppermute(backward, 'led', [(i, (i - 1) % 8) for i in range(8)])]
    all_to_all x3, blocking collectives: 63.4 us -> 51.3 us  [turn_bands(): return lax.all_to_all(blocks, 'slab', 0, 0).reshape(-1, 128)]
    dynamic_update_slice x2 -> x16, local copies, waits for them, and re-layouts: 11.7 us -> 1.1 us  [ring_gather(): out = lax.dynamic_update_index_in_dim(out, value, (me - hop) % 8, 0)]
  transfers between devices with their start and end apart: 2 -> 17, of which waited for: 2 -> 11; matrix products, arithmetic and copies ran while one was open for 0% -> 1% of each run, Pallas kernels for 0% -> 3%
where the time goes in v1:
time: 211 us
  waiting for transfers between devices  75.2 us (36%)
  blocking collectives  51.3 us (24%)
  Pallas kernels  27.9 us (13%)
  starting transfers between devices  27.4 us (13%)
  between operations  14.4 us (7%)
  local copies, waits for them, and re-layouts  13.2 us (6%)
    all_to_all x3, blocking collectives, turn_bands(): return lax.all_to_all(blocks, 'slab', 0, 0).reshape(-1, 128)  51.3 us
    ppermute x8, waiting for transfers between devices, ring_gather(): forward = lax.ppermute(forward, 'led', [(i, (i + 1) % 8) for i in range(8)])  33.7 us
    pallas_call x7, Pallas kernels, call(): pl.pallas_call(kernel, out_shape=shapes, in_specs=[pl.BlockSpec(memory_sp...  27.9 us
    reduce_scatter x1, waiting for transfers between devices, per_device(): lax.psum_scatter(placed.reshape(2, 8, 16, NC), 'led', scatter_dimension=1)  19.3 us
    ppermute x6, starting transfers between devices, ring_gather(): lax.ppermute(backward, 'led', [(i, (i - 1) % 8) for i in range(8)])  16.8 us
    reduce_scatter x1, waiting for transfers between devices, per_device(): lax.psum_scatter(gradient.reshape(8, W // 8, 128), 'led', scatter_dimensi...  12 us
    all_to_all x1, waiting for transfers between devices, turn_bands(): return lax.all_to_all(blocks, 'slab', 0, 0).reshape(-1, 128)  10.1 us
    unnamed x20, local copies, waits for them, and re-layouts  8.11 us
  transfers between devices with their start and end apart: 17, of which 11 were waited for; matrix products, arithmetic and copies ran while one was open for 1% of the time, Pallas kernels for 3%

profile of v1, /device:TPU:2, one launch (start us, length us, event | category | flops | bytes accessed | tf_op | source)
XLA Modules:
  0.0 210.7 jit_solution(10683244722694304122)
XLA Ops:
  12.9 4.4 %shard_map.77 = bf16[4096,128]{1,0:T(8,128)(2,1)} custom-call(s32[2]{0:T(128)S(1)} %pad_add_fusion.off_ref, f32[2,128,3072]{2,1,0:T(8,128)S(1)} %copy-done.2), custom_call_target="tpu_custom_call" | custom-call | bytes 4194304 | tf_op jit(solution)/shard_map/pallas_call | solution.py:261
  17.3 7.6 %all-to-all-start = ((bf16[32,128,128]{2,1,0:T(8,128)(2,1)}), bf16[32,128,128]{2,1,0:T(8,128)(2,1)S(1)}, u32[]{:S(2)}, u32[]{:S(2)}) async-start(bf16[32,128,128]{2,1,0:T(8,128)(2,1)} %bitcast), calls=%async_computation | async-start | bytes 2097152 | tf_op jit(solution)/shard_map/all_to_all | solution.py:275
  27.2 2.7 %shard_map.78 = (f32[2048,128]{1,0:T(8,128)S(1)}, f32[2048,128]{1,0:T(8,128)S(1)}, f32[2048,128]{1,0:T(8,128)S(1)}) custom-call(f32[2,64,2048]{2,1,0:T(8,128)S(1)} %copy-done.4, f32[1,64,2048]{2,1,0:T(8,128)S(1)} %copy-done.7), custom_call_target="tpu_custom_call" | custom-call | bytes 4718592 | tf_op jit(solution)/shard_map/pallas_call | solution.py:261
  30.9 10.1 %all-to-all-done = bf16[32,128,128]{2,1,0:T(8,128)(2,1)S(1)} async-done(((bf16[32,128,128]{2,1,0:T(8,128)(2,1)}), bf16[32,128,128]{2,1,0:T(8,128)(2,1)S(1)}, u32[]{:S(2)}, u32[]{:S(2)}) %all-to-all-start) | async-done | bytes 1048608 | tf_op jit(solution)/shard_map/all_to_all | solution.py:275
  43.2 5.1 %shard_map.79 = (bf16[2048,128]{1,0:T(8,128)(2,1)S(1)}, bf16[2048,128]{1,0:T(8,128)(2,1)S(1)}) custom-call(s32[2]{0:T(128)S(1)} %pad_add_fusion.off_ref, bf16[4096,128]{1,0:T(8,128)(2,1)S(1)} %bitcast.63, f32[2048,128]{1,0:T(8,128)S(1)} %get-tuple-element.9.pr_ref, f32[2048,128]{1,0:T(8,128)S(1)} %get-tuple-element.10.pi_ref, bf16[4,512,1024]{2,1,0:T(8,128)(2,1)S(1)} %copy-done), custom_call_target="tpu_custom_call" | custom-call | flops 536870912 | bytes 8388608 | tf_op jit(solution)/shard_map/pallas_call | solution.py:261
  48.3 15.2 %all_to_all.20 = bf16[32,64,128]{2,1,0:T(8,128)(2,1)S(1)} all-to-all(bf16[32,64,128]{2,1,0:T(8,128)(2,1)S(1)} %bitcast.70), channel_id=1, replica_groups=mesh['slab'=32,'led'=8] {'slab'}, dimensions={0} | all-to-all | bytes 1048576 | tf_op jit(solution)/shard_map/all_to_all | solution.py:275
  63.6 5.1 %shard_map.80 = bf16[2048,128]{1,0:T(8,128)(2,1)S(1)} custom-call(bf16[2048,128]{1,0:T(8,128)(2,1)S(1)} %bitcast.64, f32[2048,128]{1,0:T(8,128)S(1)} %copy-done.6, bf16[4,512,1024]{2,1,0:T(8,128)(2,1)S(1)} %copy-done.1), custom_call_target="tpu_custom_call" | custom-call | flops 1073741824 | bytes 6291456 | tf_op jit(solution)/shard_map/pallas_call | solution.py:261
  68.7 15.2 %all_to_all.21 = bf16[32,64,128]{2,1,0:T(8,128)(2,1)S(1)} all-to-all(bf16[32,64,128]{2,1,0:T(8,128)(2,1)S(1)} %bitcast.65), channel_id=1, replica_groups=mesh['slab'=32,'led'=8] {'slab'}, dimensions={0} | all-to-all | bytes 1048576 | tf_op jit(solution)/shard_map/all_to_all | solution.py:275
  83.9 3.3 %shard_map.81 = (bf16[2048,128]{1,0:T(8,128)(2,1)S(1)}, bf16[4096,128]{1,0:T(8,128)(2,1)S(1)}) custom-call(s32[2]{0:T(128)S(1)} %pad_add_fusion.off_ref, bf16[2048,128]{1,0:T(8,128)(2,1)S(1)} %bitcast.67, bf16[2048,128]{1,0:T(8,128)(2,1)S(1)} %get-tuple-element.13.win_ref, f32[2048,128]{1,0:T(8,128)S(1)} %get-tuple-element.9.pr_ref, ...), custom_call_target="tpu_custom_call" | custom-call | flops 536870912 | bytes 8912896 | tf_op jit(solution)/shard_map/pallas_call | solution.py:261
  88.1 20.8 %all_to_all.22 = bf16[32,128,128]{2,1,0:T(8,128)(2,1)S(1)} all-to-all(bf16[32,128,128]{2,1,0:T(8,128)(2,1)S(1)} %bitcast.68), channel_id=1, replica_groups=mesh['slab'=32,'led'=8] {'slab'}, dimensions={0} | all-to-all | bytes 2097152 | tf_op jit(solution)/shard_map/all_to_all | solution.py:275
  108.9 3.5 %shard_map.82 = bf16[2,128,3072]{2,1,0:T(8,128)(2,1)S(1)} custom-call(s32[2]{0:T(128)S(1)} %pad_add_fusion.off_ref, bf16[4096,128]{1,0:T(8,128)(2,1)S(1)} %bitcast.62), custom_call_target="tpu_custom_call" | custom-call | bytes 2621440 | tf_op jit(solution)/shard_map/pallas_call | solution.py:261
  113.8 12.0 %reduce-scatter.5.cloned.1.call-done = bf16[1,256,128]{2,1,0:T(8,128)(2,1)} async-done(((bf16[8,256,128]{2,1,0:T(8,128)(2,1)}), bf16[1,256,128]{2,1,0:T(8,128)(2,1)}) %reduce-scatter.5.cloned.1.call-update) | async-done | bytes 65552 | tf_op jit(solution)/shard_map/reduce_scatter | solution.py:326
  126.7 2.4 %collective-permute-start.8 = (bf16[256,128]{1,0:T(8,128)(2,1)}, bf16[256,128]{1,0:T(8,128)(2,1)S(1)}, u32[]{:S(2)}, u32[]{:S(2)}) collective-permute-start(bf16[256,128]{1,0:T(8,128)(2,1)} %bitcast.74), channel_id=1, source_target_pairs={{0,7},{1,0},{2,1},{3,2},{4,3},{5,4},{6,5},{7,6},{8,15},{9,8},{10,9... | collective-permute-start | bytes 196616 | tf_op jit(solution)/shard_map/ppermute | solution.py:285
  131.5 3.2 %collective-permute-start.10 = (bf16[256,128]{1,0:T(8,128)(2,1)S(1)}, bf16[256,128]{1,0:T(8,128)(2,1)S(1)}, u32[]{:S(2)}, u32[]{:S(2)}) collective-permute-start(bf16[256,128]{1,0:T(8,128)(2,1)S(1)} %collective-permute-done.8), channel_id=1, source_target_pairs={{0,7},{1,0},{2,1},{3,2},{4,3},{5,4},{6,5},{7,6},{8,15},{9,8},{10,9... | collective-permute-start | bytes 196616 | tf_op jit(solution)/shard_map/ppermute | solution.py:285
  137.0 3.2 %collective-permute-start.12 = (bf16[256,128]{1,0:T(8,128)(2,1)S(1)}, bf16[256,128]{1,0:T(8,128)(2,1)S(1)}, u32[]{:S(2)}, u32[]{:S(2)}) collective-permute-start(bf16[256,128]{1,0:T(8,128)(2,1)S(1)} %collective-permute-done.10), channel_id=1, source_target_pairs={{0,7},{1,0},{2,1},{3,2},{4,3},{5,4},{6,5},{7,6},{8,15},{9,8},{10,9... | collective-permute-start | bytes 196616 | tf_op jit(solution)/shard_map/ppermute | solution.py:285
  142.5 6.4 %collective-permute-done.13 = bf16[256,128]{1,0:T(8,128)(2,1)S(1)} collective-permute-done((bf16[256,128]{1,0:T(8,128)(2,1)S(1)}, bf16[256,128]{1,0:T(8,128)(2,1)S(1)}, u32[]{:S(2)}, u32[]{:S(2)}) %collective-permute-start.13) | collective-permute-done | bytes 65568 | tf_op jit(solution)/shard_map/ppermute | solution.py:282
  148.9 19.3 %reduce-scatter.3.cloned.1.call-done = bf16[2,1,16,3072]{3,2,0,1:T(8,128)(2,1)} async-done(((bf16[2,8,16,3072]{3,2,0,1:T(8,128)(2,1)}), bf16[2,1,16,3072]{3,2,0,1:T(8,128)(2,1)}) %reduce-scatter.3.cloned.1.call-update) | async-done | bytes 196624 | tf_op jit(solution)/shard_map/reduce_scatter | solution.py:329
  171.7 5.0 %collective-permute-done = bf16[2,16,3072]{2,1,0:T(8,128)(2,1)S(1)} collective-permute-done((bf16[2,16,3072]{2,1,0:T(8,128)(2,1)}, bf16[2,16,3072]{2,1,0:T(8,128)(2,1)S(1)}, u32[]{:S(2)}, u32[]{:S(2)}) %collective-permute-start) | collective-permute-done | bytes 196640 | tf_op jit(solution)/shard_map/ppermute | solution.py:282
  177.3 2.8 %collective-permute-start.3 = (bf16[2,16,3072]{2,1,0:T(8,128)(2,1)S(1)}, bf16[2,16,3072]{2,1,0:T(8,128)(2,1)S(1)}, u32[]{:S(2)}, u32[]{:S(2)}) collective-permute-start(bf16[2,16,3072]{2,1,0:T(8,128)(2,1)S(1)} %collective-permute-done.1), channel_id=1, source_target_pairs={{0,7},{1,0},{2,1},{3,2},{4,3},{5,4},{6,5},{7,6},{8,15},{9,8},{10,9... | collective-permute-start | bytes 589832 | tf_op jit(solution)/shard_map/ppermute | solution.py:285
  180.2 5.1 %collective-permute-done.2 = bf16[2,16,3072]{2,1,0:T(8,128)(2,1)S(1)} collective-permute-done((bf16[2,16,3072]{2,1,0:T(8,128)(2,1)S(1)}, bf16[2,16,3072]{2,1,0:T(8,128)(2,1)S(1)}, u32[]{:S(2)}, u32[]{:S(2)}) %collective-permute-start.2) | collective-permute-done | bytes 196640 | tf_op jit(solution)/shard_map/ppermute | solution.py:282
  185.3 3.3 %collective-permute-start.5 = (bf16[2,16,3072]{2,1,0:T(8,128)(2,1)S(1)}, bf16[2,16,3072]{2,1,0:T(8,128)(2,1)S(1)}, u32[]{:S(2)}, u32[]{:S(2)}) collective-permute-start(bf16[2,16,3072]{2,1,0:T(8,128)(2,1)S(1)} %collective-permute-done.3), channel_id=1, source_target_pairs={{0,7},{1,0},{2,1},{3,2},{4,3},{5,4},{6,5},{7,6},{8,15},{9,8},{10,9... | collective-permute-start | bytes 589832 | tf_op jit(solution)/shard_map/ppermute | solution.py:285
  188.6 4.5 %collective-permute-done.4 = bf16[2,16,3072]{2,1,0:T(8,128)(2,1)S(1)} collective-permute-done((bf16[2,16,3072]{2,1,0:T(8,128)(2,1)S(1)}, bf16[2,16,3072]{2,1,0:T(8,128)(2,1)S(1)}, u32[]{:S(2)}, u32[]{:S(2)}) %collective-permute-start.4) | collective-permute-done | bytes 196640 | tf_op jit(solution)/shard_map/ppermute | solution.py:282
  193.2 6.8 %collective-permute-done.6 = bf16[2,16,3072]{2,1,0:T(8,128)(2,1)S(1)} collective-permute-done((bf16[2,16,3072]{2,1,0:T(8,128)(2,1)S(1)}, bf16[2,16,3072]{2,1,0:T(8,128)(2,1)S(1)}, u32[]{:S(2)}, u32[]{:S(2)}) %collective-permute-start.6) | collective-permute-done | bytes 196640 | tf_op jit(solution)/shard_map/ppermute | solution.py:282
  200.0 3.9 %shard_map.83 = (f32[2,128,3072]{2,1,0:T(8,128)}, f32[2,64,2048]{2,1,0:T(8,128)}) custom-call(f32[2,128,3072]{2,1,0:T(8,128)S(1)} %copy-done.3, bf16[2,128,3072]{2,1,0:T(8,128)(2,1)S(1)} %bitcast.61, bf16[2048,128]{1,0:T(8,128)(2,1)S(1)} %bitcast.66), custom_call_target="tpu_custom_call" | custom-call | bytes 9437184 | tf_op jit(solution)/shard_map/pallas_call | solution.py:261
  (64 shorter events, 25.4 us)
Async XLA Ops:
  11.0 1.9 copy-start.2
  17.3 23.7 %all-to-all-start = ((bf16[32,128,128]{2,1,0:T(8,128)(2,1)}), bf16[32,128,128]{2,1,0:T(8,128)(2,1)S(1)}, u32[]{:S(2)}, u32[]{:S(2)}) async-start(bf16[32,128,128]{2,1,0:T(8,128)(2,1)} %bitcast), calls=%async_computation | async-start | bytes 2097152 | tf_op jit(solution)/shard_map/all_to_all | solution.py:275
  24.9 100.9 %reduce-scatter.5.cloned.1.call-start = ((), (), s32[]{:S(2)}) async-start(), calls=%async_computation.7 | async-start | bytes 589824 | tf_op jit(solution)/shard_map/reduce_scatter | solution.py:326
  25.0 1.2 copy-start.4
  41.0 2.2 %copy-start = (bf16[4,512,1024]{2,1,0:T(8,128)(2,1)S(1)}, bf16[4,512,1024]{2,1,0:T(8,128)(2,1)}, u32[]{:S(2)}) copy-start(bf16[4,512,1024]{2,1,0:T(8,128)(2,1)} %constant.124.clone.t_ref) | copy-start | bytes 12582916
  43.2 20.3 %copy-start.1 = (bf16[4,512,1024]{2,1,0:T(8,128)(2,1)S(1)}, bf16[4,512,1024]{2,1,0:T(8,128)(2,1)}, u32[]{:S(2)}) copy-start(bf16[4,512,1024]{2,1,0:T(8,128)(2,1)} %constant.124.clone.t_ref) | copy-start | bytes 12582916
  48.3 15.2 %copy-start.6 = (f32[2048,128]{1,0:T(8,128)S(1)}, f32[2048,128]{1,0:T(8,128)}, u32[]{:S(2)}) copy-start(f32[2048,128]{1,0:T(8,128)} %copy-done.5) | copy-start | bytes 3145732
  88.0 80.2 %reduce-scatter.3.cloned.1.call-start = ((), (), s32[]{:S(2)}) async-start(), calls=%async_computation.6 | async-start | bytes 1769472 | tf_op jit(solution)/shard_map/reduce_scatter | solution.py:329
  125.8 5.7 %collective-permute-start.7 = (bf16[256,128]{1,0:T(8,128)(2,1)}, bf16[256,128]{1,0:T(8,128)(2,1)S(1)}, u32[]{:S(2)}, u32[]{:S(2)}) collective-permute-start(bf16[256,128]{1,0:T(8,128)(2,1)} %bitcast.73), channel_id=1, source_target_pairs={{0,1},{1,2},{2,3},{3,4},{4,5},{5,6},{6,7},{7,0},{8,9},{9,10},{10,1... | collective-permute-start | bytes 196616 | tf_op jit(solution)/shard_map/ppermute | solution.py:282
  126.7 4.8 %collective-permute-start.8 = (bf16[256,128]{1,0:T(8,128)(2,1)}, bf16[256,128]{1,0:T(8,128)(2,1)S(1)}, u32[]{:S(2)}, u32[]{:S(2)}) collective-permute-start(bf16[256,128]{1,0:T(8,128)(2,1)} %bitcast.74), channel_id=1, source_target_pairs={{0,7},{1,0},{2,1},{3,2},{4,3},{5,4},{6,5},{7,6},{8,15},{9,8},{10,9... | collective-permute-start | bytes 196616 | tf_op jit(solution)/shard_map/ppermute | solution.py:285
  131.5 5.5 %collective-permute-start.9 = (bf16[256,128]{1,0:T(8,128)(2,1)S(1)}, bf16[256,128]{1,0:T(8,128)(2,1)S(1)}, u32[]{:S(2)}, u32[]{:S(2)}) collective-permute-start(bf16[256,128]{1,0:T(8,128)(2,1)S(1)} %collective-permute-done.7), channel_id=1, source_target_pairs={{0,1},{1,2},{2,3},{3,4},{4,5},{5,6},{6,7},{7,0},{8,9},{9,10},{10,1... | collective-permute-start | bytes 196616 | tf_op jit(solution)/shard_map/ppermute | solution.py:282
  131.5 5.5 %collective-permute-start.10 = (bf16[256,128]{1,0:T(8,128)(2,1)S(1)}, bf16[256,128]{1,0:T(8,128)(2,1)S(1)}, u32[]{:S(2)}, u32[]{:S(2)}) collective-permute-start(bf16[256,128]{1,0:T(8,128)(2,1)S(1)} %collective-permute-done.8), channel_id=1, source_target_pairs={{0,7},{1,0},{2,1},{3,2},{4,3},{5,4},{6,5},{7,6},{8,15},{9,8},{10,9... | collective-permute-start | bytes 196616 | tf_op jit(solution)/shard_map/ppermute | solution.py:285
  137.0 5.5 %collective-permute-start.11 = (bf16[256,128]{1,0:T(8,128)(2,1)S(1)}, bf16[256,128]{1,0:T(8,128)(2,1)S(1)}, u32[]{:S(2)}, u32[]{:S(2)}) collective-permute-start(bf16[256,128]{1,0:T(8,128)(2,1)S(1)} %collective-permute-done.9), channel_id=1, source_target_pairs={{0,1},{1,2},{2,3},{3,4},{4,5},{5,6},{6,7},{7,0},{8,9},{9,10},{10,1... | collective-permute-start | bytes 196616 | tf_op jit(solution)/shard_map/ppermute | solution.py:282
  137.0 5.5 %collective-permute-start.12 = (bf16[256,128]{1,0:T(8,128)(2,1)S(1)}, bf16[256,128]{1,0:T(8,128)(2,1)S(1)}, u32[]{:S(2)}, u32[]{:S(2)}) collective-permute-start(bf16[256,128]{1,0:T(8,128)(2,1)S(1)} %collective-permute-done.10), channel_id=1, source_target_pairs={{0,7},{1,0},{2,1},{3,2},{4,3},{5,4},{6,5},{7,6},{8,15},{9,8},{10,9... | collective-permute-start | bytes 196616 | tf_op jit(solution)/shard_map/ppermute | solution.py:285
  142.4 6.5 %collective-permute-start.13 = (bf16[256,128]{1,0:T(8,128)(2,1)S(1)}, bf16[256,128]{1,0:T(8,128)(2,1)S(1)}, u32[]{:S(2)}, u32[]{:S(2)}) collective-permute-start(bf16[256,128]{1,0:T(8,128)(2,1)S(1)} %collective-permute-done.11), channel_id=1, source_target_pairs={{0,1},{1,2},{2,3},{3,4},{4,5},{5,6},{6,7},{7,0},{8,9},{9,10},{10,1... | collective-permute-start | bytes 196616 | tf_op jit(solution)/shard_map/ppermute | solution.py:282
  168.2 3.4 %copy-start.9 = (bf16[2,1,16,3072]{3,2,0,1:T(8,128)(2,1)S(1)}, bf16[2,1,16,3072]{3,2,0,1:T(8,128)(2,1)}, u32[]{:S(2)}) copy-start(bf16[2,1,16,3072]{3,2,0,1:T(8,128)(2,1)} %reduce-scatter.3.cloned.1.call-done) | copy-start | bytes 589828
  168.2 8.4 %collective-permute-start = (bf16[2,16,3072]{2,1,0:T(8,128)(2,1)}, bf16[2,16,3072]{2,1,0:T(8,128)(2,1)S(1)}, u32[]{:S(2)}, u32[]{:S(2)}) collective-permute-start(bf16[2,16,3072]{2,1,0:T(8,128)(2,1)} %bitcast.71), channel_id=1, source_target_pairs={{0,1},{1,2},{2,3},{3,4},{4,5},{5,6},{6,7},{7,0},{8,9},{9,10},{10,1... | collective-permute-start | bytes 589832 | tf_op jit(solution)/shard_map/ppermute | solution.py:282
  169.6 7.7 %collective-permute-start.1 = (bf16[2,16,3072]{2,1,0:T(8,128)(2,1)}, bf16[2,16,3072]{2,1,0:T(8,128)(2,1)S(1)}, u32[]{:S(2)}, u32[]{:S(2)}) collective-permute-start(bf16[2,16,3072]{2,1,0:T(8,128)(2,1)} %bitcast.72), channel_id=1, source_target_pairs={{0,7},{1,0},{2,1},{3,2},{4,3},{5,4},{6,5},{7,6},{8,15},{9,8},{10,9... | collective-permute-start | bytes 589832 | tf_op jit(solution)/shard_map/ppermute | solution.py:285
  171.7 28.3 %copy-start.3 = (f32[2,128,3072]{2,1,0:T(8,128)S(1)}, f32[2,128,3072]{2,1,0:T(8,128)}, u32[]{:S(2)}) copy-start(f32[2,128,3072]{2,1,0:T(8,128)} %spec_ref.3) | copy-start | bytes 9437188
  176.7 8.6 %collective-permute-start.2 = (bf16[2,16,3072]{2,1,0:T(8,128)(2,1)S(1)}, bf16[2,16,3072]{2,1,0:T(8,128)(2,1)S(1)}, u32[]{:S(2)}, u32[]{:S(2)}) collective-permute-start(bf16[2,16,3072]{2,1,0:T(8,128)(2,1)S(1)} %collective-permute-done), channel_id=1, source_target_pairs={{0,1},{1,2},{2,3},{3,4},{4,5},{5,6},{6,7},{7,0},{8,9},{9,10},{10,1... | collective-permute-start | bytes 589832 | tf_op jit(solution)/shard_map/ppermute | solution.py:282
  177.3 8.0 %collective-permute-start.3 = (bf16[2,16,3072]{2,1,0:T(8,128)(2,1)S(1)}, bf16[2,16,3072]{2,1,0:T(8,128)(2,1)S(1)}, u32[]{:S(2)}, u32[]{:S(2)}) collective-permute-start(bf16[2,16,3072]{2,1,0:T(8,128)(2,1)S(1)} %collective-permute-done.1), channel_id=1, source_target_pairs={{0,7},{1,0},{2,1},{3,2},{4,3},{5,4},{6,5},{7,6},{8,15},{9,8},{10,9... | collective-permute-start | bytes 589832 | tf_op jit(solution)/shard_map/ppermute | solution.py:285
  185.3 7.8 %collective-permute-start.4 = (bf16[2,16,3072]{2,1,0:T(8,128)(2,1)S(1)}, bf16[2,16,3072]{2,1,0:T(8,128)(2,1)S(1)}, u32[]{:S(2)}, u32[]{:S(2)}) collective-permute-start(bf16[2,16,3072]{2,1,0:T(8,128)(2,1)S(1)} %collective-permute-done.2), channel_id=1, source_target_pairs={{0,1},{1,2},{2,3},{3,4},{4,5},{5,6},{6,7},{7,0},{8,9},{9,10},{10,1... | collective-permute-start | bytes 589832 | tf_op jit(solution)/shard_map/ppermute | solution.py:282
  185.3 7.8 %collective-permute-start.5 = (bf16[2,16,3072]{2,1,0:T(8,128)(2,1)S(1)}, bf16[2,16,3072]{2,1,0:T(8,128)(2,1)S(1)}, u32[]{:S(2)}, u32[]{:S(2)}) collective-permute-start(bf16[2,16,3072]{2,1,0:T(8,128)(2,1)S(1)} %collective-permute-done.3), channel_id=1, source_target_pairs={{0,7},{1,0},{2,1},{3,2},{4,3},{5,4},{6,5},{7,6},{8,15},{9,8},{10,9... | collective-permute-start | bytes 589832 | tf_op jit(solution)/shard_map/ppermute | solution.py:285
  193.1 6.9 %collective-permute-start.6 = (bf16[2,16,3072]{2,1,0:T(8,128)(2,1)S(1)}, bf16[2,16,3072]{2,1,0:T(8,128)(2,1)S(1)}, u32[]{:S(2)}, u32[]{:S(2)}) collective-permute-start(bf16[2,16,3072]{2,1,0:T(8,128)(2,1)S(1)} %collective-permute-done.4), channel_id=1, source_target_pairs={{0,1},{1,2},{2,3},{3,4},{4,5},{5,6},{6,7},{7,0},{8,9},{9,10},{10,1... | collective-permute-start | bytes 589832 | tf_op jit(solution)/shard_map/ppermute | solution.py:282
  (3 other events, 2.8 us)
Sparse Core Ops, SparseCore 0:
  88.1 37.6 reduce-scatter.4
  129.1 39.0 reduce-scatter.2

commit v2 on v1

v2 whole, which is shorter than its diff:
```python
import functools
import math

import jax
import jax.numpy as jnp
import numpy as np
from jax import lax
from jax.experimental import pallas as pl
from jax.experimental.pallas import tpu as pltpu
from jax.sharding import PartitionSpec as P

W = 2048
QUARTER = W // 4
BAND = 64
NC = 3072
AMPLITUDE_FLOOR = 0.5
PUPIL_DAMPING = 0.5
MIB = 1024 * 1024

VMEM = pltpu.VMEM
F32 = jnp.float32
BF16 = jnp.bfloat16


def table():
    rows = np.arange(QUARTER, dtype=np.int64)[:, None]
    cols = np.arange(W, dtype=np.int64)[None, :]
    phases = ((rows * cols) % W).astype(np.float32) * np.float32(2.0 * math.pi / W)
    factor = np.float32(1.0 / math.sqrt(W))
    parts = []
    for res in range(4):
        part = phases[:, res::4]
        parts.append(np.concatenate([np.cos(part) * factor, np.sin(part) * factor], 1))
    return np.stack(parts).astype(jnp.bfloat16)


def low_half(shape):
    return lax.broadcasted_iota(jnp.int32, shape, 1) < BAND


def swap(x):
    return pltpu.roll(x, BAND, 1)


def times_i(x):
    s = swap(x)
    return jnp.where(low_half(x.shape), -s, s)


def dft(x_ref, t_ref, g_ref, sign, emit, chunk=32):
    for res in range(4):
        x = x_ref[pl.ds(res, QUARTER, stride=4), :]
        ix = times_i(x)
        if sign < 0:
            ix = -ix
        operand = jnp.concatenate([x.astype(BF16), ix.astype(BF16)], 0)
        g_ref[res] = jnp.dot(t_ref[res], operand, preferred_element_type=F32)

    def combine(step, carry):
        start = pl.multiple_of(step * chunk, chunk)
        rows = pl.ds(start, chunk)
        g0, g1, g2, g3 = g_ref[0, rows, :], g_ref[1, rows, :], g_ref[2, rows, :], g_ref[3, rows, :]
        h0, h1, h2 = g0 + g2, g0 - g2, g1 + g3
        h3 = times_i(g1 - g3)
        if sign < 0:
            h3 = -h3
        emit(start, h0 + h2)
        emit(QUARTER + start, h1 + h3)
        emit(2 * QUARTER + start, h0 - h2)
        emit(3 * QUARTER + start, h1 - h3)
        return carry

    lax.fori_loop(0, QUARTER // chunk, combine, 0)


def store_rows(ref, chunk=32):
    def emit(start, value):
        ref[pl.ds(pl.multiple_of(start, chunk), chunk), :] = value

    return emit


def turn_blocks(x_ref, out_ref):
    def turn(step, carry):
        base = pl.multiple_of(step * 128, 128)
        turned = x_ref[pl.ds(base, 128), :].T
        a, b = turned[:BAND], turned[BAND:]
        low = low_half(a.shape)
        out_ref[pl.ds(base, BAND), :] = jnp.where(low, a, swap(b)).astype(BF16)
        out_ref[pl.ds(pl.multiple_of(base + BAND, BAND), BAND), :] = jnp.where(low, swap(a), b).astype(BF16)
        return carry

    lax.fori_loop(0, W // 128, turn, 0)


GATHER_TILES = W // 128 + 1
GATHER_ROWS = 32


def gather_kernel(col_ref, spec_ref, out_ref, buf_ref, sem):
    col = col_ref[lax.axis_index("led")]
    tile = col // 128
    lo = col - tile * 128
    first = jnp.minimum(tile, NC // 128 - GATHER_TILES)
    skip = tile - first
    shift = lax.rem(128 - lo, 128)
    groups = 128 // GATHER_ROWS

    def fetch(group):
        rows = pl.ds(group * GATHER_ROWS, GATHER_ROWS)
        columns = pl.ds(pl.multiple_of(first * 128, 128), GATHER_TILES * 128)
        return pltpu.make_async_copy(spec_ref.at[:, rows, columns], buf_ref.at[:, rows, :], sem.at[group])

    for group in range(groups):
        fetch(group).start()

    lanes = lax.broadcasted_iota(jnp.int32, (16, 128), 1)
    keep = lanes < 128 - lo
    low = lanes < BAND
    for group in range(groups):
        fetch(group).wait()

        def step(i, carry):
            row = pl.multiple_of(group * GATHER_ROWS + i * 16, 16)

            def load(k, t):
                t = jnp.minimum(skip + t, GATHER_TILES - 1)
                x = buf_ref[k, pl.ds(row, 16), pl.ds(pl.multiple_of(t * 128, 128), 128)]
                return pltpu.roll(x, shift, 1)

            last = (load(0, 0), load(1, 0))
            for t in range(W // 128):
                nxt = (load(0, t + 1), load(1, t + 1))
                a = jnp.where(keep, last[0], nxt[0])
                b = jnp.where(keep, last[1], nxt[1])
                out_ref[pl.ds(pl.multiple_of(row + t * 256, 16), 16), :] = jnp.where(low, a, swap(b)).astype(BF16)
                out_ref[pl.ds(pl.multiple_of(row + t * 256 + 128, 16), 16), :] = jnp.where(
                    low, swap(a), b
                ).astype(BF16)
                last = nxt
            return carry

        lax.fori_loop(0, GATHER_ROWS // 16, step, 0)


def prepare_kernel(pupil_ref, intensity_ref, pr_ref, pi_ref, root_ref):
    def step(t, carry):
        rows = pl.ds(pl.multiple_of(t * 128, 128), 128)
        x = jnp.concatenate([pupil_ref[0, :, rows], pupil_ref[1, :, rows]], 0).T
        s = swap(x)
        low = low_half(x.shape)
        pr_ref[rows, :] = jnp.where(low, x, s)
        pi_ref[rows, :] = jnp.where(low, -s, x)
        v = jnp.sqrt(intensity_ref[0, :, rows])
        root_ref[rows, :] = jnp.concatenate([v, v], 0).T
        return carry

    lax.fori_loop(0, W // 128, step, 0)


def first_kernel(row_ref, recv_ref, pr_ref, pi_ref, t_ref, out_ref, win_ref, wide_ref, x_ref, g_ref):
    row = row_ref[lax.axis_index("led")]
    base = jnp.minimum(row // 16 * 16, 2 * W - (W + 16))
    off = row - base

    def widen(step, carry):
        src = pl.ds(pl.multiple_of(base + step * 48, 16), 48)
        wide_ref[pl.ds(pl.multiple_of(step * 48, 16), 48), :] = recv_ref[src, :].astype(F32)
        return carry

    lax.fori_loop(0, (W + 16) // 48, widen, 0)

    def multiply(step, carry):
        rows = pl.ds(pl.multiple_of(step * 32, 32), 32)
        w = wide_ref[pl.ds(off + step * 32, 32), :]
        product = w * pr_ref[rows, :] + swap(w) * pi_ref[rows, :]
        win_ref[rows, :] = w.astype(BF16)
        x_ref[rows, :] = product.astype(BF16).astype(F32)
        return carry

    lax.fori_loop(0, W // 32, multiply, 0)
    dft(x_ref, t_ref, g_ref, 1, store_rows(x_ref))
    turn_blocks(x_ref, out_ref)


def widen_rows(recv_ref, x_ref):
    def widen(step, carry):
        rows = pl.ds(pl.multiple_of(step * 64, 64), 64)
        x_ref[rows, :] = recv_ref[rows, :].astype(F32)
        return carry

    lax.fori_loop(0, W // 64, widen, 0)


def middle_kernel(recv_ref, root_ref, t_ref, out_ref, x_ref, g_ref):
    widen_rows(recv_ref, x_ref)

    def replace(start, value):
        squared = value * value
        magnitude = jnp.sqrt(squared + swap(squared))
        rows = pl.ds(pl.multiple_of(start, 32), 32)
        scaling = root_ref[rows, :] / jnp.maximum(magnitude, AMPLITUDE_FLOOR)
        x_ref[rows, :] = (value * scaling).astype(BF16).astype(F32)

    dft(x_ref, t_ref, g_ref, 1, replace)
    dft(x_ref, t_ref, g_ref, -1, store_rows(x_ref))
    turn_blocks(x_ref, out_ref)


def last_kernel(row_ref, recv_ref, win_ref, pr_ref, pi_ref, t_ref, grad_ref, corr_ref, x_ref, c_ref, g_ref):
    row = row_ref[lax.axis_index("led")]
    widen_rows(recv_ref, x_ref)

    def update(start, estimate):
        rows = pl.ds(pl.multiple_of(start, 32), 32)
        w = win_ref[rows, :].astype(F32)
        pr, pi = pr_ref[rows, :], pi_ref[rows, :]
        ws = swap(w)
        low = low_half(w.shape)
        change = estimate - (w * pr + ws * pi)
        cs = swap(change)
        wr = jnp.where(low, w, ws)
        wi = jnp.where(low, ws, -w)
        grad_ref[rows, :] = (change * wr + cs * wi).astype(BF16)
        c_ref[pl.ds(row + start, 32), :] = (change * pr - cs * pi) / (pr * pr + pi * pi + PUPIL_DAMPING)

    dft(x_ref, t_ref, g_ref, -1, update)

    def store(step, carry):
        start = pl.multiple_of(step * 64, 64)
        beyond = c_ref[pl.ds(pl.multiple_of(start + W, 64), 64), :]
        within = c_ref[pl.ds(start, 64), :]
        classes = start + lax.broadcasted_iota(jnp.int32, (64, 128), 0)
        dest = (step % 2) * 16 + step // 2
        corr_ref[pl.ds(pl.multiple_of(dest * 64, 64), 64), :] = jnp.where(classes < row, beyond, within).astype(BF16)
        return carry

    lax.fori_loop(0, 32, store, 0)


def reduce_kernel(row_ref, col_ref, recv_ref, own_ref, other_ref, acc_ref):
    slab, led = lax.axis_index("slab"), lax.axis_index("led")
    upper = slab // 16
    base = (slab % 16) * 128 + upper * 64 + led * 8
    acc_ref[...] = jnp.zeros_like(acc_ref)
    lanes = lax.broadcasted_iota(jnp.int32, (16, 128), 1)
    low = lax.broadcasted_iota(jnp.int32, (8, 128), 1) < BAND
    classes = base + lax.rem(lax.broadcasted_iota(jnp.int32, (16, 128), 0), 8)

    def pair(p, carry):
        for j in range(2):
            row, col = row_ref[2 * p + j], col_ref[2 * p + j]
            tile = col // 128
            lo = col - tile * 128
            take = lanes >= lo
            mine = (classes < row) == (upper == 1)

            def put(t, value):
                rows = pl.ds(pl.multiple_of((tile + t) * 16, 16), 16)
                acc_ref[0, rows, :] += jnp.where(mine, value, 0.0)
                acc_ref[1, rows, :] += jnp.where(mine, 0.0, value)

            last = jnp.zeros((16, 128), F32)
            for t in range(W // 128):
                at = pl.multiple_of(t * 128 + p * 16, 16)
                x = recv_ref[pl.ds(at, 16), :].astype(F32)[8 * j : 8 * j + 8]
                y = recv_ref[pl.ds(pl.multiple_of(at + 64, 16), 16), :].astype(F32)[8 * j : 8 * j + 8]
                both = jnp.concatenate([jnp.where(low, x, swap(y)), jnp.where(low, swap(x), y)], 0)
                both = pltpu.roll(both, lo, 1)
                put(t, jnp.where(take, both, last))
                last = both
            put(W // 128, jnp.where(take, 0.0, last))
        return carry

    lax.fori_loop(0, 4, pair, 0)

    def store(t, carry):
        rows = pl.ds(pl.multiple_of(t * 16, 16), 16)
        own_ref[rows, :] = acc_ref[0, rows, :].astype(BF16)
        other_ref[rows, :] = acc_ref[1, rows, :].astype(BF16)
        return carry

    lax.fori_loop(0, NC // 128, store, 0)


HOPS = (0, 1, -1, 2, -2, 3, -3, 4)


def finish_kernel(spec_ref, *refs):
    own, swapped, grads, (new_ref, out_ref) = refs[:8], refs[8:16], refs[16:24], refs[24:]
    slab, led = lax.axis_index("slab"), lax.axis_index("led")
    upper = slab // 16
    for hop, own_ref, swapped_ref, grad_ref in zip(HOPS, own, swapped, grads):
        source = lax.rem(led - hop + 8, 8)
        for half, ref in ((upper, own_ref), (1 - upper, swapped_ref)):
            rows = pl.ds(pl.multiple_of(half * 64 + source * 8, 8), 8)
            for t in range(NC // 128):
                x = ref[t * 16 : t * 16 + 16, :].astype(F32)
                columns = slice(t * 128, t * 128 + 128)
                new_ref[0, rows, columns] = spec_ref[0, rows, columns] + x[:8]
                new_ref[1, rows, columns] = spec_ref[1, rows, columns] + x[8:]
        for t in range(2):
            x = grad_ref[t * 128 : t * 128 + 128, :].astype(F32).T
            columns = pl.ds(pl.multiple_of(source * 256 + t * 128, 128), 128)
            out_ref[0, :, columns] = x[:BAND]
            out_ref[1, :, columns] = x[BAND:]


def call(kernel, outs, scalars, arrays, scratch=(), flops=0, limit=20 * MIB, space=VMEM):
    shapes = [jax.ShapeDtypeStruct(s, d) for s, d in outs]
    moved = sum(math.prod(s) * jnp.dtype(d).itemsize for s, d in outs)
    moved += sum(a.size * a.dtype.itemsize for a in arrays)
    return pl.pallas_call(
        kernel,
        out_shape=shapes,
        in_specs=[pl.BlockSpec(memory_space=pltpu.SMEM)] * len(scalars)
        + [pl.BlockSpec(memory_space=space)] * len(arrays),
        out_specs=[pl.BlockSpec(memory_space=VMEM)] * len(outs),
        scratch_shapes=list(scratch),
        compiler_params=pltpu.CompilerParams(vmem_limit_bytes=limit),
        cost_estimate=pl.CostEstimate(flops=flops, bytes_accessed=moved, transcendentals=0),
    )(*scalars, *arrays)


def turn_bands(values):
    blocks = values.reshape(32, -1, 128)
    return lax.all_to_all(blocks, "slab", 0, 0).reshape(-1, 128)


FORWARD = [(i, (i + 1) % 8) for i in range(8)]
BACKWARD = [(i, (i - 1) % 8) for i in range(8)]


def ring_gather(piece):
    forward = backward = piece
    found = [piece]
    for hop in range(1, 5):
        forward = lax.ppermute(forward, "led", FORWARD)
        found.append(forward)
        if hop < 4:
            backward = lax.ppermute(backward, "led", BACKWARD)
            found.append(backward)
    return found


def per_device(spectrum, pupil, intensity, row_offsets, col_offsets):
    tab = jnp.asarray(table())
    rows128 = (W, 128)
    flops = 8 * QUARTER * 1024 * 128

    (outgoing,) = call(
        gather_kernel,
        [((2 * W, 128), BF16)],
        [col_offsets],
        [spectrum],
        [VMEM((2, 128, GATHER_TILES * 128), F32), pltpu.SemaphoreType.DMA((128 // GATHER_ROWS,))],
        limit=56 * MIB,
        space=pl.ANY,
    )
    arrived = turn_bands(outgoing)
    pr, pi, root = call(prepare_kernel, [(rows128, F32)] * 3, [], [pupil, intensity])
    scratch = [VMEM(rows128, F32), VMEM((4, QUARTER, 128), F32)]
    first, window = call(
        first_kernel,
        [(rows128, BF16), (rows128, BF16)],
        [row_offsets],
        [arrived, pr, pi, tab],
        [VMEM((W + 16, 128), F32)] + scratch,
        flops,
    )
    turned = turn_bands(first)
    (second,) = call(middle_kernel, [(rows128, BF16)], [], [turned, root, tab], scratch, 2 * flops)
    returned = turn_bands(second)
    gradient, correction = call(
        last_kernel,
        [(rows128, BF16), (rows128, BF16)],
        [row_offsets],
        [returned, window, pr, pi, tab],
        [VMEM(rows128, F32), VMEM((2 * W, 128), F32), VMEM((4, QUARTER, 128), F32)],
        flops,
    )
    grad_part = lax.psum_scatter(gradient.reshape(8, W // 8, 128), "led", scatter_dimension=0)
    landed = lax.all_to_all(correction.reshape(256, 8, 128), ("slab", "led"), 0, 0).reshape(rows128)
    piece = (NC // 128 * 16, 128)
    own, other = call(
        reduce_kernel,
        [(piece, BF16), (piece, BF16)],
        [row_offsets, col_offsets],
        [landed],
        [VMEM((2, (NC // 128 + 1) * 16, 128), F32)],
    )
    swapped = lax.ppermute(other, "slab", [(i, (i + 16) % 32) for i in range(32)])
    new_spectrum, grad = call(
        finish_kernel,
        [((2, 128, NC), F32), ((2, BAND, W), F32)],
        [],
        [spectrum, *ring_gather(own), *ring_gather(swapped), *ring_gather(grad_part)],
    )
    return new_spectrum, grad


def solution(mesh):
    in_specs = (P(None, "slab", None), P(None, "slab", None), P("led", "slab", None), P(), P())
    out_specs = (P(None, "slab", None), P(None, "slab", None))
    return jax.shard_map(per_device, mesh=mesh, in_specs=in_specs, out_specs=out_specs, check_vma=False)
```

time: 211 us -> 195 us (0.924)
  blocking collectives: 51.3 us -> 30.3 us
  starting transfers between devices: 27.4 us -> 47.1 us
  waiting for transfers between devices: 75.2 us -> 58.3 us
  Pallas kernels: 27.9 us -> 37 us
  local copies, waits for them, and re-layouts: 13.2 us -> 7.86 us
    all_to_all x3 -> x2, blocking collectives: 51.3 us -> 30.3 us  [turn_bands(): return lax.all_to_all(blocks, 'slab', 0, 0).reshape(-1, 128)]
    reduce_scatter x1 -> x0, waiting for transfers between devices: 19.3 us -> none  [per_device(): lax.psum_scatter(placed.reshape(2, 8, 16, NC), 'led', scatter_dimension=1)]
    ppermute x14 -> x22, waiting for transfers between devices: 33.7 us -> 14.8 us  [the longest x12 7.61 us: ring_gather(): forward = lax.ppermute(forward, 'led', FORWARD)]
    all_to_all x0 -> x1, waiting for transfers between devices: none -> 17.5 us  [per_device(): lax.all_to_all(correction.reshape(256, 8, 128), ('slab', 'led'), 0, 0)]
    all_to_all x0 -> x1, starting transfers between devices: none -> 13 us  [per_device(): lax.all_to_all(correction.reshape(256, 8, 128), ('slab', 'led'), 0, 0)]
    pallas_call x7, Pallas kernels: 27.9 us -> 37 us  [call(): pl.pallas_call(kernel, out_shape=shapes, in_specs=[pl.BlockSpec(memory_sp...]
    ppermute x14 -> x22, starting transfers between devices: 19.7 us -> 26.4 us  [the longest x9 17.4 us: ring_gather(): backward = lax.ppermute(backward, 'led', BACKWARD)]
    reduce_scatter x1, waiting for transfers between devices: 12 us -> 15.2 us  [per_device(): lax.psum_scatter(gradient.reshape(8, W // 8, 128), 'led', scatter_dimensi...]
  transfers between devices with their start and end apart: 17 -> 25, of which waited for: 11 -> 10; matrix products, arithmetic and copies ran while one was open for 1% -> 0% of each run, Pallas kernels for 3% -> 2%
where the time goes in v2:
time: 195 us
  waiting for transfers between devices  58.3 us (30%)
  starting transfers between devices  47.1 us (24%)
  Pallas kernels  37 us (19%)
  blocking collectives  30.3 us (16%)
  between operations  14.2 us (7%)
  local copies, waits for them, and re-layouts  7.86 us (4%)
    pallas_call x7, Pallas kernels, call(): pl.pallas_call(kernel, out_shape=shapes, in_specs=[pl.BlockSpec(memory_sp...  37 us
    all_to_all x2, blocking collectives, turn_bands(): return lax.all_to_all(blocks, 'slab', 0, 0).reshape(-1, 128)  30.3 us
    all_to_all x1, waiting for transfers between devices, per_device(): lax.all_to_all(correction.reshape(256, 8, 128), ('slab', 'led'), 0, 0)  17.5 us
    ppermute x9, starting transfers between devices, ring_gather(): backward = lax.ppermute(backward, 'led', BACKWARD)  17.4 us
    reduce_scatter x1, waiting for transfers between devices, per_device(): lax.psum_scatter(gradient.reshape(8, W // 8, 128), 'led', scatter_dimensi...  15.2 us
    all_to_all x1, starting transfers between devices, per_device(): lax.all_to_all(correction.reshape(256, 8, 128), ('slab', 'led'), 0, 0)  13 us
    all_to_all x1, waiting for transfers between devices, turn_bands(): return lax.all_to_all(blocks, 'slab', 0, 0).reshape(-1, 128)  10.2 us
    unnamed x32, local copies, waits for them, and re-layouts  7.86 us
  transfers between devices with their start and end apart: 25, of which 10 were waited for; matrix products, arithmetic and copies ran while one was open for 0% of the time, Pallas kernels for 2%

profile of v2, /device:TPU:2, one launch (start us, length us, event | category | flops | bytes accessed | tf_op | source)
XLA Modules:
  0.0 194.8 jit_solution(18014199113757121362)
XLA Ops:
  7.2 4.3 %shard_map.77 = bf16[4096,128]{1,0:T(8,128)(2,1)} custom-call(s32[8]{0:T(128)} %col_ref.3, f32[2,128,3072]{2,1,0:T(8,128)} %spec_ref.3), custom_call_target="tpu_custom_call" | custom-call | bytes 4194304 | tf_op jit(solution)/shard_map/pallas_call | solution.py:313
  11.5 7.6 %all-to-all-start = ((bf16[32,128,128]{2,1,0:T(8,128)(2,1)}), bf16[32,128,128]{2,1,0:T(8,128)(2,1)S(1)}, u32[]{:S(2)}, u32[]{:S(2)}) async-start(bf16[32,128,128]{2,1,0:T(8,128)(2,1)} %bitcast.20), calls=%async_computation | async-start | bytes 2097152 | tf_op jit(solution)/shard_map/all_to_all | solution.py:327
  21.4 2.7 %shard_map.78 = (f32[2048,128]{1,0:T(8,128)S(1)}, f32[2048,128]{1,0:T(8,128)S(1)}, f32[2048,128]{1,0:T(8,128)S(1)}) custom-call(f32[2,64,2048]{2,1,0:T(8,128)S(1)} %copy-done.7, f32[1,64,2048]{2,1,0:T(8,128)S(1)} %copy-done.10), custom_call_target="tpu_custom_call" | custom-call | bytes 4718592 | tf_op jit(solution)/shard_map/pallas_call | solution.py:313
  25.1 10.2 %all-to-all-done = bf16[32,128,128]{2,1,0:T(8,128)(2,1)S(1)} async-done(((bf16[32,128,128]{2,1,0:T(8,128)(2,1)}), bf16[32,128,128]{2,1,0:T(8,128)(2,1)S(1)}, u32[]{:S(2)}, u32[]{:S(2)}) %all-to-all-start) | async-done | bytes 1048608 | tf_op jit(solution)/shard_map/all_to_all | solution.py:327
  35.3 2.2 %copy-done = bf16[4,512,1024]{2,1,0:T(8,128)(2,1)S(1)} copy-done((bf16[4,512,1024]{2,1,0:T(8,128)(2,1)S(1)}, bf16[4,512,1024]{2,1,0:T(8,128)(2,1)}, u32[]{:S(2)}) %copy-start) | copy-done | bytes 4194328
  37.4 11.0 %shard_map.79 = (bf16[2048,128]{1,0:T(8,128)(2,1)S(1)}, bf16[2048,128]{1,0:T(8,128)(2,1)S(1)}) custom-call(s32[8]{0:T(128)S(1)} %copy-done.14, bf16[4096,128]{1,0:T(8,128)(2,1)S(1)} %bitcast.10, f32[2048,128]{1,0:T(8,128)S(1)} %get-tuple-element.11.pr_ref, f32[2048,128]{1,0:T(8,128)S(1)} %get-tuple-element.12.pi_ref, bf16[4,512,1024]{2,1,0:T(8,128)(2,1)S(1)} %copy-done), custom_call_target="tpu_custom_call" | custom-call | flops 536870912 | bytes 8388608 | tf_op jit(solution)/shard_map/pallas_call | solution.py:313
  48.5 15.1 %all_to_all.20 = bf16[32,64,128]{2,1,0:T(8,128)(2,1)S(1)} all-to-all(bf16[32,64,128]{2,1,0:T(8,128)(2,1)S(1)} %bitcast.16), channel_id=1, replica_groups=mesh['slab'=32,'led'=8] {'slab'}, dimensions={0} | all-to-all | bytes 1048576 | tf_op jit(solution)/shard_map/all_to_all | solution.py:327
  63.6 9.4 %shard_map.80 = bf16[2048,128]{1,0:T(8,128)(2,1)S(1)} custom-call(bf16[2048,128]{1,0:T(8,128)(2,1)S(1)} %bitcast.11, f32[2048,128]{1,0:T(8,128)S(1)} %copy-done.9, bf16[4,512,1024]{2,1,0:T(8,128)(2,1)S(1)} %copy-done.1), custom_call_target="tpu_custom_call" | custom-call | flops 1073741824 | bytes 6291456 | tf_op jit(solution)/shard_map/pallas_call | solution.py:313
  73.0 15.2 %all_to_all.21 = bf16[32,64,128]{2,1,0:T(8,128)(2,1)S(1)} all-to-all(bf16[32,64,128]{2,1,0:T(8,128)(2,1)S(1)} %bitcast.12), channel_id=1, replica_groups=mesh['slab'=32,'led'=8] {'slab'}, dimensions={0} | all-to-all | bytes 1048576 | tf_op jit(solution)/shard_map/all_to_all | solution.py:327
  88.3 5.1 %shard_map.81 = (bf16[2048,128]{1,0:T(8,128)(2,1)S(1)}, bf16[2048,128]{1,0:T(8,128)(2,1)S(1)}) custom-call(s32[8]{0:T(128)S(1)} %copy-done.14, bf16[2048,128]{1,0:T(8,128)(2,1)S(1)} %bitcast.13, bf16[2048,128]{1,0:T(8,128)(2,1)S(1)} %get-tuple-element.15.win_ref, f32[2048,128]{1,0:T(8,128)S(1)} %copy-done.4, f32[2048,128]{1,0:T(8,128)S(1)} %copy-done.6, ...), custom_call_target="tpu_custom_call" | custom-call | flops 536870912 | bytes 8388608 | tf_op jit(solution)/shard_map/pallas_call | solution.py:313
  94.9 13.0 %all-to-all-start.3 = ((bf16[256,8,128]{2,1,0:T(8,128)(2,1)}), bf16[256,8,128]{2,1,0:T(8,128)(2,1)}, u32[]{:S(2)}, u32[]{:S(2)}) async-start(bf16[256,8,128]{2,1,0:T(8,128)(2,1)} %bitcast.15), calls=%async_computation.3 | async-start | bytes 1048576 | tf_op jit(solution)/shard_map/all_to_all | solution.py:383
  108.7 17.5 %all-to-all-done.3 = bf16[256,8,128]{2,1,0:T(8,128)(2,1)} async-done(((bf16[256,8,128]{2,1,0:T(8,128)(2,1)}), bf16[256,8,128]{2,1,0:T(8,128)(2,1)}, u32[]{:S(2)}, u32[]{:S(2)}) %all-to-all-start.3) | async-done | bytes 524320 | tf_op jit(solution)/shard_map/all_to_all | solution.py:383
  126.2 2.0 %shard_map.82 = (bf16[384,128]{1,0:T(8,128)(2,1)S(1)}, bf16[384,128]{1,0:T(8,128)(2,1)S(1)}) custom-call(s32[8]{0:T(128)S(1)} %copy-done.14, s32[8]{0:T(128)S(1)} %copy-done.15, bf16[2048,128]{1,0:T(8,128)(2,1)} %bitcast.7.recv_ref), custom_call_target="tpu_custom_call" | custom-call | bytes 720896 | tf_op jit(solution)/shard_map/pallas_call | solution.py:313
  130.6 4.8 %collective-permute-done.7.refs_8_ = bf16[384,128]{1,0:T(8,128)(2,1)S(1)} collective-permute-done((bf16[384,128]{1,0:T(8,128)(2,1)S(1)}, bf16[384,128]{1,0:T(8,128)(2,1)S(1)}, u32[]{:S(2)}, u32[]{:S(2)}) %collective-permute-start.7) | collective-permute-done | bytes 98336 | tf_op jit(solution)/shard_map/ppermute | solution.py:392
  136.0 15.2 %reduce-scatter.2.cloned.1.call-done = bf16[1,256,128]{2,1,0:T(8,128)(2,1)} async-done(((bf16[8,256,128]{2,1,0:T(8,128)(2,1)}), bf16[1,256,128]{2,1,0:T(8,128)(2,1)}) %reduce-scatter.2.cloned.1.call-update) | async-done | bytes 65552 | tf_op jit(solution)/shard_map/reduce_scatter | solution.py:382
  153.2 2.6 %collective-permute-start.1 = (bf16[384,128]{1,0:T(8,128)(2,1)S(1)}, bf16[384,128]{1,0:T(8,128)(2,1)S(1)}, u32[]{:S(2)}, u32[]{:S(2)}) collective-permute-start(bf16[384,128]{1,0:T(8,128)(2,1)S(1)} %get-tuple-element.17.refs_0_), channel_id=1, source_target_pairs={{0,7},{1,0},{2,1},{3,2},{4,3},{5,4},{6,5},{7,6},{8,15},{9,8},{10,9... | collective-permute-start | bytes 294920 | tf_op jit(solution)/shard_map/ppermute | solution.py:341
  156.4 2.4 %collective-permute-start.18 = (bf16[256,128]{1,0:T(8,128)(2,1)S(1)}, bf16[256,128]{1,0:T(8,128)(2,1)S(1)}, u32[]{:S(2)}, u32[]{:S(2)}) collective-permute-start(bf16[256,128]{1,0:T(8,128)(2,1)S(1)} %collective-permute-done.16.refs_18_), channel_id=1, source_target_pairs={{0,7},{1,0},{2,1},{3,2},{4,3},{5,4},{6,5},{7,6},{8,15},{9,8},{10,9... | collective-permute-start | bytes 196616 | tf_op jit(solution)/shard_map/ppermute | solution.py:341
  159.0 2.0 %collective-permute-start.2 = (bf16[384,128]{1,0:T(8,128)(2,1)S(1)}, bf16[384,128]{1,0:T(8,128)(2,1)S(1)}, u32[]{:S(2)}, u32[]{:S(2)}) collective-permute-start(bf16[384,128]{1,0:T(8,128)(2,1)S(1)} %collective-permute-done.refs_1_), channel_id=1, source_target_pairs={{0,1},{1,2},{2,3},{3,4},{4,5},{5,6},{6,7},{7,0},{8,9},{9,10},{10,1... | collective-permute-start | bytes 294920 | tf_op jit(solution)/shard_map/ppermute | solution.py:338
  161.5 3.0 %collective-permute-start.3 = (bf16[384,128]{1,0:T(8,128)(2,1)S(1)}, bf16[384,128]{1,0:T(8,128)(2,1)S(1)}, u32[]{:S(2)}, u32[]{:S(2)}) collective-permute-start(bf16[384,128]{1,0:T(8,128)(2,1)S(1)} %collective-permute-done.1.refs_2_), channel_id=1, source_target_pairs={{0,7},{1,0},{2,1},{3,2},{4,3},{5,4},{6,5},{7,6},{8,15},{9,8},{10,9... | collective-permute-start | bytes 294920 | tf_op jit(solution)/shard_map/ppermute | solution.py:341
  168.1 2.5 %collective-permute-start.20 = (bf16[256,128]{1,0:T(8,128)(2,1)S(1)}, bf16[256,128]{1,0:T(8,128)(2,1)S(1)}, u32[]{:S(2)}, u32[]{:S(2)}) collective-permute-start(bf16[256,128]{1,0:T(8,128)(2,1)S(1)} %collective-permute-done.18.refs_20_), channel_id=1, source_target_pairs={{0,7},{1,0},{2,1},{3,2},{4,3},{5,4},{6,5},{7,6},{8,15},{9,8},{10,9... | collective-permute-start | bytes 196616 | tf_op jit(solution)/shard_map/ppermute | solution.py:341
  172.5 3.6 %collective-permute-start.5 = (bf16[384,128]{1,0:T(8,128)(2,1)S(1)}, bf16[384,128]{1,0:T(8,128)(2,1)S(1)}, u32[]{:S(2)}, u32[]{:S(2)}) collective-permute-start(bf16[384,128]{1,0:T(8,128)(2,1)S(1)} %collective-permute-done.3.refs_4_), channel_id=1, source_target_pairs={{0,7},{1,0},{2,1},{3,2},{4,3},{5,4},{6,5},{7,6},{8,15},{9,8},{10,9... | collective-permute-start | bytes 294920 | tf_op jit(solution)/shard_map/ppermute | solution.py:341
  176.1 2.0 %collective-permute-start.6 = (bf16[384,128]{1,0:T(8,128)(2,1)S(1)}, bf16[384,128]{1,0:T(8,128)(2,1)S(1)}, u32[]{:S(2)}, u32[]{:S(2)}) collective-permute-start(bf16[384,128]{1,0:T(8,128)(2,1)S(1)} %collective-permute-done.4.refs_5_), channel_id=1, source_target_pairs={{0,1},{1,2},{2,3},{3,4},{4,5},{5,6},{6,7},{7,0},{8,9},{9,10},{10,1... | collective-permute-start | bytes 294920 | tf_op jit(solution)/shard_map/ppermute | solution.py:338
  178.9 5.8 %collective-permute-done.21.refs_23_ = bf16[256,128]{1,0:T(8,128)(2,1)S(1)} collective-permute-done((bf16[256,128]{1,0:T(8,128)(2,1)S(1)}, bf16[256,128]{1,0:T(8,128)(2,1)S(1)}, u32[]{:S(2)}, u32[]{:S(2)}) %collective-permute-start.21) | collective-permute-done | bytes 65568 | tf_op jit(solution)/shard_map/ppermute | solution.py:338
  185.5 2.4 %shard_map.83 = (f32[2,128,3072]{2,1,0:T(8,128)}, f32[2,64,2048]{2,1,0:T(8,128)}) custom-call(f32[2,128,3072]{2,1,0:T(8,128)S(1)} %copy-done.2, bf16[384,128]{1,0:T(8,128)(2,1)S(1)} %get-tuple-element.17.refs_0_, bf16[384,128]{1,0:T(8,128)(2,1)S(1)} %collective-permute-done.refs_1_, bf16[384,128]{1,0:T(8,128)(2,1)S(1)} %collective-permute-done.1.refs_2_, ...), custom_call_target="tpu_custom_call" | custom-call | bytes 9437184 | tf_op jit(solution)/shard_map/pallas_call | solution.py:313
  (68 shorter events, 19.0 us)
Async XLA Ops:
  11.5 23.8 %all-to-all-start = ((bf16[32,128,128]{2,1,0:T(8,128)(2,1)}), bf16[32,128,128]{2,1,0:T(8,128)(2,1)S(1)}, u32[]{:S(2)}, u32[]{:S(2)}) async-start(bf16[32,128,128]{2,1,0:T(8,128)(2,1)} %bitcast.20), calls=%async_computation | async-start | bytes 2097152 | tf_op jit(solution)/shard_map/all_to_all | solution.py:327
  94.9 31.2 %all-to-all-start.3 = ((bf16[256,8,128]{2,1,0:T(8,128)(2,1)}), bf16[256,8,128]{2,1,0:T(8,128)(2,1)}, u32[]{:S(2)}, u32[]{:S(2)}) async-start(bf16[256,8,128]{2,1,0:T(8,128)(2,1)} %bitcast.15), calls=%async_computation.3 | async-start | bytes 1048576 | tf_op jit(solution)/shard_map/all_to_all | solution.py:383
  107.9 43.3 %reduce-scatter.2.cloned.1.call-start = ((), (), s32[]{:S(2)}) async-start(), calls=%async_computation.5 | async-start | bytes 589824 | tf_op jit(solution)/shard_map/reduce_scatter | solution.py:382
  128.2 7.1 %collective-permute-start.7 = (bf16[384,128]{1,0:T(8,128)(2,1)S(1)}, bf16[384,128]{1,0:T(8,128)(2,1)S(1)}, u32[]{:S(2)}, u32[]{:S(2)}) collective-permute-start(bf16[384,128]{1,0:T(8,128)(2,1)S(1)} %get-tuple-element.18), channel_id=1, source_target_pairs={{0,128},{8,136},{16,144},{24,152},{32,160},{40,168},{48,176},{56,1... | collective-permute-start | bytes 294920 | tf_op jit(solution)/shard_map/ppermute | solution.py:392
  129.6 29.4 %collective-permute-start = (bf16[384,128]{1,0:T(8,128)(2,1)S(1)}, bf16[384,128]{1,0:T(8,128)(2,1)S(1)}, u32[]{:S(2)}, u32[]{:S(2)}) collective-permute-start(bf16[384,128]{1,0:T(8,128)(2,1)S(1)} %get-tuple-element.17.refs_0_), channel_id=1, source_target_pairs={{0,1},{1,2},{2,3},{3,4},{4,5},{5,6},{6,7},{7,0},{8,9},{9,10},{10,1... | collective-permute-start | bytes 294920 | tf_op jit(solution)/shard_map/ppermute | solution.py:338
  135.4 25.7 %collective-permute-start.8 = (bf16[384,128]{1,0:T(8,128)(2,1)S(1)}, bf16[384,128]{1,0:T(8,128)(2,1)S(1)}, u32[]{:S(2)}, u32[]{:S(2)}) collective-permute-start(bf16[384,128]{1,0:T(8,128)(2,1)S(1)} %collective-permute-done.7.refs_8_), channel_id=1, source_target_pairs={{0,1},{1,2},{2,3},{3,4},{4,5},{5,6},{6,7},{7,0},{8,9},{9,10},{10,1... | collective-permute-start | bytes 294920 | tf_op jit(solution)/shard_map/ppermute | solution.py:338
  151.2 5.2 %collective-permute-start.16 = (bf16[256,128]{1,0:T(8,128)(2,1)}, bf16[256,128]{1,0:T(8,128)(2,1)S(1)}, u32[]{:S(2)}, u32[]{:S(2)}) collective-permute-start(bf16[256,128]{1,0:T(8,128)(2,1)} %bitcast.17), channel_id=1, source_target_pairs={{0,7},{1,0},{2,1},{3,2},{4,3},{5,4},{6,5},{7,6},{8,15},{9,8},{10,9... | collective-permute-start | bytes 196616 | tf_op jit(solution)/shard_map/ppermute | solution.py:341
  152.6 6.4 %collective-permute-start.15 = (bf16[256,128]{1,0:T(8,128)(2,1)}, bf16[256,128]{1,0:T(8,128)(2,1)S(1)}, u32[]{:S(2)}, u32[]{:S(2)}) collective-permute-start(bf16[256,128]{1,0:T(8,128)(2,1)} %bitcast.18), channel_id=1, source_target_pairs={{0,1},{1,2},{2,3},{3,4},{4,5},{5,6},{6,7},{7,0},{8,9},{9,10},{10,1... | collective-permute-start | bytes 196616 | tf_op jit(solution)/shard_map/ppermute | solution.py:338
  153.2 7.9 %collective-permute-start.1 = (bf16[384,128]{1,0:T(8,128)(2,1)S(1)}, bf16[384,128]{1,0:T(8,128)(2,1)S(1)}, u32[]{:S(2)}, u32[]{:S(2)}) collective-permute-start(bf16[384,128]{1,0:T(8,128)(2,1)S(1)} %get-tuple-element.17.refs_0_), channel_id=1, source_target_pairs={{0,7},{1,0},{2,1},{3,2},{4,3},{5,4},{6,5},{7,6},{8,15},{9,8},{10,9... | collective-permute-start | bytes 294920 | tf_op jit(solution)/shard_map/ppermute | solution.py:341
  156.4 5.1 %collective-permute-start.18 = (bf16[256,128]{1,0:T(8,128)(2,1)S(1)}, bf16[256,128]{1,0:T(8,128)(2,1)S(1)}, u32[]{:S(2)}, u32[]{:S(2)}) collective-permute-start(bf16[256,128]{1,0:T(8,128)(2,1)S(1)} %collective-permute-done.16.refs_18_), channel_id=1, source_target_pairs={{0,7},{1,0},{2,1},{3,2},{4,3},{5,4},{6,5},{7,6},{8,15},{9,8},{10,9... | collective-permute-start | bytes 196616 | tf_op jit(solution)/shard_map/ppermute | solution.py:341
  159.0 5.5 %collective-permute-start.9 = (bf16[384,128]{1,0:T(8,128)(2,1)S(1)}, bf16[384,128]{1,0:T(8,128)(2,1)S(1)}, u32[]{:S(2)}, u32[]{:S(2)}) collective-permute-start(bf16[384,128]{1,0:T(8,128)(2,1)S(1)} %collective-permute-done.7.refs_8_), channel_id=1, source_target_pairs={{0,7},{1,0},{2,1},{3,2},{4,3},{5,4},{6,5},{7,6},{8,15},{9,8},{10,9... | collective-permute-start | bytes 294920 | tf_op jit(solution)/shard_map/ppermute | solution.py:341
  159.0 7.3 %collective-permute-start.2 = (bf16[384,128]{1,0:T(8,128)(2,1)S(1)}, bf16[384,128]{1,0:T(8,128)(2,1)S(1)}, u32[]{:S(2)}, u32[]{:S(2)}) collective-permute-start(bf16[384,128]{1,0:T(8,128)(2,1)S(1)} %collective-permute-done.refs_1_), channel_id=1, source_target_pairs={{0,1},{1,2},{2,3},{3,4},{4,5},{5,6},{6,7},{7,0},{8,9},{9,10},{10,1... | collective-permute-start | bytes 294920 | tf_op jit(solution)/shard_map/ppermute | solution.py:338
  161.1 6.3 %collective-permute-start.10 = (bf16[384,128]{1,0:T(8,128)(2,1)S(1)}, bf16[384,128]{1,0:T(8,128)(2,1)S(1)}, u32[]{:S(2)}, u32[]{:S(2)}) collective-permute-start(bf16[384,128]{1,0:T(8,128)(2,1)S(1)} %collective-permute-done.8.refs_9_), channel_id=1, source_target_pairs={{0,1},{1,2},{2,3},{3,4},{4,5},{5,6},{6,7},{7,0},{8,9},{9,10},{10,1... | collective-permute-start | bytes 294920 | tf_op jit(solution)/shard_map/ppermute | solution.py:338
  161.1 6.9 %collective-permute-start.17 = (bf16[256,128]{1,0:T(8,128)(2,1)S(1)}, bf16[256,128]{1,0:T(8,128)(2,1)S(1)}, u32[]{:S(2)}, u32[]{:S(2)}) collective-permute-start(bf16[256,128]{1,0:T(8,128)(2,1)S(1)} %collective-permute-done.15.refs_17_), channel_id=1, source_target_pairs={{0,1},{1,2},{2,3},{3,4},{4,5},{5,6},{6,7},{7,0},{8,9},{9,10},{10,1... | collective-permute-start | bytes 196616 | tf_op jit(solution)/shard_map/ppermute | solution.py:338
  161.5 9.1 %collective-permute-start.3 = (bf16[384,128]{1,0:T(8,128)(2,1)S(1)}, bf16[384,128]{1,0:T(8,128)(2,1)S(1)}, u32[]{:S(2)}, u32[]{:S(2)}) collective-permute-start(bf16[384,128]{1,0:T(8,128)(2,1)S(1)} %collective-permute-done.1.refs_2_), channel_id=1, source_target_pairs={{0,7},{1,0},{2,1},{3,2},{4,3},{5,4},{6,5},{7,6},{8,15},{9,8},{10,9... | collective-permute-start | bytes 294920 | tf_op jit(solution)/shard_map/ppermute | solution.py:341
  164.5 11.6 %collective-permute-start.11 = (bf16[384,128]{1,0:T(8,128)(2,1)S(1)}, bf16[384,128]{1,0:T(8,128)(2,1)S(1)}, u32[]{:S(2)}, u32[]{:S(2)}) collective-permute-start(bf16[384,128]{1,0:T(8,128)(2,1)S(1)} %collective-permute-done.9.refs_10_), channel_id=1, source_target_pairs={{0,7},{1,0},{2,1},{3,2},{4,3},{5,4},{6,5},{7,6},{8,15},{9,8},{10,9... | collective-permute-start | bytes 294920 | tf_op jit(solution)/shard_map/ppermute | solution.py:341
  166.3 9.8 %collective-permute-start.4 = (bf16[384,128]{1,0:T(8,128)(2,1)S(1)}, bf16[384,128]{1,0:T(8,128)(2,1)S(1)}, u32[]{:S(2)}, u32[]{:S(2)}) collective-permute-start(bf16[384,128]{1,0:T(8,128)(2,1)S(1)} %collective-permute-done.2.refs_3_), channel_id=1, source_target_pairs={{0,1},{1,2},{2,3},{3,4},{4,5},{5,6},{6,7},{7,0},{8,9},{9,10},{10,1... | collective-permute-start | bytes 294920 | tf_op jit(solution)/shard_map/ppermute | solution.py:338
  167.4 10.8 %collective-permute-start.12 = (bf16[384,128]{1,0:T(8,128)(2,1)S(1)}, bf16[384,128]{1,0:T(8,128)(2,1)S(1)}, u32[]{:S(2)}, u32[]{:S(2)}) collective-permute-start(bf16[384,128]{1,0:T(8,128)(2,1)S(1)} %collective-permute-done.10.refs_11_), channel_id=1, source_target_pairs={{0,1},{1,2},{2,3},{3,4},{4,5},{5,6},{6,7},{7,0},{8,9},{9,10},{10,1... | collective-permute-start | bytes 294920 | tf_op jit(solution)/shard_map/ppermute | solution.py:338
  170.6 7.6 %collective-permute-start.19 = (bf16[256,128]{1,0:T(8,128)(2,1)S(1)}, bf16[256,128]{1,0:T(8,128)(2,1)S(1)}, u32[]{:S(2)}, u32[]{:S(2)}) collective-permute-start(bf16[256,128]{1,0:T(8,128)(2,1)S(1)} %collective-permute-done.17.refs_19_), channel_id=1, source_target_pairs={{0,1},{1,2},{2,3},{3,4},{4,5},{5,6},{6,7},{7,0},{8,9},{9,10},{10,1... | collective-permute-start | bytes 196616 | tf_op jit(solution)/shard_map/ppermute | solution.py:338
  172.5 12.1 %collective-permute-start.5 = (bf16[384,128]{1,0:T(8,128)(2,1)S(1)}, bf16[384,128]{1,0:T(8,128)(2,1)S(1)}, u32[]{:S(2)}, u32[]{:S(2)}) collective-permute-start(bf16[384,128]{1,0:T(8,128)(2,1)S(1)} %collective-permute-done.3.refs_4_), channel_id=1, source_target_pairs={{0,7},{1,0},{2,1},{3,2},{4,3},{5,4},{6,5},{7,6},{8,15},{9,8},{10,9... | collective-permute-start | bytes 294920 | tf_op jit(solution)/shard_map/ppermute | solution.py:341
  176.1 8.6 %collective-permute-start.13 = (bf16[384,128]{1,0:T(8,128)(2,1)S(1)}, bf16[384,128]{1,0:T(8,128)(2,1)S(1)}, u32[]{:S(2)}, u32[]{:S(2)}) collective-permute-start(bf16[384,128]{1,0:T(8,128)(2,1)S(1)} %collective-permute-done.11.refs_12_), channel_id=1, source_target_pairs={{0,7},{1,0},{2,1},{3,2},{4,3},{5,4},{6,5},{7,6},{8,15},{9,8},{10,9... | collective-permute-start | bytes 294920 | tf_op jit(solution)/shard_map/ppermute | solution.py:341
  176.1 8.5 %collective-permute-start.6 = (bf16[384,128]{1,0:T(8,128)(2,1)S(1)}, bf16[384,128]{1,0:T(8,128)(2,1)S(1)}, u32[]{:S(2)}, u32[]{:S(2)}) collective-permute-start(bf16[384,128]{1,0:T(8,128)(2,1)S(1)} %collective-permute-done.4.refs_5_), channel_id=1, source_target_pairs={{0,1},{1,2},{2,3},{3,4},{4,5},{5,6},{6,7},{7,0},{8,9},{9,10},{10,1... | collective-permute-start | bytes 294920 | tf_op jit(solution)/shard_map/ppermute | solution.py:338
  178.1 6.5 %collective-permute-start.14 = (bf16[384,128]{1,0:T(8,128)(2,1)S(1)}, bf16[384,128]{1,0:T(8,128)(2,1)S(1)}, u32[]{:S(2)}, u32[]{:S(2)}) collective-permute-start(bf16[384,128]{1,0:T(8,128)(2,1)S(1)} %collective-permute-done.12.refs_13_), channel_id=1, source_target_pairs={{0,1},{1,2},{2,3},{3,4},{4,5},{5,6},{6,7},{7,0},{8,9},{9,10},{10,1... | collective-permute-start | bytes 294920 | tf_op jit(solution)/shard_map/ppermute | solution.py:338
  178.2 6.4 %collective-permute-start.21 = (bf16[256,128]{1,0:T(8,128)(2,1)S(1)}, bf16[256,128]{1,0:T(8,128)(2,1)S(1)}, u32[]{:S(2)}, u32[]{:S(2)}) collective-permute-start(bf16[256,128]{1,0:T(8,128)(2,1)S(1)} %collective-permute-done.19.refs_21_), channel_id=1, source_target_pairs={{0,1},{1,2},{2,3},{3,4},{4,5},{5,6},{6,7},{7,0},{8,9},{9,10},{10,1... | collective-permute-start | bytes 196616 | tf_op jit(solution)/shard_map/ppermute | solution.py:338
  (17 other events, 323.2 us)
Sparse Core Ops, SparseCore 0:
  111.9 39.2 reduce-scatter.1

commit v3 on v2

v3 whole, which is shorter than its diff:
```python
import functools
import math

import jax
import jax.numpy as jnp
import numpy as np
from jax import lax
from jax.experimental import pallas as pl
from jax.experimental.pallas import tpu as pltpu
from jax.sharding import PartitionSpec as P

W = 2048
QUARTER = W // 4
BAND = 64
NC = 3072
AMPLITUDE_FLOOR = 0.5
PUPIL_DAMPING = 0.5
MIB = 1024 * 1024

VMEM = pltpu.VMEM
F32 = jnp.float32
BF16 = jnp.bfloat16


def table():
    rows = np.arange(QUARTER, dtype=np.int64)[:, None]
    cols = np.arange(W, dtype=np.int64)[None, :]
    phases = ((rows * cols) % W).astype(np.float32) * np.float32(2.0 * math.pi / W)
    factor = np.float32(1.0 / math.sqrt(W))
    parts = []
    for res in range(4):
        part = phases[:, res::4]
        parts.append(np.concatenate([np.cos(part) * factor, np.sin(part) * factor], 1))
    return np.stack(parts).astype(jnp.bfloat16)


def low_half(shape):
    return lax.broadcasted_iota(jnp.int32, shape, 1) < BAND


def swap(x):
    return pltpu.roll(x, BAND, 1)


def times_i(x):
    s = swap(x)
    return jnp.where(low_half(x.shape), -s, s)


def dft(x_ref, t_ref, g_ref, sign, emit, chunk=64):
    for res in range(4):
        x = x_ref[pl.ds(res, QUARTER, stride=4), :]
        ix = times_i(x)
        if sign < 0:
            ix = -ix
        operand = jnp.concatenate([x.astype(BF16), ix.astype(BF16)], 0)
        g_ref[res] = jnp.dot(t_ref[res], operand, preferred_element_type=F32)

    for start in range(0, QUARTER, chunk):
        g0, g1, g2, g3 = (g_ref[res, start : start + chunk, :] for res in range(4))
        h0, h1, h2 = g0 + g2, g0 - g2, g1 + g3
        h3 = times_i(g1 - g3)
        if sign < 0:
            h3 = -h3
        emit(start, h0 + h2)
        emit(QUARTER + start, h1 + h3)
        emit(2 * QUARTER + start, h0 - h2)
        emit(3 * QUARTER + start, h1 - h3)


def store_rows(ref):
    def emit(start, value):
        ref[start : start + value.shape[0], :] = value

    return emit


def turn_blocks(x_ref, out_ref):
    for base in range(0, W, 128):
        turned = x_ref[base : base + 128, :].T
        a, b = turned[:BAND], turned[BAND:]
        low = low_half(a.shape)
        out_ref[base : base + BAND, :] = jnp.where(low, a, swap(b)).astype(BF16)
        out_ref[base + BAND : base + 128, :] = jnp.where(low, swap(a), b).astype(BF16)


def gather_kernel(col_ref, spec_ref, out_ref, x_ref):
    col = col_ref[lax.axis_index("led")]
    tile = col // 128
    lo = col - tile * 128
    for t in range(W // 128 + 1):
        source = jnp.minimum(tile + t, NC // 128 - 1)
        x_ref[:, :, t * 128 : t * 128 + 128] = spec_ref[:, :, pl.ds(pl.multiple_of(source * 128, 128), 128)].astype(BF16)
    source = lax.broadcasted_iota(jnp.int32, (512, 256), 0)
    target = lax.broadcasted_iota(jnp.int32, (512, 256), 1)
    moves = (source % 256 == lo + target // 128 * 64 + target % 64) & (source // 256 == target % 128 // 64)
    moves = moves.astype(F32).astype(BF16)
    for t in range(W // 128):
        columns = slice(t * 128, t * 128 + 256)
        both = jnp.concatenate([x_ref[0, :, columns], x_ref[1, :, columns]], 1)
        moved = jnp.dot(both, moves, preferred_element_type=F32)
        out_ref[t * 256 : t * 256 + 128, :] = moved[:, :128].astype(BF16)
        out_ref[t * 256 + 128 : t * 256 + 256, :] = moved[:, 128:].astype(BF16)


def first_kernel(row_ref, recv_ref, pupil_ref, t_ref, out_ref, win_ref, pr_ref, pi_ref, wide_ref, x_ref, g_ref):
    row = row_ref[lax.axis_index("led")]
    base = jnp.minimum(row // 16 * 16, 2 * W - (W + 16))
    off = row - base
    wide_ref[...] = recv_ref[pl.ds(pl.multiple_of(base, 16), W + 16), :].astype(F32)
    for start in range(0, W, 128):
        rows = slice(start, start + 128)
        x = jnp.concatenate([pupil_ref[0, :, rows], pupil_ref[1, :, rows]], 0).T
        s = swap(x)
        low = low_half(x.shape)
        pr, pi = jnp.where(low, x, s), jnp.where(low, -s, x)
        pr_ref[rows, :] = pr
        pi_ref[rows, :] = pi
        w = wide_ref[pl.ds(off + start, 128), :]
        win_ref[rows, :] = w.astype(BF16)
        x_ref[rows, :] = (w * pr + swap(w) * pi).astype(BF16).astype(F32)
    dft(x_ref, t_ref, g_ref, 1, store_rows(x_ref))
    turn_blocks(x_ref, out_ref)


def middle_kernel(recv_ref, intensity_ref, t_ref, out_ref, root_ref, x_ref, g_ref):
    x_ref[...] = recv_ref[...].astype(F32)
    for start in range(0, W, 128):
        rows = slice(start, start + 128)
        root = jnp.sqrt(intensity_ref[0, :, rows])
        root_ref[rows, :] = jnp.concatenate([root, root], 0).T

    def replace(start, value):
        squared = value * value
        magnitude = jnp.sqrt(squared + swap(squared))
        rows = slice(start, start + value.shape[0])
        scaling = root_ref[rows, :] / jnp.maximum(magnitude, AMPLITUDE_FLOOR)
        x_ref[rows, :] = (value * scaling).astype(BF16).astype(F32)

    dft(x_ref, t_ref, g_ref, 1, replace)
    dft(x_ref, t_ref, g_ref, -1, store_rows(x_ref))
    turn_blocks(x_ref, out_ref)


def last_kernel(row_ref, recv_ref, win_ref, pr_ref, pi_ref, t_ref, grad_ref, corr_ref, x_ref, c_ref, g_ref):
    row = row_ref[lax.axis_index("led")]
    x_ref[...] = recv_ref[...].astype(F32)

    def update(start, estimate):
        size = estimate.shape[0]
        rows = slice(start, start + size)
        w = win_ref[rows, :].astype(F32)
        pr, pi = pr_ref[rows, :], pi_ref[rows, :]
        ws = swap(w)
        low = low_half(w.shape)
        change = estimate - (w * pr + ws * pi)
        cs = swap(change)
        wr = jnp.where(low, w, ws)
        wi = jnp.where(low, ws, -w)
        grad_ref[rows, :] = change * wr + cs * wi
        c_ref[pl.ds(row + start, size), :] = (change * pr - cs * pi) / (pr * pr + pi * pi + PUPIL_DAMPING)

    dft(x_ref, t_ref, g_ref, -1, update)

    for part in range(32):
        start = part * 64
        classes = start + lax.broadcasted_iota(jnp.int32, (64, 128), 0)
        value = jnp.where(classes < row, c_ref[start + W : start + W + 64, :], c_ref[start : start + 64, :])
        dest = (part % 2) * 16 + part // 2
        corr_ref[dest * 64 : dest * 64 + 64, :] = value.astype(BF16)


def reduce_kernel(row_ref, col_ref, recv_ref, own_ref, other_ref, acc_ref):
    slab, led = lax.axis_index("slab"), lax.axis_index("led")
    upper = slab // 16
    base = (slab % 16) * 128 + upper * 64 + led * 8
    acc_ref[...] = jnp.zeros_like(acc_ref)
    lanes = lax.broadcasted_iota(jnp.int32, (16, 128), 1)
    low = lax.broadcasted_iota(jnp.int32, (8, 128), 1) < BAND
    classes = base + lax.rem(lax.broadcasted_iota(jnp.int32, (16, 128), 0), 8)

    def pair(p, carry):
        for j in range(2):
            row, col = row_ref[2 * p + j], col_ref[2 * p + j]
            tile = col // 128
            lo = col - tile * 128
            take = lanes >= lo
            mine = (classes < row) == (upper == 1)

            def put(t, value):
                rows = pl.ds(pl.multiple_of((tile + t) * 16, 16), 16)
                acc_ref[0, rows, :] += jnp.where(mine, value, 0.0)
                acc_ref[1, rows, :] += jnp.where(mine, 0.0, value)

            last = jnp.zeros((16, 128), F32)
            for t in range(W // 128):
                at = pl.multiple_of(t * 128 + p * 16, 16)
                x = recv_ref[pl.ds(at, 16), :].astype(F32)[8 * j : 8 * j + 8]
                y = recv_ref[pl.ds(pl.multiple_of(at + 64, 16), 16), :].astype(F32)[8 * j : 8 * j + 8]
                both = jnp.concatenate([jnp.where(low, x, swap(y)), jnp.where(low, swap(x), y)], 0)
                both = pltpu.roll(both, lo, 1)
                put(t, jnp.where(take, both, last))
                last = both
            put(W // 128, jnp.where(take, 0.0, last))
        return carry

    lax.fori_loop(0, 4, pair, 0)
    own_ref[...] = acc_ref[0, : NC // 8, :].astype(BF16)
    other_ref[...] = acc_ref[1, : NC // 8, :].astype(BF16)


def merge_kernel(swapped_ref, grad_ref, after_ref, out_ref):
    out_ref[: NC // 8, :] = swapped_ref[...]
    out_ref[NC // 8 :, :] = grad_ref[...].astype(BF16)


HOPS = (0, 1, -1, 2, -2, 3, -3, 4)


def finish_kernel(spec_ref, *refs):
    own, rest, (new_ref, out_ref) = refs[:8], refs[8:16], refs[16:]
    slab, led = lax.axis_index("slab"), lax.axis_index("led")
    upper = slab // 16
    for hop, own_ref, rest_ref in zip(HOPS, own, rest):
        source = lax.rem(led - hop + 8, 8)
        for half, ref in ((upper, own_ref), (1 - upper, rest_ref)):
            rows = pl.ds(pl.multiple_of(half * 64 + source * 8, 8), 8)
            for t in range(NC // 128):
                x = ref[t * 16 : t * 16 + 16, :].astype(F32)
                columns = slice(t * 128, t * 128 + 128)
                new_ref[0, rows, columns] = spec_ref[0, rows, columns] + x[:8]
                new_ref[1, rows, columns] = spec_ref[1, rows, columns] + x[8:]
        for t in range(2):
            start = NC // 8 + t * 128
            x = rest_ref[start : start + 128, :].astype(F32).T
            columns = pl.ds(pl.multiple_of(source * 256 + t * 128, 128), 128)
            out_ref[0, :, columns] = x[:BAND]
            out_ref[1, :, columns] = x[BAND:]


def call(kernel, outs, scalars, arrays, scratch=(), flops=0, limit=20 * MIB):
    shapes = [jax.ShapeDtypeStruct(s, d) for s, d in outs]
    moved = sum(math.prod(s) * jnp.dtype(d).itemsize for s, d in outs)
    moved += sum(a.size * a.dtype.itemsize for a in arrays)
    return pl.pallas_call(
        kernel,
        out_shape=shapes,
        in_specs=[pl.BlockSpec(memory_space=pltpu.SMEM)] * len(scalars)
        + [pl.BlockSpec(memory_space=VMEM)] * len(arrays),
        out_specs=[pl.BlockSpec(memory_space=VMEM)] * len(outs),
        scratch_shapes=list(scratch),
        compiler_params=pltpu.CompilerParams(vmem_limit_bytes=limit),
        cost_estimate=pl.CostEstimate(flops=flops, bytes_accessed=moved, transcendentals=0),
    )(*scalars, *arrays)


def turn_bands(values):
    blocks = values.reshape(32, -1, 128)
    return lax.all_to_all(blocks, "slab", 0, 0).reshape(-1, 128)


FORWARD = [(i, (i + 1) % 8) for i in range(8)]
BACKWARD = [(i, (i - 1) % 8) for i in range(8)]


def ring_gather(piece):
    forward = backward = piece
    found = [piece]
    for hop in range(1, 5):
        forward = lax.ppermute(forward, "led", FORWARD)
        found.append(forward)
        if hop < 4:
            backward = lax.ppermute(backward, "led", BACKWARD)
            found.append(backward)
    return found


def per_device(spectrum, pupil, intensity, row_offsets, col_offsets):
    tab = jnp.asarray(table())
    rows128 = (W, 128)
    flops = 8 * QUARTER * 1024 * 128

    (outgoing,) = call(
        gather_kernel, [((2 * W, 128), BF16)], [col_offsets], [spectrum], [VMEM((2, 128, W + 128), BF16)]
    )
    arrived = turn_bands(outgoing)
    scratch = [VMEM(rows128, F32), VMEM((4, QUARTER, 128), F32)]
    first, window, pr, pi = call(
        first_kernel,
        [(rows128, BF16), (rows128, BF16), (rows128, F32), (rows128, F32)],
        [row_offsets],
        [arrived, pupil, tab],
        [VMEM((W + 16, 128), F32)] + scratch,
        flops,
    )
    turned = turn_bands(first)
    (second,) = call(
        middle_kernel, [(rows128, BF16)], [], [turned, intensity, tab], [VMEM(rows128, F32)] + scratch, 2 * flops
    )
    returned = turn_bands(second)
    gradient, correction = call(
        last_kernel,
        [(rows128, F32), (rows128, BF16)],
        [row_offsets],
        [returned, window, pr, pi, tab],
        [VMEM(rows128, F32), VMEM((2 * W, 128), F32), VMEM((4, QUARTER, 128), F32)],
        flops,
    )
    grad_part = lax.psum_scatter(gradient.reshape(8, W // 8, 128), "led", scatter_dimension=0)
    landed = lax.all_to_all(correction.reshape(256, 8, 128), ("slab", "led"), 0, 0).reshape(rows128)
    piece = (NC // 128 * 16, 128)
    own, other = call(
        reduce_kernel,
        [(piece, BF16), (piece, BF16)],
        [row_offsets, col_offsets],
        [landed],
        [VMEM((2, (NC // 128 + 1) * 16, 128), F32)],
    )
    swapped = lax.ppermute(other, "slab", [(i, (i + 16) % 32) for i in range(32)])
    own_pieces = ring_gather(own)
    (rest,) = call(
        merge_kernel, [((piece[0] + W // 8, 128), BF16)], [], [swapped, grad_part.reshape(W // 8, 128), own_pieces[1]]
    )
    new_spectrum, grad = call(
        finish_kernel,
        [((2, 128, NC), F32), ((2, BAND, W), F32)],
        [],
        [spectrum, *own_pieces, *ring_gather(rest)],
    )
    return new_spectrum, grad


def solution(mesh):
    in_specs = (P(None, "slab", None), P(None, "slab", None), P("led", "slab", None), P(), P())
    out_specs = (P(None, "slab", None), P(None, "slab", None))
    return jax.shard_map(per_device, mesh=mesh, in_specs=in_specs, out_specs=out_specs, check_vma=False)
```

time: 195 us -> 170 us (0.87)
  blocking collectives: 30.3 us -> 90.5 us
  waiting for transfers between devices: 58.3 us -> 21 us
  starting transfers between devices: 47.1 us -> 21.5 us
  Pallas kernels: 37 us -> 16.2 us
  local copies, waits for them, and re-layouts: 7.86 us -> 5.22 us
    all_to_all x0 -> x1, blocking collectives: none -> 36.5 us  [per_device(): lax.all_to_all(correction.reshape(256, 8, 128), ('slab', 'led'), 0, 0)]
    all_to_all x2 -> x0, waiting for transfers between devices: 27.7 us -> none  [the longest x1 17.5 us: per_device(): lax.all_to_all(correction.reshape(256, 8, 128), ('slab', 'led'), 0, 0)]
    all_to_all x2 -> x3, blocking collectives: 30.3 us -> 54 us  [turn_bands(): return lax.all_to_all(blocks, 'slab', 0, 0).reshape(-1, 128)]
    pallas_call x7, Pallas kernels: 37 us -> 16.2 us  [call(): pl.pallas_call(kernel, out_shape=shapes, in_specs=[pl.BlockSpec(memory_sp...]
    all_to_all x2 -> x0, starting transfers between devices: 20.6 us -> none  [the longest x1 13 us: per_device(): lax.all_to_all(correction.reshape(256, 8, 128), ('slab', 'led'), 0, 0)]
    reduce_scatter x1, waiting for transfers between devices: 15.2 us -> 0.01 us  [per_device(): lax.psum_scatter(gradient.reshape(8, W // 8, 128), 'led', scatter_dimensi...]
    ppermute x12 -> x8, starting transfers between devices: 7.65 us -> 1.97 us  [ring_gather(): forward = lax.ppermute(forward, 'led', FORWARD)]
    ppermute x12 -> x8, waiting for transfers between devices: 7.61 us -> 11.3 us  [ring_gather(): forward = lax.ppermute(forward, 'led', FORWARD)]
  transfers between devices with their start and end apart: 25 -> 16, of which waited for: 10 -> 8; matrix products, arithmetic and copies ran while one was open for 0% -> 0% of each run, Pallas kernels for 2% -> 1%
where the time goes in v3:
time: 170 us; the launch traced here: 169 us
  blocking collectives  90.5 us (53%)
  starting transfers between devices  21.5 us (13%)
  waiting for transfers between devices  21 us (12%)
  Pallas kernels  16.2 us (10%)
  between operations  14.1 us (8%)
  local copies, waits for them, and re-layouts  5.22 us (3%)
    all_to_all x3, blocking collectives, turn_bands(): return lax.all_to_all(blocks, 'slab', 0, 0).reshape(-1, 128)  54 us
    all_to_all x1, blocking collectives, per_device(): lax.all_to_all(correction.reshape(256, 8, 128), ('slab', 'led'), 0, 0)  36.5 us
    ppermute x6, starting transfers between devices, ring_gather(): backward = lax.ppermute(backward, 'led', BACKWARD)  18.9 us
    pallas_call x7, Pallas kernels, call(): pl.pallas_call(kernel, out_shape=shapes, in_specs=[pl.BlockSpec(memory_sp...  16.2 us
    ppermute x8, waiting for transfers between devices, ring_gather(): forward = lax.ppermute(forward, 'led', FORWARD)  11.3 us
    unnamed x20, local copies, waits for them, and re-layouts  5.22 us
    ppermute x1, waiting for transfers between devices, per_device(): lax.ppermute(other, 'slab', [(i, (i + 16) % 32) for i in range(32)])  5.02 us
    ppermute x6, waiting for transfers between devices, ring_gather(): backward = lax.ppermute(backward, 'led', BACKWARD)  4.68 us
  transfers between devices with their start and end apart: 16, of which 8 were waited for; matrix products, arithmetic and copies ran while one was open for 0% of the time, Pallas kernels for 1%

profile of v3, /device:TPU:2, one launch (start us, length us, event | category | flops | bytes accessed | tf_op | source)
XLA Modules:
  0.0 168.6 jit_solution(14541170129250084109)
XLA Ops:
  7.2 1.9 %copy-done.1 = f32[2,128,3072]{2,1,0:T(8,128)S(1)} copy-done((f32[2,128,3072]{2,1,0:T(8,128)S(1)}, f32[2,128,3072]{2,1,0:T(8,128)}, u32[]{:S(2)}) %copy-start.1) | copy-done | bytes 3145752
  9.8 1.4 shard_map.77
  11.2 23.7 %all_to_all.20 = bf16[32,128,128]{2,1,0:T(8,128)(2,1)S(1)} all-to-all(bf16[32,128,128]{2,1,0:T(8,128)(2,1)S(1)} %bitcast.11), channel_id=1, replica_groups=mesh['slab'=32,'led'=8] {'slab'}, dimensions={0} | all-to-all | bytes 2097152 | tf_op jit(solution)/shard_map/all_to_all | solution.py:259
  34.9 3.2 %shard_map.78 = (bf16[2048,128]{1,0:T(8,128)(2,1)S(1)}, bf16[2048,128]{1,0:T(8,128)(2,1)S(1)}, f32[2048,128]{1,0:T(8,128)S(1)}, f32[2048,128]{1,0:T(8,128)S(1)}) custom-call(s32[8]{0:T(128)S(1)} %copy-done.8, bf16[4096,128]{1,0:T(8,128)(2,1)S(1)} %bitcast.10, f32[2,64,2048]{2,1,0:T(8,128)S(1)} %copy-done.3, bf16[4,512,1024]{2,1,0:T(8,128)(2,1)S(1)} %copy-done), custom_call_target="tpu_custom_call" | custom-call | flops 536870912 | bytes 9437184 | tf_op jit(solution)/shard_map/pallas_call | solution.py:245
  38.1 15.1 %all_to_all.21 = bf16[32,64,128]{2,1,0:T(8,128)(2,1)S(1)} all-to-all(bf16[32,64,128]{2,1,0:T(8,128)(2,1)S(1)} %bitcast.18), channel_id=1, replica_groups=mesh['slab'=32,'led'=8] {'slab'}, dimensions={0} | all-to-all | bytes 1048576 | tf_op jit(solution)/shard_map/all_to_all | solution.py:259
  53.2 3.5 %shard_map.79 = bf16[2048,128]{1,0:T(8,128)(2,1)S(1)} custom-call(bf16[2048,128]{1,0:T(8,128)(2,1)S(1)} %bitcast.14, f32[1,64,2048]{2,1,0:T(8,128)S(1)} %copy-done.6, bf16[4,512,1024]{2,1,0:T(8,128)(2,1)S(1)} %copy-done), custom_call_target="tpu_custom_call" | custom-call | flops 1073741824 | bytes 5767168 | tf_op jit(solution)/shard_map/pallas_call | solution.py:245
  56.7 15.2 %all_to_all.22 = bf16[32,64,128]{2,1,0:T(8,128)(2,1)S(1)} all-to-all(bf16[32,64,128]{2,1,0:T(8,128)(2,1)S(1)} %bitcast.15), channel_id=1, replica_groups=mesh['slab'=32,'led'=8] {'slab'}, dimensions={0} | all-to-all | bytes 1048576 | tf_op jit(solution)/shard_map/all_to_all | solution.py:259
  71.9 2.7 %shard_map.80 = (f32[2048,128]{1,0:T(8,128)S(1)}, bf16[2048,128]{1,0:T(8,128)(2,1)S(1)}) custom-call(s32[8]{0:T(128)S(1)} %copy-done.8, bf16[2048,128]{1,0:T(8,128)(2,1)S(1)} %bitcast.13, bf16[2048,128]{1,0:T(8,128)(2,1)S(1)} %get-tuple-element.11.win_ref, f32[2048,128]{1,0:T(8,128)S(1)} %get-tuple-element.12.pr_ref, ...), custom_call_target="tpu_custom_call" | custom-call | flops 536870912 | bytes 8912896 | tf_op jit(solution)/shard_map/pallas_call | solution.py:245
  76.4 36.5 %all_to_all.23 = bf16[256,8,128]{2,1,0:T(8,128)(2,1)S(1)} all-to-all(bf16[256,8,128]{2,1,0:T(8,128)(2,1)} %bitcast.17), channel_id=1, replica_groups=mesh['slab'=32,'led'=8] {'slab','led'}, dimensions={0} | all-to-all | bytes 1048576 | tf_op jit(solution)/shard_map/all_to_all | solution.py:310
  112.9 2.0 %shard_map.81 = (bf16[384,128]{1,0:T(8,128)(2,1)}, bf16[384,128]{1,0:T(8,128)(2,1)S(1)}) custom-call(s32[8]{0:T(128)S(1)} %copy-done.8, s32[8]{0:T(128)S(1)} %copy-done.9, bf16[2048,128]{1,0:T(8,128)(2,1)S(1)} %bitcast.12), custom_call_target="tpu_custom_call" | custom-call | bytes 720896 | tf_op jit(solution)/shard_map/pallas_call | solution.py:245
  115.6 1.0 collective-permute-start
  116.6 5.0 %collective-permute-done.7.swapped_ref = bf16[384,128]{1,0:T(8,128)(2,1)S(1)} collective-permute-done((bf16[384,128]{1,0:T(8,128)(2,1)S(1)}, bf16[384,128]{1,0:T(8,128)(2,1)S(1)}, u32[]{:S(2)}, u32[]{:S(2)}) %collective-permute-start.7) | collective-permute-done | bytes 98336 | tf_op jit(solution)/shard_map/ppermute | solution.py:319
  123.8 2.5 %collective-permute-start.9 = (bf16[640,128]{1,0:T(8,128)(2,1)S(1)}, bf16[640,128]{1,0:T(8,128)(2,1)S(1)}, u32[]{:S(2)}, u32[]{:S(2)}) collective-permute-start(bf16[640,128]{1,0:T(8,128)(2,1)S(1)} %shard_map.82.refs_8_), channel_id=1, source_target_pairs={{0,7},{1,0},{2,1},{3,2},{4,3},{5,4},{6,5},{7,6},{8,15},{9,8},{10,9... | collective-permute-start | bytes 491528 | tf_op jit(solution)/shard_map/ppermute | solution.py:273
  126.3 3.6 %collective-permute-done.8.refs_9_ = bf16[640,128]{1,0:T(8,128)(2,1)S(1)} collective-permute-done((bf16[640,128]{1,0:T(8,128)(2,1)S(1)}, bf16[640,128]{1,0:T(8,128)(2,1)S(1)}, u32[]{:S(2)}, u32[]{:S(2)}) %collective-permute-start.8) | collective-permute-done | bytes 163872 | tf_op jit(solution)/shard_map/ppermute | solution.py:270
  129.9 3.2 %collective-permute-start.11 = (bf16[640,128]{1,0:T(8,128)(2,1)S(1)}, bf16[640,128]{1,0:T(8,128)(2,1)S(1)}, u32[]{:S(2)}, u32[]{:S(2)}) collective-permute-start(bf16[640,128]{1,0:T(8,128)(2,1)S(1)} %collective-permute-done.9.refs_10_), channel_id=1, source_target_pairs={{0,7},{1,0},{2,1},{3,2},{4,3},{5,4},{6,5},{7,6},{8,15},{9,8},{10,9... | collective-permute-start | bytes 491528 | tf_op jit(solution)/shard_map/ppermute | solution.py:273
  133.1 3.3 %collective-permute-done.10.refs_11_ = bf16[640,128]{1,0:T(8,128)(2,1)S(1)} collective-permute-done((bf16[640,128]{1,0:T(8,128)(2,1)S(1)}, bf16[640,128]{1,0:T(8,128)(2,1)S(1)}, u32[]{:S(2)}, u32[]{:S(2)}) %collective-permute-start.10) | collective-permute-done | bytes 163872 | tf_op jit(solution)/shard_map/ppermute | solution.py:270
  136.4 3.2 %collective-permute-start.1 = (bf16[384,128]{1,0:T(8,128)(2,1)}, bf16[384,128]{1,0:T(8,128)(2,1)S(1)}, u32[]{:S(2)}, u32[]{:S(2)}) collective-permute-start(bf16[384,128]{1,0:T(8,128)(2,1)} %get-tuple-element.15.refs_0_), channel_id=1, source_target_pairs={{0,7},{1,0},{2,1},{3,2},{4,3},{5,4},{6,5},{7,6},{8,15},{9,8},{10,9... | collective-permute-start | bytes 294920 | tf_op jit(solution)/shard_map/ppermute | solution.py:273
  139.6 2.7 %collective-permute-done.1.refs_2_ = bf16[384,128]{1,0:T(8,128)(2,1)S(1)} collective-permute-done((bf16[384,128]{1,0:T(8,128)(2,1)}, bf16[384,128]{1,0:T(8,128)(2,1)S(1)}, u32[]{:S(2)}, u32[]{:S(2)}) %collective-permute-start.1) | collective-permute-done | bytes 98336 | tf_op jit(solution)/shard_map/ppermute | solution.py:273
  142.3 3.6 %collective-permute-start.3 = (bf16[384,128]{1,0:T(8,128)(2,1)S(1)}, bf16[384,128]{1,0:T(8,128)(2,1)S(1)}, u32[]{:S(2)}, u32[]{:S(2)}) collective-permute-start(bf16[384,128]{1,0:T(8,128)(2,1)S(1)} %collective-permute-done.1.refs_2_), channel_id=1, source_target_pairs={{0,7},{1,0},{2,1},{3,2},{4,3},{5,4},{6,5},{7,6},{8,15},{9,8},{10,9... | collective-permute-start | bytes 294920 | tf_op jit(solution)/shard_map/ppermute | solution.py:273
  145.9 3.2 %collective-permute-start.13 = (bf16[640,128]{1,0:T(8,128)(2,1)S(1)}, bf16[640,128]{1,0:T(8,128)(2,1)S(1)}, u32[]{:S(2)}, u32[]{:S(2)}) collective-permute-start(bf16[640,128]{1,0:T(8,128)(2,1)S(1)} %collective-permute-done.11.refs_12_), channel_id=1, source_target_pairs={{0,7},{1,0},{2,1},{3,2},{4,3},{5,4},{6,5},{7,6},{8,15},{9,8},{10,9... | collective-permute-start | bytes 491528 | tf_op jit(solution)/shard_map/ppermute | solution.py:273
  149.1 3.2 %collective-permute-start.5 = (bf16[384,128]{1,0:T(8,128)(2,1)S(1)}, bf16[384,128]{1,0:T(8,128)(2,1)S(1)}, u32[]{:S(2)}, u32[]{:S(2)}) collective-permute-start(bf16[384,128]{1,0:T(8,128)(2,1)S(1)} %collective-permute-done.3.refs_4_), channel_id=1, source_target_pairs={{0,7},{1,0},{2,1},{3,2},{4,3},{5,4},{6,5},{7,6},{8,15},{9,8},{10,9... | collective-permute-start | bytes 294920 | tf_op jit(solution)/shard_map/ppermute | solution.py:273
  152.6 2.0 %collective-permute-done.5.refs_6_ = bf16[384,128]{1,0:T(8,128)(2,1)S(1)} collective-permute-done((bf16[384,128]{1,0:T(8,128)(2,1)S(1)}, bf16[384,128]{1,0:T(8,128)(2,1)S(1)}, u32[]{:S(2)}, u32[]{:S(2)}) %collective-permute-start.5) | collective-permute-done | bytes 98336 | tf_op jit(solution)/shard_map/ppermute | solution.py:273
  154.6 3.8 %collective-permute-done.6.refs_7_ = bf16[384,128]{1,0:T(8,128)(2,1)S(1)} collective-permute-done((bf16[384,128]{1,0:T(8,128)(2,1)S(1)}, bf16[384,128]{1,0:T(8,128)(2,1)S(1)}, u32[]{:S(2)}, u32[]{:S(2)}) %collective-permute-start.6) | collective-permute-done | bytes 98336 | tf_op jit(solution)/shard_map/ppermute | solution.py:270
  158.4 3.3 %shard_map.83 = (f32[2,128,3072]{2,1,0:T(8,128)}, f32[2,64,2048]{2,1,0:T(8,128)}) custom-call(f32[2,128,3072]{2,1,0:T(8,128)S(1)} %copy-done.2, bf16[384,128]{1,0:T(8,128)(2,1)} %get-tuple-element.15.refs_0_, bf16[384,128]{1,0:T(8,128)(2,1)S(1)} %collective-permute-done.after_ref.refs_1_, bf16[384,128]{1,0:T(8,128)(2,1)S(1)} %collective-permute-done.1.refs_2_, ...), custom_call_target="tpu_custom_call" | custom-call | bytes 9437184 | tf_op jit(solution)/shard_map/pallas_call | solution.py:245
  (40 shorter events, 5.5 us)
Async XLA Ops:
  7.2 114.9 %reduce-scatter.2.cloned.1.call-start = ((), (), s32[]{:S(2)}) async-start(), calls=%async_computation.5 | async-start | bytes 1179648 | tf_op jit(solution)/shard_map/reduce_scatter | solution.py:309
  7.2 1.9 %copy-start.1 = (f32[2,128,3072]{2,1,0:T(8,128)S(1)}, f32[2,128,3072]{2,1,0:T(8,128)}, u32[]{:S(2)}) copy-start(f32[2,128,3072]{2,1,0:T(8,128)} %spec_ref.3) | copy-start | bytes 9437188
  9.8 25.1 %copy-start = (bf16[4,512,1024]{2,1,0:T(8,128)(2,1)S(1)}, bf16[4,512,1024]{2,1,0:T(8,128)(2,1)}, u32[]{:S(2)}) copy-start(bf16[4,512,1024]{2,1,0:T(8,128)(2,1)} %constant.2.clone.t_ref) | copy-start | bytes 12582916
  9.8 25.1 %copy-start.3 = (f32[2,64,2048]{2,1,0:T(8,128)S(1)}, f32[2,64,2048]{2,1,0:T(8,128)}, u32[]{:S(2)}) copy-start(f32[2,64,2048]{2,1,0:T(8,128)} %pupil_ref.1) | copy-start | bytes 3145732
  9.8 25.1 %copy-start.8 = (s32[8]{0:T(128)S(1)}, s32[8]{0:T(128)}, u32[]{:S(2)}) copy-start(s32[8]{0:T(128)} %row_ref.5) | copy-start | bytes 100
  34.9 18.3 %copy-start.6 = (f32[1,64,2048]{2,1,0:T(8,128)S(1)}, f32[1,64,2048]{2,1,0:T(8,128)}, u32[]{:S(2)}) copy-start(f32[1,64,2048]{2,1,0:T(8,128)} %intensity_ref.1) | copy-start | bytes 1572868
  71.9 86.5 %copy-start.2 = (f32[2,128,3072]{2,1,0:T(8,128)S(1)}, f32[2,128,3072]{2,1,0:T(8,128)}, u32[]{:S(2)}) copy-start(f32[2,128,3072]{2,1,0:T(8,128)} %spec_ref.3) | copy-start | bytes 9437188
  74.6 1.0 copy-start.4
  115.0 6.7 %collective-permute-start.7 = (bf16[384,128]{1,0:T(8,128)(2,1)S(1)}, bf16[384,128]{1,0:T(8,128)(2,1)S(1)}, u32[]{:S(2)}, u32[]{:S(2)}) collective-permute-start(bf16[384,128]{1,0:T(8,128)(2,1)S(1)} %get-tuple-element.16), channel_id=1, source_target_pairs={{0,128},{8,136},{16,144},{24,152},{32,160},{40,168},{48,176},{56,1... | collective-permute-start | bytes 294920 | tf_op jit(solution)/shard_map/ppermute | solution.py:319
  115.6 6.4 %collective-permute-start = (bf16[384,128]{1,0:T(8,128)(2,1)}, bf16[384,128]{1,0:T(8,128)(2,1)S(1)}, u32[]{:S(2)}, u32[]{:S(2)}) collective-permute-start(bf16[384,128]{1,0:T(8,128)(2,1)} %get-tuple-element.15.refs_0_), channel_id=1, source_target_pairs={{0,1},{1,2},{2,3},{3,4},{4,5},{5,6},{6,7},{7,0},{8,9},{9,10},{10,1... | collective-permute-start | bytes 294920 | tf_op jit(solution)/shard_map/ppermute | solution.py:270
  122.0 0.9 copy-start.7
  122.9 6.9 %collective-permute-start.8 = (bf16[640,128]{1,0:T(8,128)(2,1)S(1)}, bf16[640,128]{1,0:T(8,128)(2,1)S(1)}, u32[]{:S(2)}, u32[]{:S(2)}) collective-permute-start(bf16[640,128]{1,0:T(8,128)(2,1)S(1)} %shard_map.82.refs_8_), channel_id=1, source_target_pairs={{0,1},{1,2},{2,3},{3,4},{4,5},{5,6},{6,7},{7,0},{8,9},{9,10},{10,1... | collective-permute-start | bytes 491528 | tf_op jit(solution)/shard_map/ppermute | solution.py:270
  123.8 6.1 %collective-permute-start.9 = (bf16[640,128]{1,0:T(8,128)(2,1)S(1)}, bf16[640,128]{1,0:T(8,128)(2,1)S(1)}, u32[]{:S(2)}, u32[]{:S(2)}) collective-permute-start(bf16[640,128]{1,0:T(8,128)(2,1)S(1)} %shard_map.82.refs_8_), channel_id=1, source_target_pairs={{0,7},{1,0},{2,1},{3,2},{4,3},{5,4},{6,5},{7,6},{8,15},{9,8},{10,9... | collective-permute-start | bytes 491528 | tf_op jit(solution)/shard_map/ppermute | solution.py:273
  129.8 6.5 %collective-permute-start.10 = (bf16[640,128]{1,0:T(8,128)(2,1)S(1)}, bf16[640,128]{1,0:T(8,128)(2,1)S(1)}, u32[]{:S(2)}, u32[]{:S(2)}) collective-permute-start(bf16[640,128]{1,0:T(8,128)(2,1)S(1)} %collective-permute-done.8.refs_9_), channel_id=1, source_target_pairs={{0,1},{1,2},{2,3},{3,4},{4,5},{5,6},{6,7},{7,0},{8,9},{9,10},{10,1... | collective-permute-start | bytes 491528 | tf_op jit(solution)/shard_map/ppermute | solution.py:270
  129.9 16.0 %collective-permute-start.11 = (bf16[640,128]{1,0:T(8,128)(2,1)S(1)}, bf16[640,128]{1,0:T(8,128)(2,1)S(1)}, u32[]{:S(2)}, u32[]{:S(2)}) collective-permute-start(bf16[640,128]{1,0:T(8,128)(2,1)S(1)} %collective-permute-done.9.refs_10_), channel_id=1, source_target_pairs={{0,7},{1,0},{2,1},{3,2},{4,3},{5,4},{6,5},{7,6},{8,15},{9,8},{10,9... | collective-permute-start | bytes 491528 | tf_op jit(solution)/shard_map/ppermute | solution.py:273
  136.4 12.7 %collective-permute-start.12 = (bf16[640,128]{1,0:T(8,128)(2,1)S(1)}, bf16[640,128]{1,0:T(8,128)(2,1)S(1)}, u32[]{:S(2)}, u32[]{:S(2)}) collective-permute-start(bf16[640,128]{1,0:T(8,128)(2,1)S(1)} %collective-permute-done.10.refs_11_), channel_id=1, source_target_pairs={{0,1},{1,2},{2,3},{3,4},{4,5},{5,6},{6,7},{7,0},{8,9},{9,10},{10,1... | collective-permute-start | bytes 491528 | tf_op jit(solution)/shard_map/ppermute | solution.py:270
  136.4 5.9 %collective-permute-start.1 = (bf16[384,128]{1,0:T(8,128)(2,1)}, bf16[384,128]{1,0:T(8,128)(2,1)S(1)}, u32[]{:S(2)}, u32[]{:S(2)}) collective-permute-start(bf16[384,128]{1,0:T(8,128)(2,1)} %get-tuple-element.15.refs_0_), channel_id=1, source_target_pairs={{0,7},{1,0},{2,1},{3,2},{4,3},{5,4},{6,5},{7,6},{8,15},{9,8},{10,9... | collective-permute-start | bytes 294920 | tf_op jit(solution)/shard_map/ppermute | solution.py:273
  139.6 6.3 %collective-permute-start.2 = (bf16[384,128]{1,0:T(8,128)(2,1)S(1)}, bf16[384,128]{1,0:T(8,128)(2,1)S(1)}, u32[]{:S(2)}, u32[]{:S(2)}) collective-permute-start(bf16[384,128]{1,0:T(8,128)(2,1)S(1)} %collective-permute-done.after_ref.refs_1_), channel_id=1, source_target_pairs={{0,1},{1,2},{2,3},{3,4},{4,5},{5,6},{6,7},{7,0},{8,9},{9,10},{10,1... | collective-permute-start | bytes 294920 | tf_op jit(solution)/shard_map/ppermute | solution.py:270
  142.3 6.8 %collective-permute-start.3 = (bf16[384,128]{1,0:T(8,128)(2,1)S(1)}, bf16[384,128]{1,0:T(8,128)(2,1)S(1)}, u32[]{:S(2)}, u32[]{:S(2)}) collective-permute-start(bf16[384,128]{1,0:T(8,128)(2,1)S(1)} %collective-permute-done.1.refs_2_), channel_id=1, source_target_pairs={{0,7},{1,0},{2,1},{3,2},{4,3},{5,4},{6,5},{7,6},{8,15},{9,8},{10,9... | collective-permute-start | bytes 294920 | tf_op jit(solution)/shard_map/ppermute | solution.py:273
  145.9 6.7 %collective-permute-start.4 = (bf16[384,128]{1,0:T(8,128)(2,1)S(1)}, bf16[384,128]{1,0:T(8,128)(2,1)S(1)}, u32[]{:S(2)}, u32[]{:S(2)}) collective-permute-start(bf16[384,128]{1,0:T(8,128)(2,1)S(1)} %collective-permute-done.2.refs_3_), channel_id=1, source_target_pairs={{0,1},{1,2},{2,3},{3,4},{4,5},{5,6},{6,7},{7,0},{8,9},{9,10},{10,1... | collective-permute-start | bytes 294920 | tf_op jit(solution)/shard_map/ppermute | solution.py:270
  145.9 12.5 %collective-permute-start.13 = (bf16[640,128]{1,0:T(8,128)(2,1)S(1)}, bf16[640,128]{1,0:T(8,128)(2,1)S(1)}, u32[]{:S(2)}, u32[]{:S(2)}) collective-permute-start(bf16[640,128]{1,0:T(8,128)(2,1)S(1)} %collective-permute-done.11.refs_12_), channel_id=1, source_target_pairs={{0,7},{1,0},{2,1},{3,2},{4,3},{5,4},{6,5},{7,6},{8,15},{9,8},{10,9... | collective-permute-start | bytes 491528 | tf_op jit(solution)/shard_map/ppermute | solution.py:273
  149.1 9.3 %collective-permute-start.14 = (bf16[640,128]{1,0:T(8,128)(2,1)S(1)}, bf16[640,128]{1,0:T(8,128)(2,1)S(1)}, u32[]{:S(2)}, u32[]{:S(2)}) collective-permute-start(bf16[640,128]{1,0:T(8,128)(2,1)S(1)} %collective-permute-done.12.refs_13_), channel_id=1, source_target_pairs={{0,1},{1,2},{2,3},{3,4},{4,5},{5,6},{6,7},{7,0},{8,9},{9,10},{10,1... | collective-permute-start | bytes 491528 | tf_op jit(solution)/shard_map/ppermute | solution.py:270
  149.1 5.5 %collective-permute-start.5 = (bf16[384,128]{1,0:T(8,128)(2,1)S(1)}, bf16[384,128]{1,0:T(8,128)(2,1)S(1)}, u32[]{:S(2)}, u32[]{:S(2)}) collective-permute-start(bf16[384,128]{1,0:T(8,128)(2,1)S(1)} %collective-permute-done.3.refs_4_), channel_id=1, source_target_pairs={{0,7},{1,0},{2,1},{3,2},{4,3},{5,4},{6,5},{7,6},{8,15},{9,8},{10,9... | collective-permute-start | bytes 294920 | tf_op jit(solution)/shard_map/ppermute | solution.py:273
  152.6 5.8 %collective-permute-start.6 = (bf16[384,128]{1,0:T(8,128)(2,1)S(1)}, bf16[384,128]{1,0:T(8,128)(2,1)S(1)}, u32[]{:S(2)}, u32[]{:S(2)}) collective-permute-start(bf16[384,128]{1,0:T(8,128)(2,1)S(1)} %collective-permute-done.4.refs_5_), channel_id=1, source_target_pairs={{0,1},{1,2},{2,3},{3,4},{4,5},{5,6},{6,7},{7,0},{8,9},{9,10},{10,1... | collective-permute-start | bytes 294920 | tf_op jit(solution)/shard_map/ppermute | solution.py:270
  (2 other events, 1.4 us)
Sparse Core Ops, SparseCore 0:
  76.5 44.4 reduce-scatter.1

commit v4 on v3

--- a/solution.py
+++ b/solution.py
@@ -157,7 +157,7 @@
         cs = swap(change)
         wr = jnp.where(low, w, ws)
         wi = jnp.where(low, ws, -w)
-        grad_ref[rows, :] = change * wr + cs * wi
+        grad_ref[rows, :] = (change * wr + cs * wi).astype(BF16)
         c_ref[pl.ds(row + start, size), :] = (change * pr - cs * pi) / (pr * pr + pi * pi + PUPIL_DAMPING)
 
     dft(x_ref, t_ref, g_ref, -1, update)
@@ -170,7 +170,7 @@
         corr_ref[dest * 64 : dest * 64 + 64, :] = value.astype(BF16)
 
 
-def reduce_kernel(row_ref, col_ref, recv_ref, own_ref, other_ref, acc_ref):
+def reduce_kernel(row_ref, col_ref, recv_ref, grad_ref, own_ref, other_ref, acc_ref):
     slab, led = lax.axis_index("slab"), lax.axis_index("led")
     upper = slab // 16
     base = (slab % 16) * 128 + upper * 64 + led * 8
@@ -205,25 +205,25 @@
         return carry
 
     lax.fori_loop(0, 4, pair, 0)
-    own_ref[...] = acc_ref[0, : NC // 8, :].astype(BF16)
+    own_ref[: NC // 8, :] = acc_ref[0, : NC // 8, :].astype(BF16)
+    for start in range(0, W // 8, 64):
+        total = grad_ref[start : start + 64, :].astype(F32)
+        for j in range(1, 8):
+            total += grad_ref[j * (W // 8) + start : j * (W // 8) + start + 64, :].astype(F32)
+        own_ref[NC // 8 + start : NC // 8 + start + 64, :] = total.astype(BF16)
     other_ref[...] = acc_ref[1, : NC // 8, :].astype(BF16)
 
 
-def merge_kernel(swapped_ref, grad_ref, after_ref, out_ref):
-    out_ref[: NC // 8, :] = swapped_ref[...]
-    out_ref[NC // 8 :, :] = grad_ref[...].astype(BF16)
-
-
 HOPS = (0, 1, -1, 2, -2, 3, -3, 4)
 
 
 def finish_kernel(spec_ref, *refs):
-    own, rest, (new_ref, out_ref) = refs[:8], refs[8:16], refs[16:]
+    own, swapped, (new_ref, out_ref) = refs[:8], refs[8:16], refs[16:]
     slab, led = lax.axis_index("slab"), lax.axis_index("led")
     upper = slab // 16
-    for hop, own_ref, rest_ref in zip(HOPS, own, rest):
+    for hop, own_ref, swapped_ref in zip(HOPS, own, swapped):
         source = lax.rem(led - hop + 8, 8)
-        for half, ref in ((upper, own_ref), (1 - upper, rest_ref)):
+        for half, ref in ((upper, own_ref), (1 - upper, swapped_ref)):
             rows = pl.ds(pl.multiple_of(half * 64 + source * 8, 8), 8)
             for t in range(NC // 128):
                 x = ref[t * 16 : t * 16 + 16, :].astype(F32)
@@ -232,7 +232,7 @@
                 new_ref[1, rows, columns] = spec_ref[1, rows, columns] + x[8:]
         for t in range(2):
             start = NC // 8 + t * 128
-            x = rest_ref[start : start + 128, :].astype(F32).T
+            x = own_ref[start : start + 128, :].astype(F32).T
             columns = pl.ds(pl.multiple_of(source * 256 + t * 128, 128), 128)
             out_ref[0, :, columns] = x[:BAND]
             out_ref[1, :, columns] = x[BAND:]
@@ -300,34 +300,30 @@
     returned = turn_bands(second)
     gradient, correction = call(
         last_kernel,
-        [(rows128, F32), (rows128, BF16)],
+        [(rows128, BF16), (rows128, BF16)],
         [row_offsets],
         [returned, window, pr, pi, tab],
         [VMEM(rows128, F32), VMEM((2 * W, 128), F32), VMEM((4, QUARTER, 128), F32)],
         flops,
     )
-    grad_part = lax.psum_scatter(gradient.reshape(8, W // 8, 128), "led", scatter_dimension=0)
+    grads = lax.all_to_all(gradient.reshape(8, W // 8, 128), "led", 0, 0).reshape(rows128)
     landed = lax.all_to_all(correction.reshape(256, 8, 128), ("slab", "led"), 0, 0).reshape(rows128)
-    piece = (NC // 128 * 16, 128)
+    piece = NC // 8
     own, other = call(
         reduce_kernel,
-        [(piece, BF16), (piece, BF16)],
+        [((piece + W // 8, 128), BF16), ((piece, 128), BF16)],
         [row_offsets, col_offsets],
-        [landed],
-        [VMEM((2, (NC // 128 + 1) * 16, 128), F32)],
-    )
+        [landed, grads],
+        [VMEM((2, piece + 16, 128), F32)],
+    )
+    own_pieces = ring_gather(own)
     swapped = lax.ppermute(other, "slab", [(i, (i + 16) % 32) for i in range(32)])
-    own_pieces = ring_gather(own)
-    (rest,) = call(
-        merge_kernel, [((piece[0] + W // 8, 128), BF16)], [], [swapped, grad_part.reshape(W // 8, 128), own_pieces[1]]
-    )
-    new_spectrum, grad = call(
+    return call(
         finish_kernel,
         [((2, 128, NC), F32), ((2, BAND, W), F32)],
         [],
-        [spectrum, *own_pieces, *ring_gather(rest)],
-    )
-    return new_spectrum, grad
+        [spectrum, *own_pieces, *ring_gather(swapped)],
+    )
 
 
 def solution(mesh):

time: 170 us -> 163 us (0.959)
  blocking collectives: 90.5 us -> 106 us
  between operations: 14.1 us -> 0.73 us
  waiting for transfers between devices: 21 us -> 16.3 us
  local copies, waits for them, and re-layouts: 5.22 us -> 2.87 us
    all_to_all x0 -> x1, blocking collectives: none -> 26.6 us  [per_device(): lax.all_to_all(gradient.reshape(8, W // 8, 128), 'led', 0, 0)]
    all_to_all x1, blocking collectives: 36.5 us -> 25.2 us  [per_device(): lax.all_to_all(correction.reshape(256, 8, 128), ('slab', 'led'), 0, 0)]
    ppermute x1, waiting for transfers between devices: 5.02 us -> 0.01 us  [per_device(): lax.ppermute(other, 'slab', [(i, (i + 16) % 32) for i in range(32)])]
    unnamed x20 -> x14, local copies, waits for them, and re-layouts: 5.22 us -> 2.87 us
    pallas_call x7 -> x6, Pallas kernels: 16.2 us -> 15 us  [call(): pl.pallas_call(kernel, out_shape=shapes, in_specs=[pl.BlockSpec(memory_sp...]
  transfers between devices with their start and end apart: 16 -> 15, of which waited for: 8 -> 6; matrix products, arithmetic and copies ran while one was open for 0% -> 0% of each run, Pallas kernels for 1% -> 0%
where the time goes in v4:
time: 163 us
  blocking collectives  106 us (65%)
  starting transfers between devices  22.1 us (14%)
  waiting for transfers between devices  16.3 us (10%)
  Pallas kernels  15 us (9%)
  local copies, waits for them, and re-layouts  2.87 us (2%)
    all_to_all x3, blocking collectives, turn_bands(): return lax.all_to_all(blocks, 'slab', 0, 0).reshape(-1, 128)  53.8 us
    all_to_all x1, blocking collectives, per_device(): lax.all_to_all(gradient.reshape(8, W // 8, 128), 'led', 0, 0)  26.6 us
    all_to_all x1, blocking collectives, per_device(): lax.all_to_all(correction.reshape(256, 8, 128), ('slab', 'led'), 0, 0)  25.2 us
    ppermute x6, starting transfers between devices, ring_gather(): backward = lax.ppermute(backward, 'led', BACKWARD)  19.2 us
    pallas_call x6, Pallas kernels, call(): pl.pallas_call(kernel, out_shape=shapes, in_specs=[pl.BlockSpec(memory_sp...  15 us
    ppermute x8, waiting for transfers between devices, ring_gather(): forward = lax.ppermute(forward, 'led', FORWARD)  12 us
    ppermute x6, waiting for transfers between devices, ring_gather(): backward = lax.ppermute(backward, 'led', BACKWARD)  4.34 us
  transfers between devices with their start and end apart: 15, of which 6 were waited for; matrix products, arithmetic and copies ran while one was open for 0% of the time, Pallas kernels for 0%

profile of v4, /device:TPU:2, one launch (start us, length us, event | category | flops | bytes accessed | tf_op | source)
XLA Modules:
  0.0 162.6 jit_solution(1213856918708715032)
XLA Ops:
  0.7 2.0 %copy-done.1 = f32[2,128,3072]{2,1,0:T(8,128)S(1)} copy-done((f32[2,128,3072]{2,1,0:T(8,128)S(1)}, f32[2,128,3072]{2,1,0:T(8,128)}, u32[]{:S(2)}) %copy-start.1) | copy-done | bytes 3145752
  3.5 1.4 shard_map.77
  4.9 23.5 %all_to_all.25 = bf16[32,128,128]{2,1,0:T(8,128)(2,1)S(1)} all-to-all(bf16[32,128,128]{2,1,0:T(8,128)(2,1)S(1)} %bitcast.11), channel_id=1, replica_groups=mesh['slab'=32,'led'=8] {'slab'}, dimensions={0} | all-to-all | bytes 2097152 | tf_op jit(solution)/shard_map/all_to_all | solution.py:259
  28.5 3.2 %shard_map.78 = (bf16[2048,128]{1,0:T(8,128)(2,1)S(1)}, bf16[2048,128]{1,0:T(8,128)(2,1)S(1)}, f32[2048,128]{1,0:T(8,128)S(1)}, f32[2048,128]{1,0:T(8,128)S(1)}) custom-call(s32[8]{0:T(128)S(1)} %copy-done.5, bf16[4096,128]{1,0:T(8,128)(2,1)S(1)} %bitcast.10, f32[2,64,2048]{2,1,0:T(8,128)S(1)} %copy-done.3, bf16[4,512,1024]{2,1,0:T(8,128)(2,1)S(1)} %copy-done), custom_call_target="tpu_custom_call" | custom-call | flops 536870912 | bytes 9437184 | tf_op jit(solution)/shard_map/pallas_call | solution.py:245
  31.7 15.1 %all_to_all.26 = bf16[32,64,128]{2,1,0:T(8,128)(2,1)S(1)} all-to-all(bf16[32,64,128]{2,1,0:T(8,128)(2,1)S(1)} %bitcast.19), channel_id=1, replica_groups=mesh['slab'=32,'led'=8] {'slab'}, dimensions={0} | all-to-all | bytes 1048576 | tf_op jit(solution)/shard_map/all_to_all | solution.py:259
  46.8 3.5 %shard_map.79 = bf16[2048,128]{1,0:T(8,128)(2,1)S(1)} custom-call(bf16[2048,128]{1,0:T(8,128)(2,1)S(1)} %bitcast.15, f32[1,64,2048]{2,1,0:T(8,128)S(1)} %copy-done.4, bf16[4,512,1024]{2,1,0:T(8,128)(2,1)S(1)} %copy-done), custom_call_target="tpu_custom_call" | custom-call | flops 1073741824 | bytes 5767168 | tf_op jit(solution)/shard_map/pallas_call | solution.py:245
  50.3 15.2 %all_to_all.27 = bf16[32,64,128]{2,1,0:T(8,128)(2,1)S(1)} all-to-all(bf16[32,64,128]{2,1,0:T(8,128)(2,1)S(1)} %bitcast.16), channel_id=1, replica_groups=mesh['slab'=32,'led'=8] {'slab'}, dimensions={0} | all-to-all | bytes 1048576 | tf_op jit(solution)/shard_map/all_to_all | solution.py:259
  65.5 2.9 %shard_map.80 = (bf16[2048,128]{1,0:T(8,128)(2,1)S(1)}, bf16[2048,128]{1,0:T(8,128)(2,1)S(1)}) custom-call(s32[8]{0:T(128)S(1)} %copy-done.5, bf16[2048,128]{1,0:T(8,128)(2,1)S(1)} %bitcast.14, bf16[2048,128]{1,0:T(8,128)(2,1)S(1)} %get-tuple-element.11.win_ref, f32[2048,128]{1,0:T(8,128)S(1)} %get-tuple-element.12.pr_ref, ...), custom_call_target="tpu_custom_call" | custom-call | flops 536870912 | bytes 8388608 | tf_op jit(solution)/shard_map/pallas_call | solution.py:245
  68.4 26.6 %all_to_all.28 = bf16[8,256,128]{2,1,0:T(8,128)(2,1)S(1)} all-to-all(bf16[8,256,128]{2,1,0:T(8,128)(2,1)S(1)} %bitcast.18), channel_id=1, replica_groups=mesh['slab'=32,'led'=8] {'led'}, dimensions={0} | all-to-all | bytes 1048576 | tf_op jit(solution)/shard_map/all_to_all | solution.py:309
  95.0 25.2 %all_to_all.29 = bf16[256,8,128]{2,1,0:T(8,128)(2,1)S(1)} all-to-all(bf16[256,8,128]{2,1,0:T(8,128)(2,1)S(1)} %bitcast.17), channel_id=1, replica_groups=mesh['slab'=32,'led'=8] {'slab','led'}, dimensions={0} | all-to-all | bytes 1048576 | tf_op jit(solution)/shard_map/all_to_all | solution.py:310
  120.2 1.5 shard_map.81
  122.7 1.5 collective-permute-start.7
  124.2 2.2 %collective-permute-start.1 = (bf16[640,128]{1,0:T(8,128)(2,1)S(1)}, bf16[640,128]{1,0:T(8,128)(2,1)S(1)}, u32[]{:S(2)}, u32[]{:S(2)}) collective-permute-start(bf16[640,128]{1,0:T(8,128)(2,1)S(1)} %get-tuple-element.16.refs_0_), channel_id=1, source_target_pairs={{0,7},{1,0},{2,1},{3,2},{4,3},{5,4},{6,5},{7,6},{8,15},{9,8},{10,9... | collective-permute-start | bytes 491528 | tf_op jit(solution)/shard_map/ppermute | solution.py:273
  126.4 3.6 %collective-permute-done.refs_1_ = bf16[640,128]{1,0:T(8,128)(2,1)S(1)} collective-permute-done((bf16[640,128]{1,0:T(8,128)(2,1)S(1)}, bf16[640,128]{1,0:T(8,128)(2,1)S(1)}, u32[]{:S(2)}, u32[]{:S(2)}) %collective-permute-start) | collective-permute-done | bytes 163872 | tf_op jit(solution)/shard_map/ppermute | solution.py:270
  130.4 3.3 %collective-permute-start.3 = (bf16[640,128]{1,0:T(8,128)(2,1)S(1)}, bf16[640,128]{1,0:T(8,128)(2,1)S(1)}, u32[]{:S(2)}, u32[]{:S(2)}) collective-permute-start(bf16[640,128]{1,0:T(8,128)(2,1)S(1)} %collective-permute-done.1.refs_2_), channel_id=1, source_target_pairs={{0,7},{1,0},{2,1},{3,2},{4,3},{5,4},{6,5},{7,6},{8,15},{9,8},{10,9... | collective-permute-start | bytes 491528 | tf_op jit(solution)/shard_map/ppermute | solution.py:273
  133.7 4.6 %collective-permute-done.2.refs_3_ = bf16[640,128]{1,0:T(8,128)(2,1)S(1)} collective-permute-done((bf16[640,128]{1,0:T(8,128)(2,1)S(1)}, bf16[640,128]{1,0:T(8,128)(2,1)S(1)}, u32[]{:S(2)}, u32[]{:S(2)}) %collective-permute-start.2) | collective-permute-done | bytes 163872 | tf_op jit(solution)/shard_map/ppermute | solution.py:270
  138.3 3.2 %collective-permute-start.9 = (bf16[384,128]{1,0:T(8,128)(2,1)S(1)}, bf16[384,128]{1,0:T(8,128)(2,1)S(1)}, u32[]{:S(2)}, u32[]{:S(2)}) collective-permute-start(bf16[384,128]{1,0:T(8,128)(2,1)S(1)} %collective-permute-done.7.refs_8_), channel_id=1, source_target_pairs={{0,7},{1,0},{2,1},{3,2},{4,3},{5,4},{6,5},{7,6},{8,15},{9,8},{10,9... | collective-permute-start | bytes 294920 | tf_op jit(solution)/shard_map/ppermute | solution.py:273
  141.6 2.2 %collective-permute-done.9.refs_10_ = bf16[384,128]{1,0:T(8,128)(2,1)S(1)} collective-permute-done((bf16[384,128]{1,0:T(8,128)(2,1)S(1)}, bf16[384,128]{1,0:T(8,128)(2,1)S(1)}, u32[]{:S(2)}, u32[]{:S(2)}) %collective-permute-start.9) | collective-permute-done | bytes 98336 | tf_op jit(solution)/shard_map/ppermute | solution.py:273
  143.8 3.6 %collective-permute-start.11 = (bf16[384,128]{1,0:T(8,128)(2,1)S(1)}, bf16[384,128]{1,0:T(8,128)(2,1)S(1)}, u32[]{:S(2)}, u32[]{:S(2)}) collective-permute-start(bf16[384,128]{1,0:T(8,128)(2,1)S(1)} %collective-permute-done.9.refs_10_), channel_id=1, source_target_pairs={{0,7},{1,0},{2,1},{3,2},{4,3},{5,4},{6,5},{7,6},{8,15},{9,8},{10,9... | collective-permute-start | bytes 294920 | tf_op jit(solution)/shard_map/ppermute | solution.py:273
  147.4 3.2 %collective-permute-start.5 = (bf16[640,128]{1,0:T(8,128)(2,1)S(1)}, bf16[640,128]{1,0:T(8,128)(2,1)S(1)}, u32[]{:S(2)}, u32[]{:S(2)}) collective-permute-start(bf16[640,128]{1,0:T(8,128)(2,1)S(1)} %collective-permute-done.3.refs_4_), channel_id=1, source_target_pairs={{0,7},{1,0},{2,1},{3,2},{4,3},{5,4},{6,5},{7,6},{8,15},{9,8},{10,9... | collective-permute-start | bytes 491528 | tf_op jit(solution)/shard_map/ppermute | solution.py:273
  150.6 3.5 %collective-permute-start.13 = (bf16[384,128]{1,0:T(8,128)(2,1)S(1)}, bf16[384,128]{1,0:T(8,128)(2,1)S(1)}, u32[]{:S(2)}, u32[]{:S(2)}) collective-permute-start(bf16[384,128]{1,0:T(8,128)(2,1)S(1)} %collective-permute-done.11.refs_12_), channel_id=1, source_target_pairs={{0,7},{1,0},{2,1},{3,2},{4,3},{5,4},{6,5},{7,6},{8,15},{9,8},{10,9... | collective-permute-start | bytes 294920 | tf_op jit(solution)/shard_map/ppermute | solution.py:273
  154.3 2.1 %collective-permute-done.13.refs_14_ = bf16[384,128]{1,0:T(8,128)(2,1)S(1)} collective-permute-done((bf16[384,128]{1,0:T(8,128)(2,1)S(1)}, bf16[384,128]{1,0:T(8,128)(2,1)S(1)}, u32[]{:S(2)}, u32[]{:S(2)}) %collective-permute-start.13) | collective-permute-done | bytes 98336 | tf_op jit(solution)/shard_map/ppermute | solution.py:273
  156.4 3.7 %collective-permute-done.14.refs_15_ = bf16[384,128]{1,0:T(8,128)(2,1)S(1)} collective-permute-done((bf16[384,128]{1,0:T(8,128)(2,1)S(1)}, bf16[384,128]{1,0:T(8,128)(2,1)S(1)}, u32[]{:S(2)}, u32[]{:S(2)}) %collective-permute-start.14) | collective-permute-done | bytes 98336 | tf_op jit(solution)/shard_map/ppermute | solution.py:270
  160.1 2.5 %shard_map.82 = (f32[2,128,3072]{2,1,0:T(8,128)}, f32[2,64,2048]{2,1,0:T(8,128)}) custom-call(f32[2,128,3072]{2,1,0:T(8,128)S(1)} %copy-done.2, bf16[640,128]{1,0:T(8,128)(2,1)S(1)} %get-tuple-element.16.refs_0_, bf16[640,128]{1,0:T(8,128)(2,1)S(1)} %collective-permute-done.refs_1_, bf16[640,128]{1,0:T(8,128)(2,1)S(1)} %collective-permute-done.1.refs_2_, ...), custom_call_target="tpu_custom_call" | custom-call | bytes 9437184 | tf_op jit(solution)/shard_map/pallas_call | solution.py:245
  (31 shorter events, 2.4 us)
Async XLA Ops:
  0.6 27.8 %copy-start = (bf16[4,512,1024]{2,1,0:T(8,128)(2,1)S(1)}, bf16[4,512,1024]{2,1,0:T(8,128)(2,1)}, u32[]{:S(2)}) copy-start(bf16[4,512,1024]{2,1,0:T(8,128)(2,1)} %constant.2.clone.t_ref) | copy-start | bytes 12582916
  0.6 2.0 %copy-start.1 = (f32[2,128,3072]{2,1,0:T(8,128)S(1)}, f32[2,128,3072]{2,1,0:T(8,128)}, u32[]{:S(2)}) copy-start(f32[2,128,3072]{2,1,0:T(8,128)} %spec_ref.3) | copy-start | bytes 9437188
  2.7 0.8 copy-start.6
  3.5 25.0 %copy-start.3 = (f32[2,64,2048]{2,1,0:T(8,128)S(1)}, f32[2,64,2048]{2,1,0:T(8,128)}, u32[]{:S(2)}) copy-start(f32[2,64,2048]{2,1,0:T(8,128)} %pupil_ref.1) | copy-start | bytes 3145732
  3.5 25.0 %copy-start.5 = (s32[8]{0:T(128)S(1)}, s32[8]{0:T(128)}, u32[]{:S(2)}) copy-start(s32[8]{0:T(128)} %row_ref.5) | copy-start | bytes 100
  28.5 18.3 %copy-start.4 = (f32[1,64,2048]{2,1,0:T(8,128)S(1)}, f32[1,64,2048]{2,1,0:T(8,128)}, u32[]{:S(2)}) copy-start(f32[1,64,2048]{2,1,0:T(8,128)} %intensity_ref.1) | copy-start | bytes 1572868
  68.4 91.7 %copy-start.2 = (f32[2,128,3072]{2,1,0:T(8,128)S(1)}, f32[2,128,3072]{2,1,0:T(8,128)}, u32[]{:S(2)}) copy-start(f32[2,128,3072]{2,1,0:T(8,128)} %spec_ref.3) | copy-start | bytes 9437188
  121.6 8.4 %collective-permute-start = (bf16[640,128]{1,0:T(8,128)(2,1)S(1)}, bf16[640,128]{1,0:T(8,128)(2,1)S(1)}, u32[]{:S(2)}, u32[]{:S(2)}) collective-permute-start(bf16[640,128]{1,0:T(8,128)(2,1)S(1)} %get-tuple-element.16.refs_0_), channel_id=1, source_target_pairs={{0,1},{1,2},{2,3},{3,4},{4,5},{5,6},{6,7},{7,0},{8,9},{9,10},{10,1... | collective-permute-start | bytes 491528 | tf_op jit(solution)/shard_map/ppermute | solution.py:270
  122.7 7.3 %collective-permute-start.7 = (bf16[384,128]{1,0:T(8,128)(2,1)S(1)}, bf16[384,128]{1,0:T(8,128)(2,1)S(1)}, u32[]{:S(2)}, u32[]{:S(2)}) collective-permute-start(bf16[384,128]{1,0:T(8,128)(2,1)S(1)} %get-tuple-element.17), channel_id=1, source_target_pairs={{0,128},{8,136},{16,144},{24,152},{32,160},{40,168},{48,176},{56,1... | collective-permute-start | bytes 294920 | tf_op jit(solution)/shard_map/ppermute | solution.py:320
  124.2 6.2 %collective-permute-start.1 = (bf16[640,128]{1,0:T(8,128)(2,1)S(1)}, bf16[640,128]{1,0:T(8,128)(2,1)S(1)}, u32[]{:S(2)}, u32[]{:S(2)}) collective-permute-start(bf16[640,128]{1,0:T(8,128)(2,1)S(1)} %get-tuple-element.16.refs_0_), channel_id=1, source_target_pairs={{0,7},{1,0},{2,1},{3,2},{4,3},{5,4},{6,5},{7,6},{8,15},{9,8},{10,9... | collective-permute-start | bytes 491528 | tf_op jit(solution)/shard_map/ppermute | solution.py:273
  130.1 8.3 %collective-permute-start.2 = (bf16[640,128]{1,0:T(8,128)(2,1)S(1)}, bf16[640,128]{1,0:T(8,128)(2,1)S(1)}, u32[]{:S(2)}, u32[]{:S(2)}) collective-permute-start(bf16[640,128]{1,0:T(8,128)(2,1)S(1)} %collective-permute-done.refs_1_), channel_id=1, source_target_pairs={{0,1},{1,2},{2,3},{3,4},{4,5},{5,6},{6,7},{7,0},{8,9},{9,10},{10,1... | collective-permute-start | bytes 491528 | tf_op jit(solution)/shard_map/ppermute | solution.py:270
  130.1 11.5 %collective-permute-start.8 = (bf16[384,128]{1,0:T(8,128)(2,1)S(1)}, bf16[384,128]{1,0:T(8,128)(2,1)S(1)}, u32[]{:S(2)}, u32[]{:S(2)}) collective-permute-start(bf16[384,128]{1,0:T(8,128)(2,1)S(1)} %collective-permute-done.7.refs_8_), channel_id=1, source_target_pairs={{0,1},{1,2},{2,3},{3,4},{4,5},{5,6},{6,7},{7,0},{8,9},{9,10},{10,1... | collective-permute-start | bytes 294920 | tf_op jit(solution)/shard_map/ppermute | solution.py:270
  130.4 17.0 %collective-permute-start.3 = (bf16[640,128]{1,0:T(8,128)(2,1)S(1)}, bf16[640,128]{1,0:T(8,128)(2,1)S(1)}, u32[]{:S(2)}, u32[]{:S(2)}) collective-permute-start(bf16[640,128]{1,0:T(8,128)(2,1)S(1)} %collective-permute-done.1.refs_2_), channel_id=1, source_target_pairs={{0,7},{1,0},{2,1},{3,2},{4,3},{5,4},{6,5},{7,6},{8,15},{9,8},{10,9... | collective-permute-start | bytes 491528 | tf_op jit(solution)/shard_map/ppermute | solution.py:273
  138.3 12.3 %collective-permute-start.4 = (bf16[640,128]{1,0:T(8,128)(2,1)S(1)}, bf16[640,128]{1,0:T(8,128)(2,1)S(1)}, u32[]{:S(2)}, u32[]{:S(2)}) collective-permute-start(bf16[640,128]{1,0:T(8,128)(2,1)S(1)} %collective-permute-done.2.refs_3_), channel_id=1, source_target_pairs={{0,1},{1,2},{2,3},{3,4},{4,5},{5,6},{6,7},{7,0},{8,9},{9,10},{10,1... | collective-permute-start | bytes 491528 | tf_op jit(solution)/shard_map/ppermute | solution.py:270
  138.3 5.4 %collective-permute-start.9 = (bf16[384,128]{1,0:T(8,128)(2,1)S(1)}, bf16[384,128]{1,0:T(8,128)(2,1)S(1)}, u32[]{:S(2)}, u32[]{:S(2)}) collective-permute-start(bf16[384,128]{1,0:T(8,128)(2,1)S(1)} %collective-permute-done.7.refs_8_), channel_id=1, source_target_pairs={{0,7},{1,0},{2,1},{3,2},{4,3},{5,4},{6,5},{7,6},{8,15},{9,8},{10,9... | collective-permute-start | bytes 294920 | tf_op jit(solution)/shard_map/ppermute | solution.py:273
  141.6 5.8 %collective-permute-start.10 = (bf16[384,128]{1,0:T(8,128)(2,1)S(1)}, bf16[384,128]{1,0:T(8,128)(2,1)S(1)}, u32[]{:S(2)}, u32[]{:S(2)}) collective-permute-start(bf16[384,128]{1,0:T(8,128)(2,1)S(1)} %collective-permute-done.8.refs_9_), channel_id=1, source_target_pairs={{0,1},{1,2},{2,3},{3,4},{4,5},{5,6},{6,7},{7,0},{8,9},{9,10},{10,1... | collective-permute-start | bytes 294920 | tf_op jit(solution)/shard_map/ppermute | solution.py:270
  143.8 6.9 %collective-permute-start.11 = (bf16[384,128]{1,0:T(8,128)(2,1)S(1)}, bf16[384,128]{1,0:T(8,128)(2,1)S(1)}, u32[]{:S(2)}, u32[]{:S(2)}) collective-permute-start(bf16[384,128]{1,0:T(8,128)(2,1)S(1)} %collective-permute-done.9.refs_10_), channel_id=1, source_target_pairs={{0,7},{1,0},{2,1},{3,2},{4,3},{5,4},{6,5},{7,6},{8,15},{9,8},{10,9... | collective-permute-start | bytes 294920 | tf_op jit(solution)/shard_map/ppermute | solution.py:273
  147.4 6.9 %collective-permute-start.12 = (bf16[384,128]{1,0:T(8,128)(2,1)S(1)}, bf16[384,128]{1,0:T(8,128)(2,1)S(1)}, u32[]{:S(2)}, u32[]{:S(2)}) collective-permute-start(bf16[384,128]{1,0:T(8,128)(2,1)S(1)} %collective-permute-done.10.refs_11_), channel_id=1, source_target_pairs={{0,1},{1,2},{2,3},{3,4},{4,5},{5,6},{6,7},{7,0},{8,9},{9,10},{10,1... | collective-permute-start | bytes 294920 | tf_op jit(solution)/shard_map/ppermute | solution.py:270
  147.4 12.7 %collective-permute-start.5 = (bf16[640,128]{1,0:T(8,128)(2,1)S(1)}, bf16[640,128]{1,0:T(8,128)(2,1)S(1)}, u32[]{:S(2)}, u32[]{:S(2)}) collective-permute-start(bf16[640,128]{1,0:T(8,128)(2,1)S(1)} %collective-permute-done.3.refs_4_), channel_id=1, source_target_pairs={{0,7},{1,0},{2,1},{3,2},{4,3},{5,4},{6,5},{7,6},{8,15},{9,8},{10,9... | collective-permute-start | bytes 491528 | tf_op jit(solution)/shard_map/ppermute | solution.py:273
  150.6 9.5 %collective-permute-start.6 = (bf16[640,128]{1,0:T(8,128)(2,1)S(1)}, bf16[640,128]{1,0:T(8,128)(2,1)S(1)}, u32[]{:S(2)}, u32[]{:S(2)}) collective-permute-start(bf16[640,128]{1,0:T(8,128)(2,1)S(1)} %collective-permute-done.4.refs_5_), channel_id=1, source_target_pairs={{0,1},{1,2},{2,3},{3,4},{4,5},{5,6},{6,7},{7,0},{8,9},{9,10},{10,1... | collective-permute-start | bytes 491528 | tf_op jit(solution)/shard_map/ppermute | solution.py:270
  150.6 5.8 %collective-permute-start.13 = (bf16[384,128]{1,0:T(8,128)(2,1)S(1)}, bf16[384,128]{1,0:T(8,128)(2,1)S(1)}, u32[]{:S(2)}, u32[]{:S(2)}) collective-permute-start(bf16[384,128]{1,0:T(8,128)(2,1)S(1)} %collective-permute-done.11.refs_12_), channel_id=1, source_target_pairs={{0,7},{1,0},{2,1},{3,2},{4,3},{5,4},{6,5},{7,6},{8,15},{9,8},{10,9... | collective-permute-start | bytes 294920 | tf_op jit(solution)/shard_map/ppermute | solution.py:273
  154.3 5.8 %collective-permute-start.14 = (bf16[384,128]{1,0:T(8,128)(2,1)S(1)}, bf16[384,128]{1,0:T(8,128)(2,1)S(1)}, u32[]{:S(2)}, u32[]{:S(2)}) collective-permute-start(bf16[384,128]{1,0:T(8,128)(2,1)S(1)} %collective-permute-done.12.refs_13_), channel_id=1, source_target_pairs={{0,1},{1,2},{2,3},{3,4},{4,5},{5,6},{6,7},{7,0},{8,9},{9,10},{10,1... | collective-permute-start | bytes 294920 | tf_op jit(solution)/shard_map/ppermute | solution.py:270

commit v5 on v4

--- a/solution.py
+++ b/solution.py
@@ -170,7 +170,7 @@
         corr_ref[dest * 64 : dest * 64 + 64, :] = value.astype(BF16)
 
 
-def reduce_kernel(row_ref, col_ref, recv_ref, grad_ref, own_ref, other_ref, acc_ref):
+def reduce_kernel(row_ref, col_ref, recv_ref, own_ref, other_ref, acc_ref):
     slab, led = lax.axis_index("slab"), lax.axis_index("led")
     upper = slab // 16
     base = (slab % 16) * 128 + upper * 64 + led * 8
@@ -205,13 +205,18 @@
         return carry
 
     lax.fori_loop(0, 4, pair, 0)
-    own_ref[: NC // 8, :] = acc_ref[0, : NC // 8, :].astype(BF16)
+    own_ref[...] = acc_ref[0, : NC // 8, :].astype(BF16)
+    other_ref[...] = acc_ref[1, : NC // 8, :].astype(BF16)
+
+
+def merge_kernel(grad_ref, swapped_ref, *refs):
+    out_ref = refs[-1]
+    out_ref[: NC // 8, :] = swapped_ref[...]
     for start in range(0, W // 8, 64):
         total = grad_ref[start : start + 64, :].astype(F32)
         for j in range(1, 8):
             total += grad_ref[j * (W // 8) + start : j * (W // 8) + start + 64, :].astype(F32)
-        own_ref[NC // 8 + start : NC // 8 + start + 64, :] = total.astype(BF16)
-    other_ref[...] = acc_ref[1, : NC // 8, :].astype(BF16)
+        out_ref[NC // 8 + start : NC // 8 + start + 64, :] = total.astype(BF16)
 
 
 HOPS = (0, 1, -1, 2, -2, 3, -3, 4)
@@ -232,7 +237,7 @@
                 new_ref[1, rows, columns] = spec_ref[1, rows, columns] + x[8:]
         for t in range(2):
             start = NC // 8 + t * 128
-            x = own_ref[start : start + 128, :].astype(F32).T
+            x = swapped_ref[start : start + 128, :].astype(F32).T
             columns = pl.ds(pl.multiple_of(source * 256 + t * 128, 128), 128)
             out_ref[0, :, columns] = x[:BAND]
             out_ref[1, :, columns] = x[BAND:]
@@ -306,23 +311,25 @@
         [VMEM(rows128, F32), VMEM((2 * W, 128), F32), VMEM((4, QUARTER, 128), F32)],
         flops,
     )
-    grads = lax.all_to_all(gradient.reshape(8, W // 8, 128), "led", 0, 0).reshape(rows128)
     landed = lax.all_to_all(correction.reshape(256, 8, 128), ("slab", "led"), 0, 0).reshape(rows128)
+    gradient, landed = lax.optimization_barrier((gradient, landed))
     piece = NC // 8
     own, other = call(
         reduce_kernel,
-        [((piece + W // 8, 128), BF16), ((piece, 128), BF16)],
+        [((piece, 128), BF16)] * 2,
         [row_offsets, col_offsets],
-        [landed, grads],
+        [landed],
         [VMEM((2, piece + 16, 128), F32)],
     )
+    swapped = lax.ppermute(other, "slab", [(i, (i + 16) % 32) for i in range(32)])
+    grads = lax.all_to_all(gradient.reshape(8, W // 8, 128), "led", 0, 0).reshape(rows128)
     own_pieces = ring_gather(own)
-    swapped = lax.ppermute(other, "slab", [(i, (i + 16) % 32) for i in range(32)])
+    (rest,) = call(merge_kernel, [((piece + W // 8, 128), BF16)], [], [grads, swapped, *own_pieces[1:3]])
     return call(
         finish_kernel,
         [((2, 128, NC), F32), ((2, BAND, W), F32)],
         [],
-        [spectrum, *own_pieces, *ring_gather(swapped)],
+        [spectrum, *own_pieces, *ring_gather(rest)],
     )
 
 

time: 163 us -> 160 us (0.982)
  blocking collectives: 106 us -> 84.9 us
  waiting for transfers between devices: 16.3 us -> 29.4 us
  starting transfers between devices: 22.1 us -> 25.1 us
    all_to_all x1 -> x0, blocking collectives: 26.6 us -> none  [per_device(): lax.all_to_all(gradient.reshape(8, W // 8, 128), 'led', 0, 0)]
    all_to_all x1, blocking collectives: 25.2 us -> 31.1 us  [per_device(): lax.all_to_all(correction.reshape(256, 8, 128), ('slab', 'led'), 0, 0)]
    ppermute x6, waiting for transfers between devices: 4.34 us -> 9.28 us  [ring_gather(): backward = lax.ppermute(backward, 'led', BACKWARD)]
    ppermute x8, waiting for transfers between devices: 12 us -> 16.2 us  [ring_gather(): forward = lax.ppermute(forward, 'led', FORWARD)]
    all_to_all x0 -> x1, starting transfers between devices: none -> 4.14 us  [per_device(): lax.all_to_all(gradient.reshape(8, W // 8, 128), 'led', 0, 0)]
    ppermute x1, waiting for transfers between devices: 0.01 us -> 2.6 us  [per_device(): lax.ppermute(other, 'slab', [(i, (i + 16) % 32) for i in range(32)])]
    unnamed x14 -> x20, local copies, waits for them, and re-layouts: 2.87 us -> 3.92 us
    pallas_call x6 -> x7, Pallas kernels: 15 us -> 15.7 us  [call(): pl.pallas_call(kernel, out_shape=shapes, in_specs=[pl.BlockSpec(memory_sp...]
  transfers between devices with their start and end apart: 15 -> 16, of which waited for: 6 -> 9; matrix products, arithmetic and copies ran while one was open for 0% -> 0% of each run, Pallas kernels for 0% -> 1%
where the time goes in v5:
time: 160 us
  blocking collectives  84.9 us (53%)
  waiting for transfers between devices  29.4 us (18%)
  starting transfers between devices  25.1 us (16%)
  Pallas kernels  15.7 us (10%)
  local copies, waits for them, and re-layouts  3.92 us (2%)
    all_to_all x3, blocking collectives, turn_bands(): return lax.all_to_all(blocks, 'slab', 0, 0).reshape(-1, 128)  53.8 us
    all_to_all x1, blocking collectives, per_device(): lax.all_to_all(correction.reshape(256, 8, 128), ('slab', 'led'), 0, 0)  31.1 us
    ppermute x6, starting transfers between devices, ring_gather(): backward = lax.ppermute(backward, 'led', BACKWARD)  19 us
    ppermute x8, waiting for transfers between devices, ring_gather(): forward = lax.ppermute(forward, 'led', FORWARD)  16.2 us
    pallas_call x7, Pallas kernels, call(): pl.pallas_call(kernel, out_shape=shapes, in_specs=[pl.BlockSpec(memory_sp...  15.7 us
    ppermute x6, waiting for transfers between devices, ring_gather(): backward = lax.ppermute(backward, 'led', BACKWARD)  9.28 us
    all_to_all x1, starting transfers between devices, per_device(): lax.all_to_all(gradient.reshape(8, W // 8, 128), 'led', 0, 0)  4.14 us
    unnamed x20, local copies, waits for them, and re-layouts  3.92 us
  transfers between devices with their start and end apart: 16, of which 9 were waited for; matrix products, arithmetic and copies ran while one was open for 0% of the time, Pallas kernels for 1%

profile of v5, /device:TPU:2, one launch (start us, length us, event | category | flops | bytes accessed | tf_op | source)
XLA Modules:
  0.0 159.9 jit_solution(4230219999548506134)
XLA Ops:
  0.7 2.0 %copy-done.1 = f32[2,128,3072]{2,1,0:T(8,128)S(1)} copy-done((f32[2,128,3072]{2,1,0:T(8,128)S(1)}, f32[2,128,3072]{2,1,0:T(8,128)}, u32[]{:S(2)}) %copy-start.1) | copy-done | bytes 3145752
  4.9 23.5 %all_to_all.25 = bf16[32,128,128]{2,1,0:T(8,128)(2,1)S(1)} all-to-all(bf16[32,128,128]{2,1,0:T(8,128)(2,1)S(1)} %bitcast.11), channel_id=1, replica_groups=mesh['slab'=32,'led'=8] {'slab'}, dimensions={0} | all-to-all | bytes 2097152 | tf_op jit(solution)/shard_map/all_to_all | solution.py:264
  28.5 3.2 %shard_map.78 = (bf16[2048,128]{1,0:T(8,128)(2,1)S(1)}, bf16[2048,128]{1,0:T(8,128)(2,1)S(1)}, f32[2048,128]{1,0:T(8,128)S(1)}, f32[2048,128]{1,0:T(8,128)S(1)}) custom-call(s32[8]{0:T(128)S(1)} %copy-done.7, bf16[4096,128]{1,0:T(8,128)(2,1)S(1)} %bitcast.10, f32[2,64,2048]{2,1,0:T(8,128)S(1)} %copy-done.4, bf16[4,512,1024]{2,1,0:T(8,128)(2,1)S(1)} %copy-done), custom_call_target="tpu_custom_call" | custom-call | flops 536870912 | bytes 9437184 | tf_op jit(solution)/shard_map/pallas_call | solution.py:250
  31.7 15.1 %all_to_all.26 = bf16[32,64,128]{2,1,0:T(8,128)(2,1)S(1)} all-to-all(bf16[32,64,128]{2,1,0:T(8,128)(2,1)S(1)} %bitcast.18), channel_id=1, replica_groups=mesh['slab'=32,'led'=8] {'slab'}, dimensions={0} | all-to-all | bytes 1048576 | tf_op jit(solution)/shard_map/all_to_all | solution.py:264
  46.8 3.5 %shard_map.79 = bf16[2048,128]{1,0:T(8,128)(2,1)S(1)} custom-call(bf16[2048,128]{1,0:T(8,128)(2,1)S(1)} %bitcast.14, f32[1,64,2048]{2,1,0:T(8,128)S(1)} %copy-done.6, bf16[4,512,1024]{2,1,0:T(8,128)(2,1)S(1)} %copy-done), custom_call_target="tpu_custom_call" | custom-call | flops 1073741824 | bytes 5767168 | tf_op jit(solution)/shard_map/pallas_call | solution.py:250
  50.2 15.2 %all_to_all.27 = bf16[32,64,128]{2,1,0:T(8,128)(2,1)S(1)} all-to-all(bf16[32,64,128]{2,1,0:T(8,128)(2,1)S(1)} %bitcast.15), channel_id=1, replica_groups=mesh['slab'=32,'led'=8] {'slab'}, dimensions={0} | all-to-all | bytes 1048576 | tf_op jit(solution)/shard_map/all_to_all | solution.py:264
  65.5 2.7 %shard_map.80 = (bf16[2048,128]{1,0:T(8,128)(2,1)S(1)}, bf16[2048,128]{1,0:T(8,128)(2,1)S(1)}) custom-call(s32[8]{0:T(128)S(1)} %copy-done.7, bf16[2048,128]{1,0:T(8,128)(2,1)S(1)} %bitcast.13, bf16[2048,128]{1,0:T(8,128)(2,1)S(1)} %get-tuple-element.13.win_ref, f32[2048,128]{1,0:T(8,128)S(1)} %get-tuple-element.14.pr_ref, ...), custom_call_target="tpu_custom_call" | custom-call | flops 536870912 | bytes 8388608 | tf_op jit(solution)/shard_map/pallas_call | solution.py:250
  68.2 31.1 %all_to_all.28 = bf16[256,8,128]{2,1,0:T(8,128)(2,1)} all-to-all(bf16[256,8,128]{2,1,0:T(8,128)(2,1)S(1)} %bitcast.17), channel_id=1, replica_groups=mesh['slab'=32,'led'=8] {'slab','led'}, dimensions={0} | all-to-all | bytes 1048576 | tf_op jit(solution)/shard_map/all_to_all | solution.py:314
  99.3 4.1 %all-to-all-start.4 = ((bf16[8,256,128]{2,1,0:T(8,128)(2,1)}), bf16[8,256,128]{2,1,0:T(8,128)(2,1)}, u32[]{:S(2)}, u32[]{:S(2)}) async-start(bf16[8,256,128]{2,1,0:T(8,128)(2,1)} %bitcast.16), calls=%async_computation.4 | async-start | bytes 1048576 | tf_op jit(solution)/shard_map/all_to_all | solution.py:325
  105.9 1.6 collective-permute-start.7
  107.5 3.1 %collective-permute-start.1 = (bf16[384,128]{1,0:T(8,128)(2,1)S(1)}, bf16[384,128]{1,0:T(8,128)(2,1)S(1)}, u32[]{:S(2)}, u32[]{:S(2)}) collective-permute-start(bf16[384,128]{1,0:T(8,128)(2,1)S(1)} %get-tuple-element.19.refs_0_), channel_id=1, source_target_pairs={{0,7},{1,0},{2,1},{3,2},{4,3},{5,4},{6,5},{7,6},{8,15},{9,8},{10,9... | collective-permute-start | bytes 294920 | tf_op jit(solution)/shard_map/ppermute | solution.py:278
  110.6 2.6 %collective-permute-done.7.swapped_ref = bf16[384,128]{1,0:T(8,128)(2,1)S(1)} collective-permute-done((bf16[384,128]{1,0:T(8,128)(2,1)S(1)}, bf16[384,128]{1,0:T(8,128)(2,1)S(1)}, u32[]{:S(2)}, u32[]{:S(2)}) %collective-permute-start.7) | collective-permute-done | bytes 98336 | tf_op jit(solution)/shard_map/ppermute | solution.py:324
  113.2 7.1 %collective-permute-done.1.refs_1_.refs_2_ = bf16[384,128]{1,0:T(8,128)(2,1)S(1)} collective-permute-done((bf16[384,128]{1,0:T(8,128)(2,1)S(1)}, bf16[384,128]{1,0:T(8,128)(2,1)S(1)}, u32[]{:S(2)}, u32[]{:S(2)}) %collective-permute-start.1) | collective-permute-done | bytes 98336 | tf_op jit(solution)/shard_map/ppermute | solution.py:278
  124.1 2.9 %collective-permute-start.9 = (bf16[640,128]{1,0:T(8,128)(2,1)S(1)}, bf16[640,128]{1,0:T(8,128)(2,1)S(1)}, u32[]{:S(2)}, u32[]{:S(2)}) collective-permute-start(bf16[640,128]{1,0:T(8,128)(2,1)S(1)} %shard_map.82.refs_8_), channel_id=1, source_target_pairs={{0,7},{1,0},{2,1},{3,2},{4,3},{5,4},{6,5},{7,6},{8,15},{9,8},{10,9... | collective-permute-start | bytes 491528 | tf_op jit(solution)/shard_map/ppermute | solution.py:278
  126.9 4.0 %collective-permute-done.8.refs_9_ = bf16[640,128]{1,0:T(8,128)(2,1)S(1)} collective-permute-done((bf16[640,128]{1,0:T(8,128)(2,1)S(1)}, bf16[640,128]{1,0:T(8,128)(2,1)S(1)}, u32[]{:S(2)}, u32[]{:S(2)}) %collective-permute-start.8) | collective-permute-done | bytes 163872 | tf_op jit(solution)/shard_map/ppermute | solution.py:275
  131.0 3.2 %collective-permute-start.11 = (bf16[640,128]{1,0:T(8,128)(2,1)S(1)}, bf16[640,128]{1,0:T(8,128)(2,1)S(1)}, u32[]{:S(2)}, u32[]{:S(2)}) collective-permute-start(bf16[640,128]{1,0:T(8,128)(2,1)S(1)} %collective-permute-done.9.refs_10_), channel_id=1, source_target_pairs={{0,7},{1,0},{2,1},{3,2},{4,3},{5,4},{6,5},{7,6},{8,15},{9,8},{10,9... | collective-permute-start | bytes 491528 | tf_op jit(solution)/shard_map/ppermute | solution.py:278
  134.2 3.3 %collective-permute-done.10.refs_11_ = bf16[640,128]{1,0:T(8,128)(2,1)S(1)} collective-permute-done((bf16[640,128]{1,0:T(8,128)(2,1)S(1)}, bf16[640,128]{1,0:T(8,128)(2,1)S(1)}, u32[]{:S(2)}, u32[]{:S(2)}) %collective-permute-start.10) | collective-permute-done | bytes 163872 | tf_op jit(solution)/shard_map/ppermute | solution.py:275
  137.5 3.3 %collective-permute-start.3 = (bf16[384,128]{1,0:T(8,128)(2,1)S(1)}, bf16[384,128]{1,0:T(8,128)(2,1)S(1)}, u32[]{:S(2)}, u32[]{:S(2)}) collective-permute-start(bf16[384,128]{1,0:T(8,128)(2,1)S(1)} %collective-permute-done.1.refs_1_.refs_2_), channel_id=1, source_target_pairs={{0,7},{1,0},{2,1},{3,2},{4,3},{5,4},{6,5},{7,6},{8,15},{9,8},{10,9... | collective-permute-start | bytes 294920 | tf_op jit(solution)/shard_map/ppermute | solution.py:278
  140.8 4.3 %collective-permute-done.2.refs_3_ = bf16[384,128]{1,0:T(8,128)(2,1)S(1)} collective-permute-done((bf16[384,128]{1,0:T(8,128)(2,1)S(1)}, bf16[384,128]{1,0:T(8,128)(2,1)S(1)}, u32[]{:S(2)}, u32[]{:S(2)}) %collective-permute-start.2) | collective-permute-done | bytes 98336 | tf_op jit(solution)/shard_map/ppermute | solution.py:275
  145.1 3.2 %collective-permute-start.13 = (bf16[640,128]{1,0:T(8,128)(2,1)S(1)}, bf16[640,128]{1,0:T(8,128)(2,1)S(1)}, u32[]{:S(2)}, u32[]{:S(2)}) collective-permute-start(bf16[640,128]{1,0:T(8,128)(2,1)S(1)} %collective-permute-done.11.refs_12_), channel_id=1, source_target_pairs={{0,7},{1,0},{2,1},{3,2},{4,3},{5,4},{6,5},{7,6},{8,15},{9,8},{10,9... | collective-permute-start | bytes 491528 | tf_op jit(solution)/shard_map/ppermute | solution.py:278
  148.3 3.2 %collective-permute-start.5 = (bf16[384,128]{1,0:T(8,128)(2,1)S(1)}, bf16[384,128]{1,0:T(8,128)(2,1)S(1)}, u32[]{:S(2)}, u32[]{:S(2)}) collective-permute-start(bf16[384,128]{1,0:T(8,128)(2,1)S(1)} %collective-permute-done.3.refs_4_), channel_id=1, source_target_pairs={{0,7},{1,0},{2,1},{3,2},{4,3},{5,4},{6,5},{7,6},{8,15},{9,8},{10,9... | collective-permute-start | bytes 294920 | tf_op jit(solution)/shard_map/ppermute | solution.py:278
  151.6 2.2 %collective-permute-done.5.refs_6_ = bf16[384,128]{1,0:T(8,128)(2,1)S(1)} collective-permute-done((bf16[384,128]{1,0:T(8,128)(2,1)S(1)}, bf16[384,128]{1,0:T(8,128)(2,1)S(1)}, u32[]{:S(2)}, u32[]{:S(2)}) %collective-permute-start.5) | collective-permute-done | bytes 98336 | tf_op jit(solution)/shard_map/ppermute | solution.py:278
  153.8 3.6 %collective-permute-done.6.refs_7_ = bf16[384,128]{1,0:T(8,128)(2,1)S(1)} collective-permute-done((bf16[384,128]{1,0:T(8,128)(2,1)S(1)}, bf16[384,128]{1,0:T(8,128)(2,1)S(1)}, u32[]{:S(2)}, u32[]{:S(2)}) %collective-permute-start.6) | collective-permute-done | bytes 98336 | tf_op jit(solution)/shard_map/ppermute | solution.py:275
  157.4 2.4 %shard_map.83 = (f32[2,128,3072]{2,1,0:T(8,128)}, f32[2,64,2048]{2,1,0:T(8,128)}) custom-call(f32[2,128,3072]{2,1,0:T(8,128)S(1)} %copy-done.2, bf16[384,128]{1,0:T(8,128)(2,1)S(1)} %get-tuple-element.19.refs_0_, bf16[384,128]{1,0:T(8,128)(2,1)S(1)} %collective-permute-done.refs_0_.refs_1_, bf16[384,128]{1,0:T(8,128)(2,1)S(1)} %collective-permute-done.1.refs_1_.refs_2_, ...), custom_call_target="tpu_custom_call" | custom-call | bytes 9437184 | tf_op jit(solution)/shard_map/pallas_call | solution.py:250
  (39 shorter events, 8.6 us)
Async XLA Ops:
  0.6 27.8 %copy-start = (bf16[4,512,1024]{2,1,0:T(8,128)(2,1)S(1)}, bf16[4,512,1024]{2,1,0:T(8,128)(2,1)}, u32[]{:S(2)}) copy-start(bf16[4,512,1024]{2,1,0:T(8,128)(2,1)} %constant.2.clone.t_ref) | copy-start | bytes 12582916
  0.6 2.0 %copy-start.1 = (f32[2,128,3072]{2,1,0:T(8,128)S(1)}, f32[2,128,3072]{2,1,0:T(8,128)}, u32[]{:S(2)}) copy-start(f32[2,128,3072]{2,1,0:T(8,128)} %spec_ref.3) | copy-start | bytes 9437188
  3.5 25.0 %copy-start.4 = (f32[2,64,2048]{2,1,0:T(8,128)S(1)}, f32[2,64,2048]{2,1,0:T(8,128)}, u32[]{:S(2)}) copy-start(f32[2,64,2048]{2,1,0:T(8,128)} %pupil_ref.1) | copy-start | bytes 3145732
  3.5 25.0 %copy-start.7 = (s32[8]{0:T(128)S(1)}, s32[8]{0:T(128)}, u32[]{:S(2)}) copy-start(s32[8]{0:T(128)} %row_ref.5) | copy-start | bytes 100
  28.5 18.3 %copy-start.6 = (f32[1,64,2048]{2,1,0:T(8,128)S(1)}, f32[1,64,2048]{2,1,0:T(8,128)}, u32[]{:S(2)}) copy-start(f32[1,64,2048]{2,1,0:T(8,128)} %intensity_ref.1) | copy-start | bytes 1572868
  65.5 38.0 %copy-start.9 = (s32[8]{0:T(128)S(1)}, s32[8]{0:T(128)}, u32[]{:S(2)}) copy-start(s32[8]{0:T(128)} %col_ref.3) | copy-start | bytes 100
  68.2 31.1 %copy-start.5 = (bf16[2048,128]{1,0:T(8,128)(2,1)}, bf16[2048,128]{1,0:T(8,128)(2,1)S(1)}, u32[]{:S(2)}) copy-start(bf16[2048,128]{1,0:T(8,128)(2,1)S(1)} %get-tuple-element.20) | copy-start | bytes 1572868
  68.2 89.2 %copy-start.2 = (f32[2,128,3072]{2,1,0:T(8,128)S(1)}, f32[2,128,3072]{2,1,0:T(8,128)}, u32[]{:S(2)}) copy-start(f32[2,128,3072]{2,1,0:T(8,128)} %spec_ref.3) | copy-start | bytes 9437188
  99.3 23.2 %all-to-all-start.4 = ((bf16[8,256,128]{2,1,0:T(8,128)(2,1)}), bf16[8,256,128]{2,1,0:T(8,128)(2,1)}, u32[]{:S(2)}, u32[]{:S(2)}) async-start(bf16[8,256,128]{2,1,0:T(8,128)(2,1)} %bitcast.16), calls=%async_computation.4 | async-start | bytes 1048576 | tf_op jit(solution)/shard_map/all_to_all | solution.py:325
  105.9 7.3 %collective-permute-start.7 = (bf16[384,128]{1,0:T(8,128)(2,1)S(1)}, bf16[384,128]{1,0:T(8,128)(2,1)S(1)}, u32[]{:S(2)}, u32[]{:S(2)}) collective-permute-start(bf16[384,128]{1,0:T(8,128)(2,1)S(1)} %get-tuple-element.21), channel_id=1, source_target_pairs={{0,128},{8,136},{16,144},{24,152},{32,160},{40,168},{48,176},{56,1... | collective-permute-start | bytes 294920 | tf_op jit(solution)/shard_map/ppermute | solution.py:324
  107.5 12.8 %collective-permute-start.1 = (bf16[384,128]{1,0:T(8,128)(2,1)S(1)}, bf16[384,128]{1,0:T(8,128)(2,1)S(1)}, u32[]{:S(2)}, u32[]{:S(2)}) collective-permute-start(bf16[384,128]{1,0:T(8,128)(2,1)S(1)} %get-tuple-element.19.refs_0_), channel_id=1, source_target_pairs={{0,7},{1,0},{2,1},{3,2},{4,3},{5,4},{6,5},{7,6},{8,15},{9,8},{10,9... | collective-permute-start | bytes 294920 | tf_op jit(solution)/shard_map/ppermute | solution.py:278
  110.6 10.6 %collective-permute-start = (bf16[384,128]{1,0:T(8,128)(2,1)S(1)}, bf16[384,128]{1,0:T(8,128)(2,1)S(1)}, u32[]{:S(2)}, u32[]{:S(2)}) collective-permute-start(bf16[384,128]{1,0:T(8,128)(2,1)S(1)} %get-tuple-element.19.refs_0_), channel_id=1, source_target_pairs={{0,1},{1,2},{2,3},{3,4},{4,5},{5,6},{6,7},{7,0},{8,9},{9,10},{10,1... | collective-permute-start | bytes 294920 | tf_op jit(solution)/shard_map/ppermute | solution.py:275
  123.6 7.4 %collective-permute-start.8 = (bf16[640,128]{1,0:T(8,128)(2,1)S(1)}, bf16[640,128]{1,0:T(8,128)(2,1)S(1)}, u32[]{:S(2)}, u32[]{:S(2)}) collective-permute-start(bf16[640,128]{1,0:T(8,128)(2,1)S(1)} %shard_map.82.refs_8_), channel_id=1, source_target_pairs={{0,1},{1,2},{2,3},{3,4},{4,5},{5,6},{6,7},{7,0},{8,9},{9,10},{10,1... | collective-permute-start | bytes 491528 | tf_op jit(solution)/shard_map/ppermute | solution.py:275
  124.1 6.9 %collective-permute-start.9 = (bf16[640,128]{1,0:T(8,128)(2,1)S(1)}, bf16[640,128]{1,0:T(8,128)(2,1)S(1)}, u32[]{:S(2)}, u32[]{:S(2)}) collective-permute-start(bf16[640,128]{1,0:T(8,128)(2,1)S(1)} %shard_map.82.refs_8_), channel_id=1, source_target_pairs={{0,7},{1,0},{2,1},{3,2},{4,3},{5,4},{6,5},{7,6},{8,15},{9,8},{10,9... | collective-permute-start | bytes 491528 | tf_op jit(solution)/shard_map/ppermute | solution.py:278
  131.0 6.5 %collective-permute-start.10 = (bf16[640,128]{1,0:T(8,128)(2,1)S(1)}, bf16[640,128]{1,0:T(8,128)(2,1)S(1)}, u32[]{:S(2)}, u32[]{:S(2)}) collective-permute-start(bf16[640,128]{1,0:T(8,128)(2,1)S(1)} %collective-permute-done.8.refs_9_), channel_id=1, source_target_pairs={{0,1},{1,2},{2,3},{3,4},{4,5},{5,6},{6,7},{7,0},{8,9},{9,10},{10,1... | collective-permute-start | bytes 491528 | tf_op jit(solution)/shard_map/ppermute | solution.py:275
  131.0 14.1 %collective-permute-start.11 = (bf16[640,128]{1,0:T(8,128)(2,1)S(1)}, bf16[640,128]{1,0:T(8,128)(2,1)S(1)}, u32[]{:S(2)}, u32[]{:S(2)}) collective-permute-start(bf16[640,128]{1,0:T(8,128)(2,1)S(1)} %collective-permute-done.9.refs_10_), channel_id=1, source_target_pairs={{0,7},{1,0},{2,1},{3,2},{4,3},{5,4},{6,5},{7,6},{8,15},{9,8},{10,9... | collective-permute-start | bytes 491528 | tf_op jit(solution)/shard_map/ppermute | solution.py:278
  137.5 10.8 %collective-permute-start.12 = (bf16[640,128]{1,0:T(8,128)(2,1)S(1)}, bf16[640,128]{1,0:T(8,128)(2,1)S(1)}, u32[]{:S(2)}, u32[]{:S(2)}) collective-permute-start(bf16[640,128]{1,0:T(8,128)(2,1)S(1)} %collective-permute-done.10.refs_11_), channel_id=1, source_target_pairs={{0,1},{1,2},{2,3},{3,4},{4,5},{5,6},{6,7},{7,0},{8,9},{9,10},{10,1... | collective-permute-start | bytes 491528 | tf_op jit(solution)/shard_map/ppermute | solution.py:275
  137.5 7.6 %collective-permute-start.2 = (bf16[384,128]{1,0:T(8,128)(2,1)S(1)}, bf16[384,128]{1,0:T(8,128)(2,1)S(1)}, u32[]{:S(2)}, u32[]{:S(2)}) collective-permute-start(bf16[384,128]{1,0:T(8,128)(2,1)S(1)} %collective-permute-done.refs_0_.refs_1_), channel_id=1, source_target_pairs={{0,1},{1,2},{2,3},{3,4},{4,5},{5,6},{6,7},{7,0},{8,9},{9,10},{10,1... | collective-permute-start | bytes 294920 | tf_op jit(solution)/shard_map/ppermute | solution.py:275
  137.5 10.8 %collective-permute-start.3 = (bf16[384,128]{1,0:T(8,128)(2,1)S(1)}, bf16[384,128]{1,0:T(8,128)(2,1)S(1)}, u32[]{:S(2)}, u32[]{:S(2)}) collective-permute-start(bf16[384,128]{1,0:T(8,128)(2,1)S(1)} %collective-permute-done.1.refs_1_.refs_2_), channel_id=1, source_target_pairs={{0,7},{1,0},{2,1},{3,2},{4,3},{5,4},{6,5},{7,6},{8,15},{9,8},{10,9... | collective-permute-start | bytes 294920 | tf_op jit(solution)/shard_map/ppermute | solution.py:278
  145.1 6.5 %collective-permute-start.4 = (bf16[384,128]{1,0:T(8,128)(2,1)S(1)}, bf16[384,128]{1,0:T(8,128)(2,1)S(1)}, u32[]{:S(2)}, u32[]{:S(2)}) collective-permute-start(bf16[384,128]{1,0:T(8,128)(2,1)S(1)} %collective-permute-done.2.refs_3_), channel_id=1, source_target_pairs={{0,1},{1,2},{2,3},{3,4},{4,5},{5,6},{6,7},{7,0},{8,9},{9,10},{10,1... | collective-permute-start | bytes 294920 | tf_op jit(solution)/shard_map/ppermute | solution.py:275
  145.1 12.3 %collective-permute-start.13 = (bf16[640,128]{1,0:T(8,128)(2,1)S(1)}, bf16[640,128]{1,0:T(8,128)(2,1)S(1)}, u32[]{:S(2)}, u32[]{:S(2)}) collective-permute-start(bf16[640,128]{1,0:T(8,128)(2,1)S(1)} %collective-permute-done.11.refs_12_), channel_id=1, source_target_pairs={{0,7},{1,0},{2,1},{3,2},{4,3},{5,4},{6,5},{7,6},{8,15},{9,8},{10,9... | collective-permute-start | bytes 491528 | tf_op jit(solution)/shard_map/ppermute | solution.py:278
  148.3 9.1 %collective-permute-start.14 = (bf16[640,128]{1,0:T(8,128)(2,1)S(1)}, bf16[640,128]{1,0:T(8,128)(2,1)S(1)}, u32[]{:S(2)}, u32[]{:S(2)}) collective-permute-start(bf16[640,128]{1,0:T(8,128)(2,1)S(1)} %collective-permute-done.12.refs_13_), channel_id=1, source_target_pairs={{0,1},{1,2},{2,3},{3,4},{4,5},{5,6},{6,7},{7,0},{8,9},{9,10},{10,1... | collective-permute-start | bytes 491528 | tf_op jit(solution)/shard_map/ppermute | solution.py:275
  148.3 5.4 %collective-permute-start.5 = (bf16[384,128]{1,0:T(8,128)(2,1)S(1)}, bf16[384,128]{1,0:T(8,128)(2,1)S(1)}, u32[]{:S(2)}, u32[]{:S(2)}) collective-permute-start(bf16[384,128]{1,0:T(8,128)(2,1)S(1)} %collective-permute-done.3.refs_4_), channel_id=1, source_target_pairs={{0,7},{1,0},{2,1},{3,2},{4,3},{5,4},{6,5},{7,6},{8,15},{9,8},{10,9... | collective-permute-start | bytes 294920 | tf_op jit(solution)/shard_map/ppermute | solution.py:278
  151.6 5.8 %collective-permute-start.6 = (bf16[384,128]{1,0:T(8,128)(2,1)S(1)}, bf16[384,128]{1,0:T(8,128)(2,1)S(1)}, u32[]{:S(2)}, u32[]{:S(2)}) collective-permute-start(bf16[384,128]{1,0:T(8,128)(2,1)S(1)} %collective-permute-done.4.refs_5_), channel_id=1, source_target_pairs={{0,1},{1,2},{2,3},{3,4},{4,5},{5,6},{6,7},{7,0},{8,9},{9,10},{10,1... | collective-permute-start | bytes 294920 | tf_op jit(solution)/shard_map/ppermute | solution.py:275
  (2 other events, 1.9 us)

commit v6 on v5

--- a/solution.py
+++ b/solution.py
@@ -222,25 +222,56 @@
 HOPS = (0, 1, -1, 2, -2, 3, -3, 4)
 
 
-def finish_kernel(spec_ref, *refs):
-    own, swapped, (new_ref, out_ref) = refs[:8], refs[8:16], refs[16:]
+def finish_kernel(hops, *refs):
+    n = len(hops)
+    spec_ref, own, rest = refs[0], refs[1 : n + 1], refs[n + 1 : 2 * n + 1]
+    new_ref, out_ref, sum_ref, turn_ref, sum_sem, turn_sem = refs[-6:]
     slab, led = lax.axis_index("slab"), lax.axis_index("led")
     upper = slab // 16
-    for hop, own_ref, swapped_ref in zip(HOPS, own, swapped):
+    copies = []
+    for i, hop in enumerate(hops):
         source = lax.rem(led - hop + 8, 8)
-        for half, ref in ((upper, own_ref), (1 - upper, swapped_ref)):
+        for part, half, ref in ((0, upper, own[i]), (1, 1 - upper, rest[i])):
             rows = pl.ds(pl.multiple_of(half * 64 + source * 8, 8), 8)
             for t in range(NC // 128):
                 x = ref[t * 16 : t * 16 + 16, :].astype(F32)
                 columns = slice(t * 128, t * 128 + 128)
-                new_ref[0, rows, columns] = spec_ref[0, rows, columns] + x[:8]
-                new_ref[1, rows, columns] = spec_ref[1, rows, columns] + x[8:]
+                sum_ref[2 * i + part, 0, :, columns] = spec_ref[0, rows, columns] + x[:8]
+                sum_ref[2 * i + part, 1, :, columns] = spec_ref[1, rows, columns] + x[8:]
+            copies.append(
+                pltpu.make_async_copy(sum_ref.at[2 * i + part], new_ref.at[:, rows, :], sum_sem.at[2 * i + part])
+            )
+            copies[-1].start()
         for t in range(2):
             start = NC // 8 + t * 128
-            x = swapped_ref[start : start + 128, :].astype(F32).T
-            columns = pl.ds(pl.multiple_of(source * 256 + t * 128, 128), 128)
-            out_ref[0, :, columns] = x[:BAND]
-            out_ref[1, :, columns] = x[BAND:]
+            x = rest[i][start : start + 128, :].astype(F32).T
+            turn_ref[i, 0, :, t * 128 : t * 128 + 128] = x[:BAND]
+            turn_ref[i, 1, :, t * 128 : t * 128 + 128] = x[BAND:]
+        columns = pl.ds(pl.multiple_of(source * 256, 256), 256)
+        copies.append(pltpu.make_async_copy(turn_ref.at[i], out_ref.at[:, :, columns], turn_sem.at[i]))
+        copies[-1].start()
+    for copy in copies:
+        copy.wait()
+
+
+def finish(hops, spectrum, own, rest, before=()):
+    n = len(hops)
+    shapes = [jax.ShapeDtypeStruct((2, 128, NC), F32), jax.ShapeDtypeStruct((2, BAND, W), F32)]
+    return pl.pallas_call(
+        functools.partial(finish_kernel, hops),
+        out_shape=shapes,
+        in_specs=[pl.BlockSpec(memory_space=VMEM)] * (2 * n + 1) + [pl.BlockSpec(memory_space=pl.ANY)] * len(before),
+        out_specs=[pl.BlockSpec(memory_space=pl.ANY)] * 2,
+        input_output_aliases={2 * n + 1 + i: i for i in range(len(before))},
+        scratch_shapes=[
+            VMEM((2 * n, 2, 8, NC), F32),
+            VMEM((n, 2, BAND, W // 8), F32),
+            pltpu.SemaphoreType.DMA((2 * n,)),
+            pltpu.SemaphoreType.DMA((n,)),
+        ],
+        compiler_params=pltpu.CompilerParams(vmem_limit_bytes=20 * MIB),
+        cost_estimate=pl.CostEstimate(flops=0, bytes_accessed=n * 2 * MIB, transcendentals=0),
+    )(spectrum, *own, *rest, *before)
 
 
 def call(kernel, outs, scalars, arrays, scratch=(), flops=0, limit=20 * MIB):
@@ -325,12 +356,9 @@
     grads = lax.all_to_all(gradient.reshape(8, W // 8, 128), "led", 0, 0).reshape(rows128)
     own_pieces = ring_gather(own)
     (rest,) = call(merge_kernel, [((piece + W // 8, 128), BF16)], [], [grads, swapped, *own_pieces[1:3]])
-    return call(
-        finish_kernel,
-        [((2, 128, NC), F32), ((2, BAND, W), F32)],
-        [],
-        [spectrum, *own_pieces, *ring_gather(rest)],
-    )
+    rest_pieces = ring_gather(rest)
+    near = finish(HOPS[:7], spectrum, own_pieces[:7], rest_pieces[:7])
+    return finish(HOPS[7:], spectrum, own_pieces[7:], rest_pieces[7:], near)
 
 
 def solution(mesh):

time: 160 us -> 159 us (level)
  waiting for transfers between devices: 29.4 us -> 27.3 us
    pallas_call x0 -> x2, Pallas kernels: none -> 2.96 us  [finish(): pl.pallas_call(functools.partial(finish_kernel, hops), out_shape=shapes,...]
    pallas_call x7 -> x6, Pallas kernels: 15.7 us -> 13.4 us  [call(): pl.pallas_call(kernel, out_shape=shapes, in_specs=[pl.BlockSpec(memory_sp...]
    ppermute x8, waiting for transfers between devices: 16.2 us -> 14 us  [ring_gather(): forward = lax.ppermute(forward, 'led', FORWARD)]
  transfers between devices with their start and end apart: 16 -> 16, of which waited for: 9 -> 9; matrix products, arithmetic and copies ran while one was open for 0% -> 0% of each run, Pallas kernels for 1% -> 2%
where the time goes in v6:
time: 159 us; the launch traced here: 158 us
  blocking collectives  84.9 us (53%)
  waiting for transfers between devices  27.3 us (17%)
  starting transfers between devices  25.2 us (16%)
  Pallas kernels  16.3 us (10%)
  local copies, waits for them, and re-layouts  3.92 us (2%)
    all_to_all x3, blocking collectives, turn_bands(): return lax.all_to_all(blocks, 'slab', 0, 0).reshape(-1, 128)  53.8 us
    all_to_all x1, blocking collectives, per_device(): lax.all_to_all(correction.reshape(256, 8, 128), ('slab', 'led'), 0, 0)  31 us
    ppermute x6, starting transfers between devices, ring_gather(): backward = lax.ppermute(backward, 'led', BACKWARD)  19 us
    ppermute x8, waiting for transfers between devices, ring_gather(): forward = lax.ppermute(forward, 'led', FORWARD)  14 us
    pallas_call x6, Pallas kernels, call(): pl.pallas_call(kernel, out_shape=shapes, in_specs=[pl.BlockSpec(memory_sp...  13.4 us
    ppermute x6, waiting for transfers between devices, ring_gather(): backward = lax.ppermute(backward, 'led', BACKWARD)  9.28 us
    all_to_all x1, starting transfers between devices, per_device(): lax.all_to_all(gradient.reshape(8, W // 8, 128), 'led', 0, 0)  4.15 us
    unnamed x20, local copies, waits for them, and re-layouts  3.92 us
  transfers between devices with their start and end apart: 16, of which 9 were waited for; matrix products, arithmetic and copies ran while one was open for 0% of the time, Pallas kernels for 2%

profile of v6, /device:TPU:2, one launch (start us, length us, event | category | flops | bytes accessed | tf_op | source)
XLA Modules:
  0.0 158.5 jit_solution(8129145132831277459)
XLA Ops:
  0.7 2.0 %copy-done.1 = f32[2,128,3072]{2,1,0:T(8,128)S(1)} copy-done((f32[2,128,3072]{2,1,0:T(8,128)S(1)}, f32[2,128,3072]{2,1,0:T(8,128)}, u32[]{:S(2)}) %copy-start.1) | copy-done | bytes 3145752
  4.9 23.5 %all_to_all.25 = bf16[32,128,128]{2,1,0:T(8,128)(2,1)S(1)} all-to-all(bf16[32,128,128]{2,1,0:T(8,128)(2,1)S(1)} %bitcast.11), channel_id=1, replica_groups=mesh['slab'=32,'led'=8] {'slab'}, dimensions={0} | all-to-all | bytes 2097152 | tf_op jit(solution)/shard_map/all_to_all | solution.py:295
  28.5 3.2 %shard_map.78 = (bf16[2048,128]{1,0:T(8,128)(2,1)S(1)}, bf16[2048,128]{1,0:T(8,128)(2,1)S(1)}, f32[2048,128]{1,0:T(8,128)S(1)}, f32[2048,128]{1,0:T(8,128)S(1)}) custom-call(s32[8]{0:T(128)S(1)} %copy-done.7, bf16[4096,128]{1,0:T(8,128)(2,1)S(1)} %bitcast.10, f32[2,64,2048]{2,1,0:T(8,128)S(1)} %copy-done.4, bf16[4,512,1024]{2,1,0:T(8,128)(2,1)S(1)} %copy-done), custom_call_target="tpu_custom_call" | custom-call | flops 536870912 | bytes 9437184 | tf_op jit(solution)/shard_map/pallas_call | solution.py:281
  31.8 15.1 %all_to_all.26 = bf16[32,64,128]{2,1,0:T(8,128)(2,1)S(1)} all-to-all(bf16[32,64,128]{2,1,0:T(8,128)(2,1)S(1)} %bitcast.18), channel_id=1, replica_groups=mesh['slab'=32,'led'=8] {'slab'}, dimensions={0} | all-to-all | bytes 1048576 | tf_op jit(solution)/shard_map/all_to_all | solution.py:295
  46.8 3.5 %shard_map.79 = bf16[2048,128]{1,0:T(8,128)(2,1)S(1)} custom-call(bf16[2048,128]{1,0:T(8,128)(2,1)S(1)} %bitcast.14, f32[1,64,2048]{2,1,0:T(8,128)S(1)} %copy-done.6, bf16[4,512,1024]{2,1,0:T(8,128)(2,1)S(1)} %copy-done), custom_call_target="tpu_custom_call" | custom-call | flops 1073741824 | bytes 5767168 | tf_op jit(solution)/shard_map/pallas_call | solution.py:281
  50.3 15.2 %all_to_all.27 = bf16[32,64,128]{2,1,0:T(8,128)(2,1)S(1)} all-to-all(bf16[32,64,128]{2,1,0:T(8,128)(2,1)S(1)} %bitcast.15), channel_id=1, replica_groups=mesh['slab'=32,'led'=8] {'slab'}, dimensions={0} | all-to-all | bytes 1048576 | tf_op jit(solution)/shard_map/all_to_all | solution.py:295
  65.5 2.7 %shard_map.80 = (bf16[2048,128]{1,0:T(8,128)(2,1)S(1)}, bf16[2048,128]{1,0:T(8,128)(2,1)S(1)}) custom-call(s32[8]{0:T(128)S(1)} %copy-done.7, bf16[2048,128]{1,0:T(8,128)(2,1)S(1)} %bitcast.13, bf16[2048,128]{1,0:T(8,128)(2,1)S(1)} %get-tuple-element.15.win_ref, f32[2048,128]{1,0:T(8,128)S(1)} %get-tuple-element.16.pr_ref, ...), custom_call_target="tpu_custom_call" | custom-call | flops 536870912 | bytes 8388608 | tf_op jit(solution)/shard_map/pallas_call | solution.py:281
  68.3 31.0 %all_to_all.28 = bf16[256,8,128]{2,1,0:T(8,128)(2,1)} all-to-all(bf16[256,8,128]{2,1,0:T(8,128)(2,1)S(1)} %bitcast.17), channel_id=1, replica_groups=mesh['slab'=32,'led'=8] {'slab','led'}, dimensions={0} | all-to-all | bytes 1048576 | tf_op jit(solution)/shard_map/all_to_all | solution.py:345
  99.3 4.2 %all-to-all-start.4 = ((bf16[8,256,128]{2,1,0:T(8,128)(2,1)}), bf16[8,256,128]{2,1,0:T(8,128)(2,1)}, u32[]{:S(2)}, u32[]{:S(2)}) async-start(bf16[8,256,128]{2,1,0:T(8,128)(2,1)} %bitcast.16), calls=%async_computation.4 | async-start | bytes 1048576 | tf_op jit(solution)/shard_map/all_to_all | solution.py:356
  105.9 1.6 collective-permute-start.4
  107.5 3.1 %collective-permute-start.5 = (bf16[384,128]{1,0:T(8,128)(2,1)S(1)}, bf16[384,128]{1,0:T(8,128)(2,1)S(1)}, u32[]{:S(2)}, u32[]{:S(2)}) collective-permute-start(bf16[384,128]{1,0:T(8,128)(2,1)S(1)} %get-tuple-element.21.refs_1_), channel_id=1, source_target_pairs={{0,7},{1,0},{2,1},{3,2},{4,3},{5,4},{6,5},{7,6},{8,15},{9,8},{10,9... | collective-permute-start | bytes 294920 | tf_op jit(solution)/shard_map/ppermute | solution.py:309
  110.6 2.6 %collective-permute-done.4.swapped_ref = bf16[384,128]{1,0:T(8,128)(2,1)S(1)} collective-permute-done((bf16[384,128]{1,0:T(8,128)(2,1)S(1)}, bf16[384,128]{1,0:T(8,128)(2,1)S(1)}, u32[]{:S(2)}, u32[]{:S(2)}) %collective-permute-start.4) | collective-permute-done | bytes 98336 | tf_op jit(solution)/shard_map/ppermute | solution.py:355
  113.2 7.1 %collective-permute-done.5.refs_1_.refs_3_ = bf16[384,128]{1,0:T(8,128)(2,1)S(1)} collective-permute-done((bf16[384,128]{1,0:T(8,128)(2,1)S(1)}, bf16[384,128]{1,0:T(8,128)(2,1)S(1)}, u32[]{:S(2)}, u32[]{:S(2)}) %collective-permute-start.5) | collective-permute-done | bytes 98336 | tf_op jit(solution)/shard_map/ppermute | solution.py:309
  124.1 2.9 %collective-permute-start.12 = (bf16[640,128]{1,0:T(8,128)(2,1)S(1)}, bf16[640,128]{1,0:T(8,128)(2,1)S(1)}, u32[]{:S(2)}, u32[]{:S(2)}) collective-permute-start(bf16[640,128]{1,0:T(8,128)(2,1)S(1)} %shard_map.82.refs_8_), channel_id=1, source_target_pairs={{0,7},{1,0},{2,1},{3,2},{4,3},{5,4},{6,5},{7,6},{8,15},{9,8},{10,9... | collective-permute-start | bytes 491528 | tf_op jit(solution)/shard_map/ppermute | solution.py:309
  127.0 4.0 %collective-permute-done.6.refs_9_ = bf16[640,128]{1,0:T(8,128)(2,1)S(1)} collective-permute-done((bf16[640,128]{1,0:T(8,128)(2,1)S(1)}, bf16[640,128]{1,0:T(8,128)(2,1)S(1)}, u32[]{:S(2)}, u32[]{:S(2)}) %collective-permute-start.6) | collective-permute-done | bytes 163872 | tf_op jit(solution)/shard_map/ppermute | solution.py:306
  131.0 3.2 %collective-permute-start.13 = (bf16[640,128]{1,0:T(8,128)(2,1)S(1)}, bf16[640,128]{1,0:T(8,128)(2,1)S(1)}, u32[]{:S(2)}, u32[]{:S(2)}) collective-permute-start(bf16[640,128]{1,0:T(8,128)(2,1)S(1)} %collective-permute-done.12.refs_10_), channel_id=1, source_target_pairs={{0,7},{1,0},{2,1},{3,2},{4,3},{5,4},{6,5},{7,6},{8,15},{9,8},{10,9... | collective-permute-start | bytes 491528 | tf_op jit(solution)/shard_map/ppermute | solution.py:309
  134.3 3.3 %collective-permute-done.7.refs_11_ = bf16[640,128]{1,0:T(8,128)(2,1)S(1)} collective-permute-done((bf16[640,128]{1,0:T(8,128)(2,1)S(1)}, bf16[640,128]{1,0:T(8,128)(2,1)S(1)}, u32[]{:S(2)}, u32[]{:S(2)}) %collective-permute-start.7) | collective-permute-done | bytes 163872 | tf_op jit(solution)/shard_map/ppermute | solution.py:306
  137.6 3.3 %collective-permute-start.10 = (bf16[384,128]{1,0:T(8,128)(2,1)S(1)}, bf16[384,128]{1,0:T(8,128)(2,1)S(1)}, u32[]{:S(2)}, u32[]{:S(2)}) collective-permute-start(bf16[384,128]{1,0:T(8,128)(2,1)S(1)} %collective-permute-done.5.refs_1_.refs_3_), channel_id=1, source_target_pairs={{0,7},{1,0},{2,1},{3,2},{4,3},{5,4},{6,5},{7,6},{8,15},{9,8},{10,9... | collective-permute-start | bytes 294920 | tf_op jit(solution)/shard_map/ppermute | solution.py:309
  140.8 4.3 %collective-permute-done.1.refs_4_ = bf16[384,128]{1,0:T(8,128)(2,1)S(1)} collective-permute-done((bf16[384,128]{1,0:T(8,128)(2,1)S(1)}, bf16[384,128]{1,0:T(8,128)(2,1)S(1)}, u32[]{:S(2)}, u32[]{:S(2)}) %collective-permute-start.1) | collective-permute-done | bytes 98336 | tf_op jit(solution)/shard_map/ppermute | solution.py:306
  145.1 3.2 %collective-permute-start.14 = (bf16[640,128]{1,0:T(8,128)(2,1)S(1)}, bf16[640,128]{1,0:T(8,128)(2,1)S(1)}, u32[]{:S(2)}, u32[]{:S(2)}) collective-permute-start(bf16[640,128]{1,0:T(8,128)(2,1)S(1)} %collective-permute-done.13.refs_12_), channel_id=1, source_target_pairs={{0,7},{1,0},{2,1},{3,2},{4,3},{5,4},{6,5},{7,6},{8,15},{9,8},{10,9... | collective-permute-start | bytes 491528 | tf_op jit(solution)/shard_map/ppermute | solution.py:309
  148.4 3.2 %collective-permute-start.11 = (bf16[384,128]{1,0:T(8,128)(2,1)S(1)}, bf16[384,128]{1,0:T(8,128)(2,1)S(1)}, u32[]{:S(2)}, u32[]{:S(2)}) collective-permute-start(bf16[384,128]{1,0:T(8,128)(2,1)S(1)} %collective-permute-done.10.refs_5_), channel_id=1, source_target_pairs={{0,7},{1,0},{2,1},{3,2},{4,3},{5,4},{6,5},{7,6},{8,15},{9,8},{10,9... | collective-permute-start | bytes 294920 | tf_op jit(solution)/shard_map/ppermute | solution.py:309
  151.6 2.2 %collective-permute-done.11.refs_7_ = bf16[384,128]{1,0:T(8,128)(2,1)S(1)} collective-permute-done((bf16[384,128]{1,0:T(8,128)(2,1)S(1)}, bf16[384,128]{1,0:T(8,128)(2,1)S(1)}, u32[]{:S(2)}, u32[]{:S(2)}) %collective-permute-start.11) | collective-permute-done | bytes 98336 | tf_op jit(solution)/shard_map/ppermute | solution.py:309
  153.8 2.1 %shard_map.83 = (f32[2,128,3072]{2,1,0:T(8,128)}, f32[2,64,2048]{2,1,0:T(8,128)}) custom-call(f32[2,128,3072]{2,1,0:T(8,128)S(1)} %copy-done.2, bf16[384,128]{1,0:T(8,128)(2,1)S(1)} %get-tuple-element.21.refs_1_, bf16[384,128]{1,0:T(8,128)(2,1)S(1)} %collective-permute-done.refs_0_.refs_2_, bf16[384,128]{1,0:T(8,128)(2,1)S(1)} %collective-permute-done.5.refs_1_.refs_3_, ...), custom_call_target="tpu_custom_call" | custom-call | bytes 14680064 | tf_op jit(solution)/shard_map/pallas_call | solution.py:260
  156.0 1.5 collective-permute-done.3.refs_1_
  (40 shorter events, 9.4 us)
Async XLA Ops:
  0.6 27.9 %copy-start = (bf16[4,512,1024]{2,1,0:T(8,128)(2,1)S(1)}, bf16[4,512,1024]{2,1,0:T(8,128)(2,1)}, u32[]{:S(2)}) copy-start(bf16[4,512,1024]{2,1,0:T(8,128)(2,1)} %constant.2.clone.t_ref) | copy-start | bytes 12582916
  0.6 2.0 %copy-start.1 = (f32[2,128,3072]{2,1,0:T(8,128)S(1)}, f32[2,128,3072]{2,1,0:T(8,128)}, u32[]{:S(2)}) copy-start(f32[2,128,3072]{2,1,0:T(8,128)} %refs_0_.3) | copy-start | bytes 9437188
  3.5 25.0 %copy-start.4 = (f32[2,64,2048]{2,1,0:T(8,128)S(1)}, f32[2,64,2048]{2,1,0:T(8,128)}, u32[]{:S(2)}) copy-start(f32[2,64,2048]{2,1,0:T(8,128)} %pupil_ref.1) | copy-start | bytes 3145732
  3.5 25.0 %copy-start.7 = (s32[8]{0:T(128)S(1)}, s32[8]{0:T(128)}, u32[]{:S(2)}) copy-start(s32[8]{0:T(128)} %row_ref.5) | copy-start | bytes 100
  28.5 18.3 %copy-start.6 = (f32[1,64,2048]{2,1,0:T(8,128)S(1)}, f32[1,64,2048]{2,1,0:T(8,128)}, u32[]{:S(2)}) copy-start(f32[1,64,2048]{2,1,0:T(8,128)} %intensity_ref.1) | copy-start | bytes 1572868
  65.5 37.9 %copy-start.9 = (s32[8]{0:T(128)S(1)}, s32[8]{0:T(128)}, u32[]{:S(2)}) copy-start(s32[8]{0:T(128)} %col_ref.3) | copy-start | bytes 100
  68.2 31.1 %copy-start.5 = (bf16[2048,128]{1,0:T(8,128)(2,1)}, bf16[2048,128]{1,0:T(8,128)(2,1)S(1)}, u32[]{:S(2)}) copy-start(bf16[2048,128]{1,0:T(8,128)(2,1)S(1)} %get-tuple-element.22) | copy-start | bytes 1572868
  68.3 85.6 %copy-start.2 = (f32[2,128,3072]{2,1,0:T(8,128)S(1)}, f32[2,128,3072]{2,1,0:T(8,128)}, u32[]{:S(2)}) copy-start(f32[2,128,3072]{2,1,0:T(8,128)} %refs_0_.3) | copy-start | bytes 9437188
  99.3 23.2 %all-to-all-start.4 = ((bf16[8,256,128]{2,1,0:T(8,128)(2,1)}), bf16[8,256,128]{2,1,0:T(8,128)(2,1)}, u32[]{:S(2)}, u32[]{:S(2)}) async-start(bf16[8,256,128]{2,1,0:T(8,128)(2,1)} %bitcast.16), calls=%async_computation.4 | async-start | bytes 1048576 | tf_op jit(solution)/shard_map/all_to_all | solution.py:356
  105.9 7.3 %collective-permute-start.4 = (bf16[384,128]{1,0:T(8,128)(2,1)S(1)}, bf16[384,128]{1,0:T(8,128)(2,1)S(1)}, u32[]{:S(2)}, u32[]{:S(2)}) collective-permute-start(bf16[384,128]{1,0:T(8,128)(2,1)S(1)} %get-tuple-element.23), channel_id=1, source_target_pairs={{0,128},{8,136},{16,144},{24,152},{32,160},{40,168},{48,176},{56,1... | collective-permute-start | bytes 294920 | tf_op jit(solution)/shard_map/ppermute | solution.py:355
  107.5 12.8 %collective-permute-start.5 = (bf16[384,128]{1,0:T(8,128)(2,1)S(1)}, bf16[384,128]{1,0:T(8,128)(2,1)S(1)}, u32[]{:S(2)}, u32[]{:S(2)}) collective-permute-start(bf16[384,128]{1,0:T(8,128)(2,1)S(1)} %get-tuple-element.21.refs_1_), channel_id=1, source_target_pairs={{0,7},{1,0},{2,1},{3,2},{4,3},{5,4},{6,5},{7,6},{8,15},{9,8},{10,9... | collective-permute-start | bytes 294920 | tf_op jit(solution)/shard_map/ppermute | solution.py:309
  110.6 10.6 %collective-permute-start = (bf16[384,128]{1,0:T(8,128)(2,1)S(1)}, bf16[384,128]{1,0:T(8,128)(2,1)S(1)}, u32[]{:S(2)}, u32[]{:S(2)}) collective-permute-start(bf16[384,128]{1,0:T(8,128)(2,1)S(1)} %get-tuple-element.21.refs_1_), channel_id=1, source_target_pairs={{0,1},{1,2},{2,3},{3,4},{4,5},{5,6},{6,7},{7,0},{8,9},{9,10},{10,1... | collective-permute-start | bytes 294920 | tf_op jit(solution)/shard_map/ppermute | solution.py:306
  123.7 7.4 %collective-permute-start.6 = (bf16[640,128]{1,0:T(8,128)(2,1)S(1)}, bf16[640,128]{1,0:T(8,128)(2,1)S(1)}, u32[]{:S(2)}, u32[]{:S(2)}) collective-permute-start(bf16[640,128]{1,0:T(8,128)(2,1)S(1)} %shard_map.82.refs_8_), channel_id=1, source_target_pairs={{0,1},{1,2},{2,3},{3,4},{4,5},{5,6},{6,7},{7,0},{8,9},{9,10},{10,1... | collective-permute-start | bytes 491528 | tf_op jit(solution)/shard_map/ppermute | solution.py:306
  124.1 6.9 %collective-permute-start.12 = (bf16[640,128]{1,0:T(8,128)(2,1)S(1)}, bf16[640,128]{1,0:T(8,128)(2,1)S(1)}, u32[]{:S(2)}, u32[]{:S(2)}) collective-permute-start(bf16[640,128]{1,0:T(8,128)(2,1)S(1)} %shard_map.82.refs_8_), channel_id=1, source_target_pairs={{0,7},{1,0},{2,1},{3,2},{4,3},{5,4},{6,5},{7,6},{8,15},{9,8},{10,9... | collective-permute-start | bytes 491528 | tf_op jit(solution)/shard_map/ppermute | solution.py:309
  131.0 6.5 %collective-permute-start.7 = (bf16[640,128]{1,0:T(8,128)(2,1)S(1)}, bf16[640,128]{1,0:T(8,128)(2,1)S(1)}, u32[]{:S(2)}, u32[]{:S(2)}) collective-permute-start(bf16[640,128]{1,0:T(8,128)(2,1)S(1)} %collective-permute-done.6.refs_9_), channel_id=1, source_target_pairs={{0,1},{1,2},{2,3},{3,4},{4,5},{5,6},{6,7},{7,0},{8,9},{9,10},{10,1... | collective-permute-start | bytes 491528 | tf_op jit(solution)/shard_map/ppermute | solution.py:306
  131.0 14.1 %collective-permute-start.13 = (bf16[640,128]{1,0:T(8,128)(2,1)S(1)}, bf16[640,128]{1,0:T(8,128)(2,1)S(1)}, u32[]{:S(2)}, u32[]{:S(2)}) collective-permute-start(bf16[640,128]{1,0:T(8,128)(2,1)S(1)} %collective-permute-done.12.refs_10_), channel_id=1, source_target_pairs={{0,7},{1,0},{2,1},{3,2},{4,3},{5,4},{6,5},{7,6},{8,15},{9,8},{10,9... | collective-permute-start | bytes 491528 | tf_op jit(solution)/shard_map/ppermute | solution.py:309
  137.6 10.8 %collective-permute-start.8 = (bf16[640,128]{1,0:T(8,128)(2,1)S(1)}, bf16[640,128]{1,0:T(8,128)(2,1)S(1)}, u32[]{:S(2)}, u32[]{:S(2)}) collective-permute-start(bf16[640,128]{1,0:T(8,128)(2,1)S(1)} %collective-permute-done.7.refs_11_), channel_id=1, source_target_pairs={{0,1},{1,2},{2,3},{3,4},{4,5},{5,6},{6,7},{7,0},{8,9},{9,10},{10,1... | collective-permute-start | bytes 491528 | tf_op jit(solution)/shard_map/ppermute | solution.py:306
  137.6 7.6 %collective-permute-start.1 = (bf16[384,128]{1,0:T(8,128)(2,1)S(1)}, bf16[384,128]{1,0:T(8,128)(2,1)S(1)}, u32[]{:S(2)}, u32[]{:S(2)}) collective-permute-start(bf16[384,128]{1,0:T(8,128)(2,1)S(1)} %collective-permute-done.refs_0_.refs_2_), channel_id=1, source_target_pairs={{0,1},{1,2},{2,3},{3,4},{4,5},{5,6},{6,7},{7,0},{8,9},{9,10},{10,1... | collective-permute-start | bytes 294920 | tf_op jit(solution)/shard_map/ppermute | solution.py:306
  137.6 10.8 %collective-permute-start.10 = (bf16[384,128]{1,0:T(8,128)(2,1)S(1)}, bf16[384,128]{1,0:T(8,128)(2,1)S(1)}, u32[]{:S(2)}, u32[]{:S(2)}) collective-permute-start(bf16[384,128]{1,0:T(8,128)(2,1)S(1)} %collective-permute-done.5.refs_1_.refs_3_), channel_id=1, source_target_pairs={{0,7},{1,0},{2,1},{3,2},{4,3},{5,4},{6,5},{7,6},{8,15},{9,8},{10,9... | collective-permute-start | bytes 294920 | tf_op jit(solution)/shard_map/ppermute | solution.py:309
  145.1 6.5 %collective-permute-start.2 = (bf16[384,128]{1,0:T(8,128)(2,1)S(1)}, bf16[384,128]{1,0:T(8,128)(2,1)S(1)}, u32[]{:S(2)}, u32[]{:S(2)}) collective-permute-start(bf16[384,128]{1,0:T(8,128)(2,1)S(1)} %collective-permute-done.1.refs_4_), channel_id=1, source_target_pairs={{0,1},{1,2},{2,3},{3,4},{4,5},{5,6},{6,7},{7,0},{8,9},{9,10},{10,1... | collective-permute-start | bytes 294920 | tf_op jit(solution)/shard_map/ppermute | solution.py:306
  145.1 8.7 %collective-permute-start.14 = (bf16[640,128]{1,0:T(8,128)(2,1)S(1)}, bf16[640,128]{1,0:T(8,128)(2,1)S(1)}, u32[]{:S(2)}, u32[]{:S(2)}) collective-permute-start(bf16[640,128]{1,0:T(8,128)(2,1)S(1)} %collective-permute-done.13.refs_12_), channel_id=1, source_target_pairs={{0,7},{1,0},{2,1},{3,2},{4,3},{5,4},{6,5},{7,6},{8,15},{9,8},{10,9... | collective-permute-start | bytes 491528 | tf_op jit(solution)/shard_map/ppermute | solution.py:309
  148.4 9.1 %collective-permute-start.9 = (bf16[640,128]{1,0:T(8,128)(2,1)S(1)}, bf16[640,128]{1,0:T(8,128)(2,1)S(1)}, u32[]{:S(2)}, u32[]{:S(2)}) collective-permute-start(bf16[640,128]{1,0:T(8,128)(2,1)S(1)} %collective-permute-done.8.refs_13_), channel_id=1, source_target_pairs={{0,1},{1,2},{2,3},{3,4},{4,5},{5,6},{6,7},{7,0},{8,9},{9,10},{10,1... | collective-permute-start | bytes 491528 | tf_op jit(solution)/shard_map/ppermute | solution.py:306
  148.4 5.4 %collective-permute-start.11 = (bf16[384,128]{1,0:T(8,128)(2,1)S(1)}, bf16[384,128]{1,0:T(8,128)(2,1)S(1)}, u32[]{:S(2)}, u32[]{:S(2)}) collective-permute-start(bf16[384,128]{1,0:T(8,128)(2,1)S(1)} %collective-permute-done.10.refs_5_), channel_id=1, source_target_pairs={{0,7},{1,0},{2,1},{3,2},{4,3},{5,4},{6,5},{7,6},{8,15},{9,8},{10,9... | collective-permute-start | bytes 294920 | tf_op jit(solution)/shard_map/ppermute | solution.py:309
  151.6 5.8 %collective-permute-start.3 = (bf16[384,128]{1,0:T(8,128)(2,1)S(1)}, bf16[384,128]{1,0:T(8,128)(2,1)S(1)}, u32[]{:S(2)}, u32[]{:S(2)}) collective-permute-start(bf16[384,128]{1,0:T(8,128)(2,1)S(1)} %collective-permute-done.2.refs_6_), channel_id=1, source_target_pairs={{0,1},{1,2},{2,3},{3,4},{4,5},{5,6},{6,7},{7,0},{8,9},{9,10},{10,1... | collective-permute-start | bytes 294920 | tf_op jit(solution)/shard_map/ppermute | solution.py:306
  (2 other events, 1.9 us)

commit v7 on v6

--- a/solution.py
+++ b/solution.py
@@ -299,15 +299,17 @@
 BACKWARD = [(i, (i - 1) % 8) for i in range(8)]
 
 
-def ring_gather(piece):
-    forward = backward = piece
+def ring_gather(piece, before=None):
+    up = down = piece
     found = [piece]
     for hop in range(1, 5):
-        forward = lax.ppermute(forward, "led", FORWARD)
-        found.append(forward)
+        if before is not None and hop == 2:
+            up, down = lax.optimization_barrier((up, down, *before[3:5]))[:2]
+        up = lax.ppermute(up, "led", FORWARD)
+        found.append(up)
         if hop < 4:
-            backward = lax.ppermute(backward, "led", BACKWARD)
-            found.append(backward)
+            down = lax.ppermute(down, "led", BACKWARD)
+            found.append(down)
     return found
 
 
@@ -356,7 +358,7 @@
     grads = lax.all_to_all(gradient.reshape(8, W // 8, 128), "led", 0, 0).reshape(rows128)
     own_pieces = ring_gather(own)
     (rest,) = call(merge_kernel, [((piece + W // 8, 128), BF16)], [], [grads, swapped, *own_pieces[1:3]])
-    rest_pieces = ring_gather(rest)
+    rest_pieces = ring_gather(rest, own_pieces)
     near = finish(HOPS[:7], spectrum, own_pieces[:7], rest_pieces[:7])
     return finish(HOPS[7:], spectrum, own_pieces[7:], rest_pieces[7:], near)
 

time: 159 us -> 158 us (level)
  starting transfers between devices: 25.2 us -> 22.7 us
    ppermute x14, starting transfers between devices: 19.4 us -> 17 us  [the longest x6 15.2 us: ring_gather(): down = lax.ppermute(down, 'led', BACKWARD)]
  transfers between devices with their start and end apart: 16 -> 16, of which waited for: 9 -> 10; matrix products, arithmetic and copies ran while one was open for 0% -> 0% of each run, Pallas kernels for 2% -> 2%
where the time goes in v7:
time: 158 us; the launch traced here: 157 us
  blocking collectives  84.9 us (54%)
  waiting for transfers between devices  27.9 us (18%)
  starting transfers between devices  22.7 us (14%)
  Pallas kernels  16.3 us (10%)
  local copies, waits for them, and re-layouts  3.92 us (2%)
    all_to_all x3, blocking collectives, turn_bands(): return lax.all_to_all(blocks, 'slab', 0, 0).reshape(-1, 128)  53.8 us
    all_to_all x1, blocking collectives, per_device(): lax.all_to_all(correction.reshape(256, 8, 128), ('slab', 'led'), 0, 0)  31 us
    ppermute x6, starting transfers between devices, ring_gather(): down = lax.ppermute(down, 'led', BACKWARD)  15.2 us
    ppermute x6, waiting for transfers between devices, ring_gather(): down = lax.ppermute(down, 'led', BACKWARD)  13.4 us
    pallas_call x6, Pallas kernels, call(): pl.pallas_call(kernel, out_shape=shapes, in_specs=[pl.BlockSpec(memory_sp...  13.4 us
    ppermute x8, waiting for transfers between devices, ring_gather(): up = lax.ppermute(up, 'led', FORWARD)  10.6 us
    all_to_all x1, starting transfers between devices, per_device(): lax.all_to_all(gradient.reshape(8, W // 8, 128), 'led', 0, 0)  4.15 us
    unnamed x20, local copies, waits for them, and re-layouts  3.92 us
  transfers between devices with their start and end apart: 16, of which 10 were waited for; matrix products, arithmetic and copies ran while one was open for 0% of the time, Pallas kernels for 2%

profile of v7, /device:TPU:2, one launch (start us, length us, event | category | flops | bytes accessed | tf_op | source)
XLA Modules:
  0.0 156.7 jit_solution(3449326925316302391)
XLA Ops:
  0.7 2.0 %copy-done.1 = f32[2,128,3072]{2,1,0:T(8,128)S(1)} copy-done((f32[2,128,3072]{2,1,0:T(8,128)S(1)}, f32[2,128,3072]{2,1,0:T(8,128)}, u32[]{:S(2)}) %copy-start.1) | copy-done | bytes 3145752
  4.9 23.5 %all_to_all.25 = bf16[32,128,128]{2,1,0:T(8,128)(2,1)S(1)} all-to-all(bf16[32,128,128]{2,1,0:T(8,128)(2,1)S(1)} %bitcast.11), channel_id=1, replica_groups=mesh['slab'=32,'led'=8] {'slab'}, dimensions={0} | all-to-all | bytes 2097152 | tf_op jit(solution)/shard_map/all_to_all | solution.py:295
  28.5 3.2 %shard_map.78 = (bf16[2048,128]{1,0:T(8,128)(2,1)S(1)}, bf16[2048,128]{1,0:T(8,128)(2,1)S(1)}, f32[2048,128]{1,0:T(8,128)S(1)}, f32[2048,128]{1,0:T(8,128)S(1)}) custom-call(s32[8]{0:T(128)S(1)} %copy-done.7, bf16[4096,128]{1,0:T(8,128)(2,1)S(1)} %bitcast.10, f32[2,64,2048]{2,1,0:T(8,128)S(1)} %copy-done.4, bf16[4,512,1024]{2,1,0:T(8,128)(2,1)S(1)} %copy-done), custom_call_target="tpu_custom_call" | custom-call | flops 536870912 | bytes 9437184 | tf_op jit(solution)/shard_map/pallas_call | solution.py:281
  31.7 15.1 %all_to_all.26 = bf16[32,64,128]{2,1,0:T(8,128)(2,1)S(1)} all-to-all(bf16[32,64,128]{2,1,0:T(8,128)(2,1)S(1)} %bitcast.18), channel_id=1, replica_groups=mesh['slab'=32,'led'=8] {'slab'}, dimensions={0} | all-to-all | bytes 1048576 | tf_op jit(solution)/shard_map/all_to_all | solution.py:295
  46.8 3.5 %shard_map.79 = bf16[2048,128]{1,0:T(8,128)(2,1)S(1)} custom-call(bf16[2048,128]{1,0:T(8,128)(2,1)S(1)} %bitcast.14, f32[1,64,2048]{2,1,0:T(8,128)S(1)} %copy-done.6, bf16[4,512,1024]{2,1,0:T(8,128)(2,1)S(1)} %copy-done), custom_call_target="tpu_custom_call" | custom-call | flops 1073741824 | bytes 5767168 | tf_op jit(solution)/shard_map/pallas_call | solution.py:281
  50.3 15.2 %all_to_all.27 = bf16[32,64,128]{2,1,0:T(8,128)(2,1)S(1)} all-to-all(bf16[32,64,128]{2,1,0:T(8,128)(2,1)S(1)} %bitcast.15), channel_id=1, replica_groups=mesh['slab'=32,'led'=8] {'slab'}, dimensions={0} | all-to-all | bytes 1048576 | tf_op jit(solution)/shard_map/all_to_all | solution.py:295
  65.5 2.7 %shard_map.80 = (bf16[2048,128]{1,0:T(8,128)(2,1)S(1)}, bf16[2048,128]{1,0:T(8,128)(2,1)S(1)}) custom-call(s32[8]{0:T(128)S(1)} %copy-done.7, bf16[2048,128]{1,0:T(8,128)(2,1)S(1)} %bitcast.13, bf16[2048,128]{1,0:T(8,128)(2,1)S(1)} %get-tuple-element.17.win_ref, f32[2048,128]{1,0:T(8,128)S(1)} %get-tuple-element.18.pr_ref, ...), custom_call_target="tpu_custom_call" | custom-call | flops 536870912 | bytes 8388608 | tf_op jit(solution)/shard_map/pallas_call | solution.py:281
  68.2 31.0 %all_to_all.28 = bf16[256,8,128]{2,1,0:T(8,128)(2,1)} all-to-all(bf16[256,8,128]{2,1,0:T(8,128)(2,1)S(1)} %bitcast.17), channel_id=1, replica_groups=mesh['slab'=32,'led'=8] {'slab','led'}, dimensions={0} | all-to-all | bytes 1048576 | tf_op jit(solution)/shard_map/all_to_all | solution.py:347
  99.3 4.2 %all-to-all-start.4 = ((bf16[8,256,128]{2,1,0:T(8,128)(2,1)}), bf16[8,256,128]{2,1,0:T(8,128)(2,1)}, u32[]{:S(2)}, u32[]{:S(2)}) async-start(bf16[8,256,128]{2,1,0:T(8,128)(2,1)} %bitcast.16), calls=%async_computation.4 | async-start | bytes 1048576 | tf_op jit(solution)/shard_map/all_to_all | solution.py:358
  105.9 1.6 %collective-permute-start.4 = (bf16[384,128]{1,0:T(8,128)(2,1)S(1)}, bf16[384,128]{1,0:T(8,128)(2,1)S(1)}, u32[]{:S(2)}, u32[]{:S(2)}) collective-permute-start(bf16[384,128]{1,0:T(8,128)(2,1)S(1)} %get-tuple-element.25), channel_id=1, source_target_pairs={{0,128},{8,136},{16,144},{24,152},{32,160},{40,168},{48,176},{56,1... | collective-permute-start | bytes 294920 | tf_op jit(solution)/shard_map/ppermute | solution.py:357
  107.5 3.1 %collective-permute-start.5 = (bf16[384,128]{1,0:T(8,128)(2,1)S(1)}, bf16[384,128]{1,0:T(8,128)(2,1)S(1)}, u32[]{:S(2)}, u32[]{:S(2)}) collective-permute-start(bf16[384,128]{1,0:T(8,128)(2,1)S(1)} %get-tuple-element.23.refs_1_), channel_id=1, source_target_pairs={{0,7},{1,0},{2,1},{3,2},{4,3},{5,4},{6,5},{7,6},{8,15},{9,8},{10,9... | collective-permute-start | bytes 294920 | tf_op jit(solution)/shard_map/ppermute | solution.py:311
  110.6 2.6 %collective-permute-done.4.swapped_ref = bf16[384,128]{1,0:T(8,128)(2,1)S(1)} collective-permute-done((bf16[384,128]{1,0:T(8,128)(2,1)S(1)}, bf16[384,128]{1,0:T(8,128)(2,1)S(1)}, u32[]{:S(2)}, u32[]{:S(2)}) %collective-permute-start.4) | collective-permute-done | bytes 98336 | tf_op jit(solution)/shard_map/ppermute | solution.py:357
  113.2 7.1 %collective-permute-done.5.refs_1_.refs_3_ = bf16[384,128]{1,0:T(8,128)(2,1)S(1)} collective-permute-done((bf16[384,128]{1,0:T(8,128)(2,1)S(1)}, bf16[384,128]{1,0:T(8,128)(2,1)S(1)}, u32[]{:S(2)}, u32[]{:S(2)}) %collective-permute-start.5) | collective-permute-done | bytes 98336 | tf_op jit(solution)/shard_map/ppermute | solution.py:311
  125.8 1.8 %collective-permute-start.8 = (bf16[384,128]{1,0:T(8,128)(2,1)S(1)}, bf16[384,128]{1,0:T(8,128)(2,1)S(1)}, u32[]{:S(2)}, u32[]{:S(2)}) collective-permute-start(bf16[384,128]{1,0:T(8,128)(2,1)S(1)} %collective-permute-done.5.refs_1_.refs_3_), channel_id=1, source_target_pairs={{0,7},{1,0},{2,1},{3,2},{4,3},{5,4},{6,5},{7,6},{8,15},{9,8},{10,9... | collective-permute-start | bytes 294920 | tf_op jit(solution)/shard_map/ppermute | solution.py:311
  127.8 4.1 %collective-permute-done.8.refs_5_ = bf16[384,128]{1,0:T(8,128)(2,1)S(1)} collective-permute-done((bf16[384,128]{1,0:T(8,128)(2,1)S(1)}, bf16[384,128]{1,0:T(8,128)(2,1)S(1)}, u32[]{:S(2)}, u32[]{:S(2)}) %collective-permute-start.8) | collective-permute-done | bytes 98336 | tf_op jit(solution)/shard_map/ppermute | solution.py:311
  131.9 1.6 %collective-permute-done.1.refs_4_ = bf16[384,128]{1,0:T(8,128)(2,1)S(1)} collective-permute-done((bf16[384,128]{1,0:T(8,128)(2,1)S(1)}, bf16[384,128]{1,0:T(8,128)(2,1)S(1)}, u32[]{:S(2)}, u32[]{:S(2)}) %collective-permute-start.1) | collective-permute-done | bytes 98336 | tf_op jit(solution)/shard_map/ppermute | solution.py:308
  133.7 3.1 %collective-permute-start.13 = (bf16[640,128]{1,0:T(8,128)(2,1)S(1)}, bf16[640,128]{1,0:T(8,128)(2,1)S(1)}, u32[]{:S(2)}, u32[]{:S(2)}) collective-permute-start(bf16[640,128]{1,0:T(8,128)(2,1)S(1)} %collective-permute-done.7.refs_10_), channel_id=1, source_target_pairs={{0,7},{1,0},{2,1},{3,2},{4,3},{5,4},{6,5},{7,6},{8,15},{9,8},{10,9... | collective-permute-start | bytes 491528 | tf_op jit(solution)/shard_map/ppermute | solution.py:311
  136.8 3.3 %collective-permute-done.9.refs_11_ = bf16[640,128]{1,0:T(8,128)(2,1)S(1)} collective-permute-done((bf16[640,128]{1,0:T(8,128)(2,1)S(1)}, bf16[640,128]{1,0:T(8,128)(2,1)S(1)}, u32[]{:S(2)}, u32[]{:S(2)}) %collective-permute-start.9) | collective-permute-done | bytes 163872 | tf_op jit(solution)/shard_map/ppermute | solution.py:308
  140.1 3.3 %collective-permute-start.14 = (bf16[640,128]{1,0:T(8,128)(2,1)S(1)}, bf16[640,128]{1,0:T(8,128)(2,1)S(1)}, u32[]{:S(2)}, u32[]{:S(2)}) collective-permute-start(bf16[640,128]{1,0:T(8,128)(2,1)S(1)} %collective-permute-done.13.refs_12_), channel_id=1, source_target_pairs={{0,7},{1,0},{2,1},{3,2},{4,3},{5,4},{6,5},{7,6},{8,15},{9,8},{10,9... | collective-permute-start | bytes 491528 | tf_op jit(solution)/shard_map/ppermute | solution.py:311
  143.4 3.3 %collective-permute-done.10.refs_13_ = bf16[640,128]{1,0:T(8,128)(2,1)S(1)} collective-permute-done((bf16[640,128]{1,0:T(8,128)(2,1)S(1)}, bf16[640,128]{1,0:T(8,128)(2,1)S(1)}, u32[]{:S(2)}, u32[]{:S(2)}) %collective-permute-start.10) | collective-permute-done | bytes 163872 | tf_op jit(solution)/shard_map/ppermute | solution.py:308
  146.6 3.2 %collective-permute-start.12 = (bf16[384,128]{1,0:T(8,128)(2,1)S(1)}, bf16[384,128]{1,0:T(8,128)(2,1)S(1)}, u32[]{:S(2)}, u32[]{:S(2)}) collective-permute-start(bf16[384,128]{1,0:T(8,128)(2,1)S(1)} %collective-permute-done.8.refs_5_), channel_id=1, source_target_pairs={{0,7},{1,0},{2,1},{3,2},{4,3},{5,4},{6,5},{7,6},{8,15},{9,8},{10,9... | collective-permute-start | bytes 294920 | tf_op jit(solution)/shard_map/ppermute | solution.py:311
  149.9 2.2 %collective-permute-done.12.refs_7_ = bf16[384,128]{1,0:T(8,128)(2,1)S(1)} collective-permute-done((bf16[384,128]{1,0:T(8,128)(2,1)S(1)}, bf16[384,128]{1,0:T(8,128)(2,1)S(1)}, u32[]{:S(2)}, u32[]{:S(2)}) %collective-permute-start.12) | collective-permute-done | bytes 98336 | tf_op jit(solution)/shard_map/ppermute | solution.py:311
  152.1 2.1 %shard_map.83 = (f32[2,128,3072]{2,1,0:T(8,128)}, f32[2,64,2048]{2,1,0:T(8,128)}) custom-call(f32[2,128,3072]{2,1,0:T(8,128)S(1)} %copy-done.2, bf16[384,128]{1,0:T(8,128)(2,1)S(1)} %get-tuple-element.23.refs_1_, bf16[384,128]{1,0:T(8,128)(2,1)S(1)} %collective-permute-done.refs_0_.refs_2_, bf16[384,128]{1,0:T(8,128)(2,1)S(1)} %collective-permute-done.5.refs_1_.refs_3_, ...), custom_call_target="tpu_custom_call" | custom-call | bytes 14680064 | tf_op jit(solution)/shard_map/pallas_call | solution.py:260
  154.2 1.5 collective-permute-done.3.refs_1_
  (40 shorter events, 11.4 us)
Async XLA Ops:
  0.6 27.8 %copy-start = (bf16[4,512,1024]{2,1,0:T(8,128)(2,1)S(1)}, bf16[4,512,1024]{2,1,0:T(8,128)(2,1)}, u32[]{:S(2)}) copy-start(bf16[4,512,1024]{2,1,0:T(8,128)(2,1)} %constant.2.clone.t_ref) | copy-start | bytes 12582916
  0.6 2.0 %copy-start.1 = (f32[2,128,3072]{2,1,0:T(8,128)S(1)}, f32[2,128,3072]{2,1,0:T(8,128)}, u32[]{:S(2)}) copy-start(f32[2,128,3072]{2,1,0:T(8,128)} %refs_0_.3) | copy-start | bytes 9437188
  3.5 25.0 %copy-start.4 = (f32[2,64,2048]{2,1,0:T(8,128)S(1)}, f32[2,64,2048]{2,1,0:T(8,128)}, u32[]{:S(2)}) copy-start(f32[2,64,2048]{2,1,0:T(8,128)} %pupil_ref.1) | copy-start | bytes 3145732
  3.5 25.0 %copy-start.7 = (s32[8]{0:T(128)S(1)}, s32[8]{0:T(128)}, u32[]{:S(2)}) copy-start(s32[8]{0:T(128)} %row_ref.5) | copy-start | bytes 100
  28.5 18.3 %copy-start.6 = (f32[1,64,2048]{2,1,0:T(8,128)S(1)}, f32[1,64,2048]{2,1,0:T(8,128)}, u32[]{:S(2)}) copy-start(f32[1,64,2048]{2,1,0:T(8,128)} %intensity_ref.1) | copy-start | bytes 1572868
  65.5 37.9 %copy-start.9 = (s32[8]{0:T(128)S(1)}, s32[8]{0:T(128)}, u32[]{:S(2)}) copy-start(s32[8]{0:T(128)} %col_ref.3) | copy-start | bytes 100
  68.2 31.1 %copy-start.5 = (bf16[2048,128]{1,0:T(8,128)(2,1)}, bf16[2048,128]{1,0:T(8,128)(2,1)S(1)}, u32[]{:S(2)}) copy-start(bf16[2048,128]{1,0:T(8,128)(2,1)S(1)} %get-tuple-element.24) | copy-start | bytes 1572868
  68.2 83.9 %copy-start.2 = (f32[2,128,3072]{2,1,0:T(8,128)S(1)}, f32[2,128,3072]{2,1,0:T(8,128)}, u32[]{:S(2)}) copy-start(f32[2,128,3072]{2,1,0:T(8,128)} %refs_0_.3) | copy-start | bytes 9437188
  99.3 23.2 %all-to-all-start.4 = ((bf16[8,256,128]{2,1,0:T(8,128)(2,1)}), bf16[8,256,128]{2,1,0:T(8,128)(2,1)}, u32[]{:S(2)}, u32[]{:S(2)}) async-start(bf16[8,256,128]{2,1,0:T(8,128)(2,1)} %bitcast.16), calls=%async_computation.4 | async-start | bytes 1048576 | tf_op jit(solution)/shard_map/all_to_all | solution.py:358
  105.9 7.3 %collective-permute-start.4 = (bf16[384,128]{1,0:T(8,128)(2,1)S(1)}, bf16[384,128]{1,0:T(8,128)(2,1)S(1)}, u32[]{:S(2)}, u32[]{:S(2)}) collective-permute-start(bf16[384,128]{1,0:T(8,128)(2,1)S(1)} %get-tuple-element.25), channel_id=1, source_target_pairs={{0,128},{8,136},{16,144},{24,152},{32,160},{40,168},{48,176},{56,1... | collective-permute-start | bytes 294920 | tf_op jit(solution)/shard_map/ppermute | solution.py:357
  107.5 12.8 %collective-permute-start.5 = (bf16[384,128]{1,0:T(8,128)(2,1)S(1)}, bf16[384,128]{1,0:T(8,128)(2,1)S(1)}, u32[]{:S(2)}, u32[]{:S(2)}) collective-permute-start(bf16[384,128]{1,0:T(8,128)(2,1)S(1)} %get-tuple-element.23.refs_1_), channel_id=1, source_target_pairs={{0,7},{1,0},{2,1},{3,2},{4,3},{5,4},{6,5},{7,6},{8,15},{9,8},{10,9... | collective-permute-start | bytes 294920 | tf_op jit(solution)/shard_map/ppermute | solution.py:311
  110.6 10.6 %collective-permute-start = (bf16[384,128]{1,0:T(8,128)(2,1)S(1)}, bf16[384,128]{1,0:T(8,128)(2,1)S(1)}, u32[]{:S(2)}, u32[]{:S(2)}) collective-permute-start(bf16[384,128]{1,0:T(8,128)(2,1)S(1)} %get-tuple-element.23.refs_1_), channel_id=1, source_target_pairs={{0,1},{1,2},{2,3},{3,4},{4,5},{5,6},{6,7},{7,0},{8,9},{9,10},{10,1... | collective-permute-start | bytes 294920 | tf_op jit(solution)/shard_map/ppermute | solution.py:308
  123.7 9.9 %collective-permute-start.7 = (bf16[640,128]{1,0:T(8,128)(2,1)S(1)}, bf16[640,128]{1,0:T(8,128)(2,1)S(1)}, u32[]{:S(2)}, u32[]{:S(2)}) collective-permute-start(bf16[640,128]{1,0:T(8,128)(2,1)S(1)} %shard_map.82.refs_8_), channel_id=1, source_target_pairs={{0,7},{1,0},{2,1},{3,2},{4,3},{5,4},{6,5},{7,6},{8,15},{9,8},{10,9... | collective-permute-start | bytes 491528 | tf_op jit(solution)/shard_map/ppermute | solution.py:311
  124.3 9.3 %collective-permute-start.6 = (bf16[640,128]{1,0:T(8,128)(2,1)S(1)}, bf16[640,128]{1,0:T(8,128)(2,1)S(1)}, u32[]{:S(2)}, u32[]{:S(2)}) collective-permute-start(bf16[640,128]{1,0:T(8,128)(2,1)S(1)} %shard_map.82.refs_8_), channel_id=1, source_target_pairs={{0,1},{1,2},{2,3},{3,4},{4,5},{5,6},{6,7},{7,0},{8,9},{9,10},{10,1... | collective-permute-start | bytes 491528 | tf_op jit(solution)/shard_map/ppermute | solution.py:308
  125.8 6.1 %collective-permute-start.8 = (bf16[384,128]{1,0:T(8,128)(2,1)S(1)}, bf16[384,128]{1,0:T(8,128)(2,1)S(1)}, u32[]{:S(2)}, u32[]{:S(2)}) collective-permute-start(bf16[384,128]{1,0:T(8,128)(2,1)S(1)} %collective-permute-done.5.refs_1_.refs_3_), channel_id=1, source_target_pairs={{0,7},{1,0},{2,1},{3,2},{4,3},{5,4},{6,5},{7,6},{8,15},{9,8},{10,9... | collective-permute-start | bytes 294920 | tf_op jit(solution)/shard_map/ppermute | solution.py:311
  127.5 6.0 %collective-permute-start.1 = (bf16[384,128]{1,0:T(8,128)(2,1)S(1)}, bf16[384,128]{1,0:T(8,128)(2,1)S(1)}, u32[]{:S(2)}, u32[]{:S(2)}) collective-permute-start(bf16[384,128]{1,0:T(8,128)(2,1)S(1)} %collective-permute-done.refs_0_.refs_2_), channel_id=1, source_target_pairs={{0,1},{1,2},{2,3},{3,4},{4,5},{5,6},{6,7},{7,0},{8,9},{9,10},{10,1... | collective-permute-start | bytes 294920 | tf_op jit(solution)/shard_map/ppermute | solution.py:308
  133.6 6.5 %collective-permute-start.9 = (bf16[640,128]{1,0:T(8,128)(2,1)S(1)}, bf16[640,128]{1,0:T(8,128)(2,1)S(1)}, u32[]{:S(2)}, u32[]{:S(2)}) collective-permute-start(bf16[640,128]{1,0:T(8,128)(2,1)S(1)} %collective-permute-done.6.refs_9_), channel_id=1, source_target_pairs={{0,1},{1,2},{2,3},{3,4},{4,5},{5,6},{6,7},{7,0},{8,9},{9,10},{10,1... | collective-permute-start | bytes 491528 | tf_op jit(solution)/shard_map/ppermute | solution.py:308
  133.7 6.4 %collective-permute-start.13 = (bf16[640,128]{1,0:T(8,128)(2,1)S(1)}, bf16[640,128]{1,0:T(8,128)(2,1)S(1)}, u32[]{:S(2)}, u32[]{:S(2)}) collective-permute-start(bf16[640,128]{1,0:T(8,128)(2,1)S(1)} %collective-permute-done.7.refs_10_), channel_id=1, source_target_pairs={{0,7},{1,0},{2,1},{3,2},{4,3},{5,4},{6,5},{7,6},{8,15},{9,8},{10,9... | collective-permute-start | bytes 491528 | tf_op jit(solution)/shard_map/ppermute | solution.py:311
  140.1 6.5 %collective-permute-start.10 = (bf16[640,128]{1,0:T(8,128)(2,1)S(1)}, bf16[640,128]{1,0:T(8,128)(2,1)S(1)}, u32[]{:S(2)}, u32[]{:S(2)}) collective-permute-start(bf16[640,128]{1,0:T(8,128)(2,1)S(1)} %collective-permute-done.9.refs_11_), channel_id=1, source_target_pairs={{0,1},{1,2},{2,3},{3,4},{4,5},{5,6},{6,7},{7,0},{8,9},{9,10},{10,1... | collective-permute-start | bytes 491528 | tf_op jit(solution)/shard_map/ppermute | solution.py:308
  140.1 9.8 %collective-permute-start.2 = (bf16[384,128]{1,0:T(8,128)(2,1)S(1)}, bf16[384,128]{1,0:T(8,128)(2,1)S(1)}, u32[]{:S(2)}, u32[]{:S(2)}) collective-permute-start(bf16[384,128]{1,0:T(8,128)(2,1)S(1)} %collective-permute-done.1.refs_4_), channel_id=1, source_target_pairs={{0,1},{1,2},{2,3},{3,4},{4,5},{5,6},{6,7},{7,0},{8,9},{9,10},{10,1... | collective-permute-start | bytes 294920 | tf_op jit(solution)/shard_map/ppermute | solution.py:308
  140.1 12.0 %collective-permute-start.14 = (bf16[640,128]{1,0:T(8,128)(2,1)S(1)}, bf16[640,128]{1,0:T(8,128)(2,1)S(1)}, u32[]{:S(2)}, u32[]{:S(2)}) collective-permute-start(bf16[640,128]{1,0:T(8,128)(2,1)S(1)} %collective-permute-done.13.refs_12_), channel_id=1, source_target_pairs={{0,7},{1,0},{2,1},{3,2},{4,3},{5,4},{6,5},{7,6},{8,15},{9,8},{10,9... | collective-permute-start | bytes 491528 | tf_op jit(solution)/shard_map/ppermute | solution.py:311
  146.6 9.1 %collective-permute-start.11 = (bf16[640,128]{1,0:T(8,128)(2,1)S(1)}, bf16[640,128]{1,0:T(8,128)(2,1)S(1)}, u32[]{:S(2)}, u32[]{:S(2)}) collective-permute-start(bf16[640,128]{1,0:T(8,128)(2,1)S(1)} %collective-permute-done.10.refs_13_), channel_id=1, source_target_pairs={{0,1},{1,2},{2,3},{3,4},{4,5},{5,6},{6,7},{7,0},{8,9},{9,10},{10,1... | collective-permute-start | bytes 491528 | tf_op jit(solution)/shard_map/ppermute | solution.py:308
  146.6 5.4 %collective-permute-start.12 = (bf16[384,128]{1,0:T(8,128)(2,1)S(1)}, bf16[384,128]{1,0:T(8,128)(2,1)S(1)}, u32[]{:S(2)}, u32[]{:S(2)}) collective-permute-start(bf16[384,128]{1,0:T(8,128)(2,1)S(1)} %collective-permute-done.8.refs_5_), channel_id=1, source_target_pairs={{0,7},{1,0},{2,1},{3,2},{4,3},{5,4},{6,5},{7,6},{8,15},{9,8},{10,9... | collective-permute-start | bytes 294920 | tf_op jit(solution)/shard_map/ppermute | solution.py:311
  149.9 5.8 %collective-permute-start.3 = (bf16[384,128]{1,0:T(8,128)(2,1)S(1)}, bf16[384,128]{1,0:T(8,128)(2,1)S(1)}, u32[]{:S(2)}, u32[]{:S(2)}) collective-permute-start(bf16[384,128]{1,0:T(8,128)(2,1)S(1)} %collective-permute-done.2.refs_6_), channel_id=1, source_target_pairs={{0,1},{1,2},{2,3},{3,4},{4,5},{5,6},{6,7},{7,0},{8,9},{9,10},{10,1... | collective-permute-start | bytes 294920 | tf_op jit(solution)/shard_map/ppermute | solution.py:308
  (2 other events, 1.9 us)

commit v8 on v7

--- a/solution.py
+++ b/solution.py
@@ -22,16 +22,19 @@
 BF16 = jnp.bfloat16
 
 
-def table():
+def tables():
     rows = np.arange(QUARTER, dtype=np.int64)[:, None]
-    cols = np.arange(W, dtype=np.int64)[None, :]
-    phases = ((rows * cols) % W).astype(np.float32) * np.float32(2.0 * math.pi / W)
+    columns = 4 * np.arange(QUARTER, dtype=np.int64)[None, :]
+    phases = ((rows * columns) % W).astype(np.float32) * np.float32(2.0 * math.pi / W)
     factor = np.float32(1.0 / math.sqrt(W))
-    parts = []
-    for res in range(4):
-        part = phases[:, res::4]
-        parts.append(np.concatenate([np.cos(part) * factor, np.sin(part) * factor], 1))
-    return np.stack(parts).astype(jnp.bfloat16)
+    base = np.concatenate([np.cos(phases) * factor, np.sin(phases) * factor], 1).astype(jnp.bfloat16)
+    turns = []
+    for res in range(1, 4):
+        angle = rows * res * (2.0 * math.pi / W)
+        ones = np.ones((1, BAND))
+        low, high = np.concatenate([ones, 0 * ones], 1), np.concatenate([0 * ones, ones], 1)
+        turns.append([np.cos(angle) * (low + high), np.sin(angle) * (high - low)])
+    return base, np.array(turns, np.float32)
 
 
 def low_half(shape):
@@ -47,17 +50,28 @@
     return jnp.where(low_half(x.shape), -s, s)
 
 
-def dft(x_ref, t_ref, g_ref, sign, emit, chunk=64):
+def dft(x_ref, t_ref, w_ref, g_ref, sign, emit, chunk=64):
+    operands = []
     for res in range(4):
         x = x_ref[pl.ds(res, QUARTER, stride=4), :]
         ix = times_i(x)
         if sign < 0:
             ix = -ix
-        operand = jnp.concatenate([x.astype(BF16), ix.astype(BF16)], 0)
-        g_ref[res] = jnp.dot(t_ref[res], operand, preferred_element_type=F32)
+        operands.append(jnp.concatenate([x.astype(BF16), ix.astype(BF16)], 0))
+    for half in range(2):
+        operand = jnp.concatenate(operands[2 * half : 2 * half + 2], 1)
+        g_ref[:, half * 256 : half * 256 + 256] = jnp.dot(t_ref[...], operand, preferred_element_type=F32)
 
     for start in range(0, QUARTER, chunk):
-        g0, g1, g2, g3 = (g_ref[res, start : start + chunk, :] for res in range(4))
+        rows = slice(start, start + chunk)
+        g0 = g_ref[rows, :128]
+        turned = []
+        for res in range(1, 4):
+            g = g_ref[rows, res * 128 : res * 128 + 128]
+            imaginary = swap(g) * w_ref[res - 1, 1, rows, :]
+            g = g * w_ref[res - 1, 0, rows, :]
+            turned.append(g + imaginary if sign > 0 else g - imaginary)
+        g1, g2, g3 = turned
         h0, h1, h2 = g0 + g2, g0 - g2, g1 + g3
         h3 = times_i(g1 - g3)
         if sign < 0:
@@ -103,7 +117,7 @@
         out_ref[t * 256 + 128 : t * 256 + 256, :] = moved[:, 128:].astype(BF16)
 
 
-def first_kernel(row_ref, recv_ref, pupil_ref, t_ref, out_ref, win_ref, pr_ref, pi_ref, wide_ref, x_ref, g_ref):
+def first_kernel(row_ref, recv_ref, pupil_ref, t_ref, w_ref, out_ref, win_ref, pr_ref, pi_ref, wide_ref, x_ref, g_ref):
     row = row_ref[lax.axis_index("led")]
     base = jnp.minimum(row // 16 * 16, 2 * W - (W + 16))
     off = row - base
@@ -119,11 +133,11 @@
         w = wide_ref[pl.ds(off + start, 128), :]
         win_ref[rows, :] = w.astype(BF16)
         x_ref[rows, :] = (w * pr + swap(w) * pi).astype(BF16).astype(F32)
-    dft(x_ref, t_ref, g_ref, 1, store_rows(x_ref))
+    dft(x_ref, t_ref, w_ref, g_ref, 1, store_rows(x_ref))
     turn_blocks(x_ref, out_ref)
 
 
-def middle_kernel(recv_ref, intensity_ref, t_ref, out_ref, root_ref, x_ref, g_ref):
+def middle_kernel(recv_ref, intensity_ref, t_ref, w_ref, out_ref, root_ref, x_ref, g_ref):
     x_ref[...] = recv_ref[...].astype(F32)
     for start in range(0, W, 128):
         rows = slice(start, start + 128)
@@ -137,12 +151,12 @@
         scaling = root_ref[rows, :] / jnp.maximum(magnitude, AMPLITUDE_FLOOR)
         x_ref[rows, :] = (value * scaling).astype(BF16).astype(F32)
 
-    dft(x_ref, t_ref, g_ref, 1, replace)
-    dft(x_ref, t_ref, g_ref, -1, store_rows(x_ref))
+    dft(x_ref, t_ref, w_ref, g_ref, 1, replace)
+    dft(x_ref, t_ref, w_ref, g_ref, -1, store_rows(x_ref))
     turn_blocks(x_ref, out_ref)
 
 
-def last_kernel(row_ref, recv_ref, win_ref, pr_ref, pi_ref, t_ref, grad_ref, corr_ref, x_ref, c_ref, g_ref):
+def last_kernel(row_ref, recv_ref, win_ref, pr_ref, pi_ref, t_ref, w_ref, grad_ref, corr_ref, x_ref, c_ref, g_ref):
     row = row_ref[lax.axis_index("led")]
     x_ref[...] = recv_ref[...].astype(F32)
 
@@ -160,7 +174,7 @@
         grad_ref[rows, :] = (change * wr + cs * wi).astype(BF16)
         c_ref[pl.ds(row + start, size), :] = (change * pr - cs * pi) / (pr * pr + pi * pi + PUPIL_DAMPING)
 
-    dft(x_ref, t_ref, g_ref, -1, update)
+    dft(x_ref, t_ref, w_ref, g_ref, -1, update)
 
     for part in range(32):
         start = part * 64
@@ -314,7 +328,7 @@
 
 
 def per_device(spectrum, pupil, intensity, row_offsets, col_offsets):
-    tab = jnp.asarray(table())
+    base, turns = (jnp.asarray(x) for x in tables())
     rows128 = (W, 128)
     flops = 8 * QUARTER * 1024 * 128
 
@@ -322,26 +336,26 @@
         gather_kernel, [((2 * W, 128), BF16)], [col_offsets], [spectrum], [VMEM((2, 128, W + 128), BF16)]
     )
     arrived = turn_bands(outgoing)
-    scratch = [VMEM(rows128, F32), VMEM((4, QUARTER, 128), F32)]
+    scratch = [VMEM(rows128, F32), VMEM((QUARTER, 512), F32)]
     first, window, pr, pi = call(
         first_kernel,
         [(rows128, BF16), (rows128, BF16), (rows128, F32), (rows128, F32)],
         [row_offsets],
-        [arrived, pupil, tab],
+        [arrived, pupil, base, turns],
         [VMEM((W + 16, 128), F32)] + scratch,
         flops,
     )
     turned = turn_bands(first)
     (second,) = call(
-        middle_kernel, [(rows128, BF16)], [], [turned, intensity, tab], [VMEM(rows128, F32)] + scratch, 2 * flops
+        middle_kernel, [(rows128, BF16)], [], [turned, intensity, base, turns], [VMEM(rows128, F32)] + scratch, 2 * flops
     )
     returned = turn_bands(second)
     gradient, correction = call(
         last_kernel,
         [(rows128, BF16), (rows128, BF16)],
         [row_offsets],
-        [returned, window, pr, pi, tab],
-        [VMEM(rows128, F32), VMEM((2 * W, 128), F32), VMEM((4, QUARTER, 128), F32)],
+        [returned, window, pr, pi, base, turns],
+        [VMEM(rows128, F32), VMEM((2 * W, 128), F32), VMEM((QUARTER, 512), F32)],
         flops,
     )
     landed = lax.all_to_all(correction.reshape(256, 8, 128), ("slab", "led"), 0, 0).reshape(rows128)

time: 158 us -> 157 us (level)
    unnamed x20 -> x22, local copies, waits for them, and re-layouts: 3.92 us -> 3.61 us
where the time goes in v8:
time: 157 us; the launch traced here: 156 us
  blocking collectives  84.9 us (54%)
  waiting for transfers between devices  28.1 us (18%)
  starting transfers between devices  22.6 us (14%)
  Pallas kernels  16.1 us (10%)
  local copies, waits for them, and re-layouts  3.61 us (2%)
    all_to_all x3, blocking collectives, turn_bands(): return lax.all_to_all(blocks, 'slab', 0, 0).reshape(-1, 128)  53.8 us
    all_to_all x1, blocking collectives, per_device(): lax.all_to_all(correction.reshape(256, 8, 128), ('slab', 'led'), 0, 0)  31 us
    ppermute x6, starting transfers between devices, ring_gather(): down = lax.ppermute(down, 'led', BACKWARD)  15.2 us
    ppermute x6, waiting for transfers between devices, ring_gather(): down = lax.ppermute(down, 'led', BACKWARD)  13.6 us
    pallas_call x6, Pallas kernels, call(): pl.pallas_call(kernel, out_shape=shapes, in_specs=[pl.BlockSpec(memory_sp...  13.1 us
    ppermute x8, waiting for transfers between devices, ring_gather(): up = lax.ppermute(up, 'led', FORWARD)  10.6 us
    all_to_all x1, starting transfers between devices, per_device(): lax.all_to_all(gradient.reshape(8, W // 8, 128), 'led', 0, 0)  4.15 us
    unnamed x22, local copies, waits for them, and re-layouts  3.61 us
  transfers between devices with their start and end apart: 16, of which 10 were waited for; matrix products, arithmetic and copies ran while one was open for 0% of the time, Pallas kernels for 2%

profile of v8, /device:TPU:2, one launch (start us, length us, event | category | flops | bytes accessed | tf_op | source)
XLA Modules:
  0.0 156.1 jit_solution(2142291826719211683)
XLA Ops:
  0.6 1.9 %copy-done = f32[2,128,3072]{2,1,0:T(8,128)S(1)} copy-done((f32[2,128,3072]{2,1,0:T(8,128)S(1)}, f32[2,128,3072]{2,1,0:T(8,128)}, u32[]{:S(2)}) %copy-start) | copy-done | bytes 3145752
  4.6 23.5 %all_to_all.25 = bf16[32,128,128]{2,1,0:T(8,128)(2,1)S(1)} all-to-all(bf16[32,128,128]{2,1,0:T(8,128)(2,1)S(1)} %bitcast.11), channel_id=1, replica_groups=mesh['slab'=32,'led'=8] {'slab'}, dimensions={0} | all-to-all | bytes 2097152 | tf_op jit(solution)/shard_map/all_to_all | solution.py:309
  28.2 3.3 %shard_map.87 = (bf16[2048,128]{1,0:T(8,128)(2,1)S(1)}, bf16[2048,128]{1,0:T(8,128)(2,1)S(1)}, f32[2048,128]{1,0:T(8,128)S(1)}, f32[2048,128]{1,0:T(8,128)S(1)}) custom-call(s32[8]{0:T(128)S(1)} %copy-done.8, bf16[4096,128]{1,0:T(8,128)(2,1)S(1)} %bitcast.10, f32[2,64,2048]{2,1,0:T(8,128)S(1)} %copy-done.5, bf16[512,1024]{1,0:T(8,128)(2,1)S(1)} %copy-done.3, ...), custom_call_target="tpu_custom_call" | custom-call | flops 536870912 | bytes 7864320 | tf_op jit(solution)/shard_map/pallas_call | solution.py:295
  31.5 15.1 %all_to_all.26 = bf16[32,64,128]{2,1,0:T(8,128)(2,1)S(1)} all-to-all(bf16[32,64,128]{2,1,0:T(8,128)(2,1)S(1)} %bitcast.18), channel_id=1, replica_groups=mesh['slab'=32,'led'=8] {'slab'}, dimensions={0} | all-to-all | bytes 1048576 | tf_op jit(solution)/shard_map/all_to_all | solution.py:309
  46.5 3.4 %shard_map.88 = bf16[2048,128]{1,0:T(8,128)(2,1)S(1)} custom-call(bf16[2048,128]{1,0:T(8,128)(2,1)S(1)} %bitcast.14, f32[1,64,2048]{2,1,0:T(8,128)S(1)} %copy-done.7, bf16[512,1024]{1,0:T(8,128)(2,1)S(1)} %copy-done.3, f32[3,2,512,128]{3,2,1,0:T(8,128)S(1)} %copy-done.2), custom_call_target="tpu_custom_call" | custom-call | flops 1073741824 | bytes 4194304 | tf_op jit(solution)/shard_map/pallas_call | solution.py:295
  49.9 15.2 %all_to_all.27 = bf16[32,64,128]{2,1,0:T(8,128)(2,1)S(1)} all-to-all(bf16[32,64,128]{2,1,0:T(8,128)(2,1)S(1)} %bitcast.15), channel_id=1, replica_groups=mesh['slab'=32,'led'=8] {'slab'}, dimensions={0} | all-to-all | bytes 1048576 | tf_op jit(solution)/shard_map/all_to_all | solution.py:309
  65.2 2.5 %shard_map.89 = (bf16[2048,128]{1,0:T(8,128)(2,1)S(1)}, bf16[2048,128]{1,0:T(8,128)(2,1)S(1)}) custom-call(s32[8]{0:T(128)S(1)} %copy-done.8, bf16[2048,128]{1,0:T(8,128)(2,1)S(1)} %bitcast.12, bf16[2048,128]{1,0:T(8,128)(2,1)S(1)} %get-tuple-element.17.win_ref, f32[2048,128]{1,0:T(8,128)S(1)} %get-tuple-element.18.pr_ref, ...), custom_call_target="tpu_custom_call" | custom-call | flops 536870912 | bytes 6815744 | tf_op jit(solution)/shard_map/pallas_call | solution.py:295
  67.7 31.0 %all_to_all.28 = bf16[256,8,128]{2,1,0:T(8,128)(2,1)} all-to-all(bf16[256,8,128]{2,1,0:T(8,128)(2,1)S(1)} %bitcast.17), channel_id=1, replica_groups=mesh['slab'=32,'led'=8] {'slab','led'}, dimensions={0} | all-to-all | bytes 1048576 | tf_op jit(solution)/shard_map/all_to_all | solution.py:361
  98.7 4.1 %all-to-all-start.4 = ((bf16[8,256,128]{2,1,0:T(8,128)(2,1)}), bf16[8,256,128]{2,1,0:T(8,128)(2,1)}, u32[]{:S(2)}, u32[]{:S(2)}) async-start(bf16[8,256,128]{2,1,0:T(8,128)(2,1)} %bitcast.16), calls=%async_computation.4 | async-start | bytes 1048576 | tf_op jit(solution)/shard_map/all_to_all | solution.py:372
  106.7 3.1 %collective-permute-start.5 = (bf16[384,128]{1,0:T(8,128)(2,1)S(1)}, bf16[384,128]{1,0:T(8,128)(2,1)S(1)}, u32[]{:S(2)}, u32[]{:S(2)}) collective-permute-start(bf16[384,128]{1,0:T(8,128)(2,1)S(1)} %get-tuple-element.23.refs_1_), channel_id=1, source_target_pairs={{0,7},{1,0},{2,1},{3,2},{4,3},{5,4},{6,5},{7,6},{8,15},{9,8},{10,9... | collective-permute-start | bytes 294920 | tf_op jit(solution)/shard_map/ppermute | solution.py:325
  109.9 2.6 %collective-permute-done.4.swapped_ref = bf16[384,128]{1,0:T(8,128)(2,1)S(1)} collective-permute-done((bf16[384,128]{1,0:T(8,128)(2,1)S(1)}, bf16[384,128]{1,0:T(8,128)(2,1)S(1)}, u32[]{:S(2)}, u32[]{:S(2)}) %collective-permute-start.4) | collective-permute-done | bytes 98336 | tf_op jit(solution)/shard_map/ppermute | solution.py:371
  112.5 7.2 %collective-permute-done.5.refs_1_.refs_3_ = bf16[384,128]{1,0:T(8,128)(2,1)S(1)} collective-permute-done((bf16[384,128]{1,0:T(8,128)(2,1)S(1)}, bf16[384,128]{1,0:T(8,128)(2,1)S(1)}, u32[]{:S(2)}, u32[]{:S(2)}) %collective-permute-start.5) | collective-permute-done | bytes 98336 | tf_op jit(solution)/shard_map/ppermute | solution.py:325
  123.7 1.5 collective-permute-start.6
  125.2 1.8 %collective-permute-start.8 = (bf16[384,128]{1,0:T(8,128)(2,1)S(1)}, bf16[384,128]{1,0:T(8,128)(2,1)S(1)}, u32[]{:S(2)}, u32[]{:S(2)}) collective-permute-start(bf16[384,128]{1,0:T(8,128)(2,1)S(1)} %collective-permute-done.5.refs_1_.refs_3_), channel_id=1, source_target_pairs={{0,7},{1,0},{2,1},{3,2},{4,3},{5,4},{6,5},{7,6},{8,15},{9,8},{10,9... | collective-permute-start | bytes 294920 | tf_op jit(solution)/shard_map/ppermute | solution.py:325
  127.2 4.1 %collective-permute-done.8.refs_5_ = bf16[384,128]{1,0:T(8,128)(2,1)S(1)} collective-permute-done((bf16[384,128]{1,0:T(8,128)(2,1)S(1)}, bf16[384,128]{1,0:T(8,128)(2,1)S(1)}, u32[]{:S(2)}, u32[]{:S(2)}) %collective-permute-start.8) | collective-permute-done | bytes 98336 | tf_op jit(solution)/shard_map/ppermute | solution.py:325
  131.3 1.6 %collective-permute-done.1.refs_4_ = bf16[384,128]{1,0:T(8,128)(2,1)S(1)} collective-permute-done((bf16[384,128]{1,0:T(8,128)(2,1)S(1)}, bf16[384,128]{1,0:T(8,128)(2,1)S(1)}, u32[]{:S(2)}, u32[]{:S(2)}) %collective-permute-start.1) | collective-permute-done | bytes 98336 | tf_op jit(solution)/shard_map/ppermute | solution.py:322
  133.1 3.1 %collective-permute-start.13 = (bf16[640,128]{1,0:T(8,128)(2,1)S(1)}, bf16[640,128]{1,0:T(8,128)(2,1)S(1)}, u32[]{:S(2)}, u32[]{:S(2)}) collective-permute-start(bf16[640,128]{1,0:T(8,128)(2,1)S(1)} %collective-permute-done.7.refs_10_), channel_id=1, source_target_pairs={{0,7},{1,0},{2,1},{3,2},{4,3},{5,4},{6,5},{7,6},{8,15},{9,8},{10,9... | collective-permute-start | bytes 491528 | tf_op jit(solution)/shard_map/ppermute | solution.py:325
  136.2 3.3 %collective-permute-done.9.refs_11_ = bf16[640,128]{1,0:T(8,128)(2,1)S(1)} collective-permute-done((bf16[640,128]{1,0:T(8,128)(2,1)S(1)}, bf16[640,128]{1,0:T(8,128)(2,1)S(1)}, u32[]{:S(2)}, u32[]{:S(2)}) %collective-permute-start.9) | collective-permute-done | bytes 163872 | tf_op jit(solution)/shard_map/ppermute | solution.py:322
  139.5 3.3 %collective-permute-start.14 = (bf16[640,128]{1,0:T(8,128)(2,1)S(1)}, bf16[640,128]{1,0:T(8,128)(2,1)S(1)}, u32[]{:S(2)}, u32[]{:S(2)}) collective-permute-start(bf16[640,128]{1,0:T(8,128)(2,1)S(1)} %collective-permute-done.13.refs_12_), channel_id=1, source_target_pairs={{0,7},{1,0},{2,1},{3,2},{4,3},{5,4},{6,5},{7,6},{8,15},{9,8},{10,9... | collective-permute-start | bytes 491528 | tf_op jit(solution)/shard_map/ppermute | solution.py:325
  142.8 3.3 %collective-permute-done.10.refs_13_ = bf16[640,128]{1,0:T(8,128)(2,1)S(1)} collective-permute-done((bf16[640,128]{1,0:T(8,128)(2,1)S(1)}, bf16[640,128]{1,0:T(8,128)(2,1)S(1)}, u32[]{:S(2)}, u32[]{:S(2)}) %collective-permute-start.10) | collective-permute-done | bytes 163872 | tf_op jit(solution)/shard_map/ppermute | solution.py:322
  146.0 3.2 %collective-permute-start.12 = (bf16[384,128]{1,0:T(8,128)(2,1)S(1)}, bf16[384,128]{1,0:T(8,128)(2,1)S(1)}, u32[]{:S(2)}, u32[]{:S(2)}) collective-permute-start(bf16[384,128]{1,0:T(8,128)(2,1)S(1)} %collective-permute-done.8.refs_5_), channel_id=1, source_target_pairs={{0,7},{1,0},{2,1},{3,2},{4,3},{5,4},{6,5},{7,6},{8,15},{9,8},{10,9... | collective-permute-start | bytes 294920 | tf_op jit(solution)/shard_map/ppermute | solution.py:325
  149.3 2.2 %collective-permute-done.12.refs_7_ = bf16[384,128]{1,0:T(8,128)(2,1)S(1)} collective-permute-done((bf16[384,128]{1,0:T(8,128)(2,1)S(1)}, bf16[384,128]{1,0:T(8,128)(2,1)S(1)}, u32[]{:S(2)}, u32[]{:S(2)}) %collective-permute-start.12) | collective-permute-done | bytes 98336 | tf_op jit(solution)/shard_map/ppermute | solution.py:325
  151.5 2.1 %shard_map.92 = (f32[2,128,3072]{2,1,0:T(8,128)}, f32[2,64,2048]{2,1,0:T(8,128)}) custom-call(f32[2,128,3072]{2,1,0:T(8,128)S(1)} %copy-done.1, bf16[384,128]{1,0:T(8,128)(2,1)S(1)} %get-tuple-element.23.refs_1_, bf16[384,128]{1,0:T(8,128)(2,1)S(1)} %collective-permute-done.refs_0_.refs_2_, bf16[384,128]{1,0:T(8,128)(2,1)S(1)} %collective-permute-done.5.refs_1_.refs_3_, ...), custom_call_target="tpu_custom_call" | custom-call | bytes 14680064 | tf_op jit(solution)/shard_map/pallas_call | solution.py:274
  153.6 1.5 collective-permute-done.3.refs_1_
  (42 shorter events, 11.2 us)
Async XLA Ops:
  3.2 25.0 %copy-start.2 = (f32[3,2,512,128]{3,2,1,0:T(8,128)S(1)}, f32[3,2,512,128]{3,2,1,0:T(8,128)}, u32[]{:S(2)}) copy-start(f32[3,2,512,128]{3,2,1,0:T(8,128)} %constant.5.clone.w_ref) | copy-start | bytes 4718596
  3.2 25.0 %copy-start.3 = (bf16[512,1024]{1,0:T(8,128)(2,1)S(1)}, bf16[512,1024]{1,0:T(8,128)(2,1)}, u32[]{:S(2)}) copy-start(bf16[512,1024]{1,0:T(8,128)(2,1)} %constant.4.clone.t_ref) | copy-start | bytes 3145732
  3.2 25.0 %copy-start.5 = (f32[2,64,2048]{2,1,0:T(8,128)S(1)}, f32[2,64,2048]{2,1,0:T(8,128)}, u32[]{:S(2)}) copy-start(f32[2,64,2048]{2,1,0:T(8,128)} %pupil_ref.1) | copy-start | bytes 3145732
  3.2 25.0 %copy-start.8 = (s32[8]{0:T(128)S(1)}, s32[8]{0:T(128)}, u32[]{:S(2)}) copy-start(s32[8]{0:T(128)} %row_ref.5) | copy-start | bytes 100
  28.2 18.4 %copy-start.7 = (f32[1,64,2048]{2,1,0:T(8,128)S(1)}, f32[1,64,2048]{2,1,0:T(8,128)}, u32[]{:S(2)}) copy-start(f32[1,64,2048]{2,1,0:T(8,128)} %intensity_ref.1) | copy-start | bytes 1572868
  65.2 37.7 %copy-start.10 = (s32[8]{0:T(128)S(1)}, s32[8]{0:T(128)}, u32[]{:S(2)}) copy-start(s32[8]{0:T(128)} %col_ref.3) | copy-start | bytes 100
  67.7 31.1 %copy-start.6 = (bf16[2048,128]{1,0:T(8,128)(2,1)}, bf16[2048,128]{1,0:T(8,128)(2,1)S(1)}, u32[]{:S(2)}) copy-start(bf16[2048,128]{1,0:T(8,128)(2,1)S(1)} %get-tuple-element.24) | copy-start | bytes 1572868
  67.7 83.8 %copy-start.1 = (f32[2,128,3072]{2,1,0:T(8,128)S(1)}, f32[2,128,3072]{2,1,0:T(8,128)}, u32[]{:S(2)}) copy-start(f32[2,128,3072]{2,1,0:T(8,128)} %refs_0_.3) | copy-start | bytes 9437188
  98.7 23.2 %all-to-all-start.4 = ((bf16[8,256,128]{2,1,0:T(8,128)(2,1)}), bf16[8,256,128]{2,1,0:T(8,128)(2,1)}, u32[]{:S(2)}, u32[]{:S(2)}) async-start(bf16[8,256,128]{2,1,0:T(8,128)(2,1)} %bitcast.16), calls=%async_computation.4 | async-start | bytes 1048576 | tf_op jit(solution)/shard_map/all_to_all | solution.py:372
  105.3 7.1 %collective-permute-start.4 = (bf16[384,128]{1,0:T(8,128)(2,1)S(1)}, bf16[384,128]{1,0:T(8,128)(2,1)S(1)}, u32[]{:S(2)}, u32[]{:S(2)}) collective-permute-start(bf16[384,128]{1,0:T(8,128)(2,1)S(1)} %get-tuple-element.25), channel_id=1, source_target_pairs={{0,128},{8,136},{16,144},{24,152},{32,160},{40,168},{48,176},{56,1... | collective-permute-start | bytes 294920 | tf_op jit(solution)/shard_map/ppermute | solution.py:371
  106.7 13.0 %collective-permute-start.5 = (bf16[384,128]{1,0:T(8,128)(2,1)S(1)}, bf16[384,128]{1,0:T(8,128)(2,1)S(1)}, u32[]{:S(2)}, u32[]{:S(2)}) collective-permute-start(bf16[384,128]{1,0:T(8,128)(2,1)S(1)} %get-tuple-element.23.refs_1_), channel_id=1, source_target_pairs={{0,7},{1,0},{2,1},{3,2},{4,3},{5,4},{6,5},{7,6},{8,15},{9,8},{10,9... | collective-permute-start | bytes 294920 | tf_op jit(solution)/shard_map/ppermute | solution.py:325
  109.9 10.7 %collective-permute-start = (bf16[384,128]{1,0:T(8,128)(2,1)S(1)}, bf16[384,128]{1,0:T(8,128)(2,1)S(1)}, u32[]{:S(2)}, u32[]{:S(2)}) collective-permute-start(bf16[384,128]{1,0:T(8,128)(2,1)S(1)} %get-tuple-element.23.refs_1_), channel_id=1, source_target_pairs={{0,1},{1,2},{2,3},{3,4},{4,5},{5,6},{6,7},{7,0},{8,9},{9,10},{10,1... | collective-permute-start | bytes 294920 | tf_op jit(solution)/shard_map/ppermute | solution.py:322
  123.1 9.9 %collective-permute-start.7 = (bf16[640,128]{1,0:T(8,128)(2,1)S(1)}, bf16[640,128]{1,0:T(8,128)(2,1)S(1)}, u32[]{:S(2)}, u32[]{:S(2)}) collective-permute-start(bf16[640,128]{1,0:T(8,128)(2,1)S(1)} %shard_map.91.refs_8_), channel_id=1, source_target_pairs={{0,7},{1,0},{2,1},{3,2},{4,3},{5,4},{6,5},{7,6},{8,15},{9,8},{10,9... | collective-permute-start | bytes 491528 | tf_op jit(solution)/shard_map/ppermute | solution.py:325
  123.7 9.3 %collective-permute-start.6 = (bf16[640,128]{1,0:T(8,128)(2,1)S(1)}, bf16[640,128]{1,0:T(8,128)(2,1)S(1)}, u32[]{:S(2)}, u32[]{:S(2)}) collective-permute-start(bf16[640,128]{1,0:T(8,128)(2,1)S(1)} %shard_map.91.refs_8_), channel_id=1, source_target_pairs={{0,1},{1,2},{2,3},{3,4},{4,5},{5,6},{6,7},{7,0},{8,9},{9,10},{10,1... | collective-permute-start | bytes 491528 | tf_op jit(solution)/shard_map/ppermute | solution.py:322
  125.2 6.1 %collective-permute-start.8 = (bf16[384,128]{1,0:T(8,128)(2,1)S(1)}, bf16[384,128]{1,0:T(8,128)(2,1)S(1)}, u32[]{:S(2)}, u32[]{:S(2)}) collective-permute-start(bf16[384,128]{1,0:T(8,128)(2,1)S(1)} %collective-permute-done.5.refs_1_.refs_3_), channel_id=1, source_target_pairs={{0,7},{1,0},{2,1},{3,2},{4,3},{5,4},{6,5},{7,6},{8,15},{9,8},{10,9... | collective-permute-start | bytes 294920 | tf_op jit(solution)/shard_map/ppermute | solution.py:325
  127.0 6.0 %collective-permute-start.1 = (bf16[384,128]{1,0:T(8,128)(2,1)S(1)}, bf16[384,128]{1,0:T(8,128)(2,1)S(1)}, u32[]{:S(2)}, u32[]{:S(2)}) collective-permute-start(bf16[384,128]{1,0:T(8,128)(2,1)S(1)} %collective-permute-done.refs_0_.refs_2_), channel_id=1, source_target_pairs={{0,1},{1,2},{2,3},{3,4},{4,5},{5,6},{6,7},{7,0},{8,9},{9,10},{10,1... | collective-permute-start | bytes 294920 | tf_op jit(solution)/shard_map/ppermute | solution.py:322
  133.0 6.5 %collective-permute-start.9 = (bf16[640,128]{1,0:T(8,128)(2,1)S(1)}, bf16[640,128]{1,0:T(8,128)(2,1)S(1)}, u32[]{:S(2)}, u32[]{:S(2)}) collective-permute-start(bf16[640,128]{1,0:T(8,128)(2,1)S(1)} %collective-permute-done.6.refs_9_), channel_id=1, source_target_pairs={{0,1},{1,2},{2,3},{3,4},{4,5},{5,6},{6,7},{7,0},{8,9},{9,10},{10,1... | collective-permute-start | bytes 491528 | tf_op jit(solution)/shard_map/ppermute | solution.py:322
  133.1 6.4 %collective-permute-start.13 = (bf16[640,128]{1,0:T(8,128)(2,1)S(1)}, bf16[640,128]{1,0:T(8,128)(2,1)S(1)}, u32[]{:S(2)}, u32[]{:S(2)}) collective-permute-start(bf16[640,128]{1,0:T(8,128)(2,1)S(1)} %collective-permute-done.7.refs_10_), channel_id=1, source_target_pairs={{0,7},{1,0},{2,1},{3,2},{4,3},{5,4},{6,5},{7,6},{8,15},{9,8},{10,9... | collective-permute-start | bytes 491528 | tf_op jit(solution)/shard_map/ppermute | solution.py:325
  139.5 6.5 %collective-permute-start.10 = (bf16[640,128]{1,0:T(8,128)(2,1)S(1)}, bf16[640,128]{1,0:T(8,128)(2,1)S(1)}, u32[]{:S(2)}, u32[]{:S(2)}) collective-permute-start(bf16[640,128]{1,0:T(8,128)(2,1)S(1)} %collective-permute-done.9.refs_11_), channel_id=1, source_target_pairs={{0,1},{1,2},{2,3},{3,4},{4,5},{5,6},{6,7},{7,0},{8,9},{9,10},{10,1... | collective-permute-start | bytes 491528 | tf_op jit(solution)/shard_map/ppermute | solution.py:322
  139.5 9.8 %collective-permute-start.2 = (bf16[384,128]{1,0:T(8,128)(2,1)S(1)}, bf16[384,128]{1,0:T(8,128)(2,1)S(1)}, u32[]{:S(2)}, u32[]{:S(2)}) collective-permute-start(bf16[384,128]{1,0:T(8,128)(2,1)S(1)} %collective-permute-done.1.refs_4_), channel_id=1, source_target_pairs={{0,1},{1,2},{2,3},{3,4},{4,5},{5,6},{6,7},{7,0},{8,9},{9,10},{10,1... | collective-permute-start | bytes 294920 | tf_op jit(solution)/shard_map/ppermute | solution.py:322
  139.5 12.0 %collective-permute-start.14 = (bf16[640,128]{1,0:T(8,128)(2,1)S(1)}, bf16[640,128]{1,0:T(8,128)(2,1)S(1)}, u32[]{:S(2)}, u32[]{:S(2)}) collective-permute-start(bf16[640,128]{1,0:T(8,128)(2,1)S(1)} %collective-permute-done.13.refs_12_), channel_id=1, source_target_pairs={{0,7},{1,0},{2,1},{3,2},{4,3},{5,4},{6,5},{7,6},{8,15},{9,8},{10,9... | collective-permute-start | bytes 491528 | tf_op jit(solution)/shard_map/ppermute | solution.py:325
  146.0 9.1 %collective-permute-start.11 = (bf16[640,128]{1,0:T(8,128)(2,1)S(1)}, bf16[640,128]{1,0:T(8,128)(2,1)S(1)}, u32[]{:S(2)}, u32[]{:S(2)}) collective-permute-start(bf16[640,128]{1,0:T(8,128)(2,1)S(1)} %collective-permute-done.10.refs_13_), channel_id=1, source_target_pairs={{0,1},{1,2},{2,3},{3,4},{4,5},{5,6},{6,7},{7,0},{8,9},{9,10},{10,1... | collective-permute-start | bytes 491528 | tf_op jit(solution)/shard_map/ppermute | solution.py:322
  146.0 5.4 %collective-permute-start.12 = (bf16[384,128]{1,0:T(8,128)(2,1)S(1)}, bf16[384,128]{1,0:T(8,128)(2,1)S(1)}, u32[]{:S(2)}, u32[]{:S(2)}) collective-permute-start(bf16[384,128]{1,0:T(8,128)(2,1)S(1)} %collective-permute-done.8.refs_5_), channel_id=1, source_target_pairs={{0,7},{1,0},{2,1},{3,2},{4,3},{5,4},{6,5},{7,6},{8,15},{9,8},{10,9... | collective-permute-start | bytes 294920 | tf_op jit(solution)/shard_map/ppermute | solution.py:325
  149.3 5.8 %collective-permute-start.3 = (bf16[384,128]{1,0:T(8,128)(2,1)S(1)}, bf16[384,128]{1,0:T(8,128)(2,1)S(1)}, u32[]{:S(2)}, u32[]{:S(2)}) collective-permute-start(bf16[384,128]{1,0:T(8,128)(2,1)S(1)} %collective-permute-done.2.refs_6_), channel_id=1, source_target_pairs={{0,1},{1,2},{2,3},{3,4},{4,5},{5,6},{6,7},{7,0},{8,9},{9,10},{10,1... | collective-permute-start | bytes 294920 | tf_op jit(solution)/shard_map/ppermute | solution.py:322
  (3 other events, 3.6 us)
